TPU v7x, 256 devices: a whole 4x4x8 slice. The times are simulated.
256 devices in a mesh: hour: 8 (over z), pair: 32 (over x, y, core).
Axes of the slice: x: 4, y: 4, z: 8, core: 2. Of those that a mesh axis runs over, the one named last changes fastest.
Arguments:
- raw_panels: bfloat16 [512, 24, 3, 3712], P('pair', 'hour'), may hold values from -6 to 6
- window_start: int32 [512, 24, 2], P('pair', 'hour'), may hold values from 0 to 2688
- valid_count: int32 [512, 24, 2], P('pair', 'hour'), may hold values from 512 to 1024
- send_rows: int32 [32, 32, 4], P('pair'), may hold values from 0 to 15, as said below
- pair_slots: int32 [2048, 2], P('pair'), may hold values from 0 to 127, as said below
Outputs:
- stacked: float32 [2048, 9, 256], P('pair')
Inputs may be any that keep to these rules, and one draw needn't show every extreme that they name: `send_rows`: for each source and owner the 4 rows are different. `pair_slots`: the two slots of a pair differ; a slot s * 4 + c of owner q stands for the c-th row that source s sends to q.
All inputs are finite; a program needn't handle non-finite values.
Results may differ from a plain program's by a relative error of at most 0.0094.
Values may be sent and summed in bfloat16 or wider, within the bound.
No kernel may reach another device: no remote copies, remote signals or barrier semaphores. Data moves between devices by JAX's collectives and lax.ppermute only.
A program may use at most 64 MiB of HBM per device.

v0:
```python
import math

import jax
import jax.numpy as jnp
from jax import lax
from jax.sharding import PartitionSpec as P

NFFT = 1024
NFREQ = 512
LAGS = 256


smooth_half = 11
eps_white = 1e-06


def make_dft(length, nfreq):
    time_index = lax.broadcasted_iota(jnp.int32, (length, nfreq), 0)
    freq_index = lax.broadcasted_iota(jnp.int32, (length, nfreq), 1)
    angles = (time_index * freq_index % length).astype(jnp.float32) * (2.0 * math.pi / length)
    return jnp.concatenate([jnp.cos(angles), -jnp.sin(angles)], axis=1).astype(jnp.bfloat16)


def make_band(nfreq):
    row_index = lax.broadcasted_iota(jnp.int32, (nfreq, nfreq), 0)
    col_index = lax.broadcasted_iota(jnp.int32, (nfreq, nfreq), 1)
    return (jnp.abs(row_index - col_index) <= smooth_half).astype(jnp.float32)


def make_lags(nfreq, length, lags):
    freq_index = lax.broadcasted_iota(jnp.int32, (nfreq, lags), 0)
    shift_lag = lax.broadcasted_iota(jnp.int32, (nfreq, lags), 1) - lags // 2
    angles = (freq_index * shift_lag % length).astype(jnp.float32) * (2.0 * math.pi / length)
    weights = jnp.where(freq_index == 0, 0.5, 1.0).astype(jnp.float32)
    return jnp.concatenate([weights * jnp.cos(angles), -weights * jnp.sin(angles)], axis=0).astype(
        jnp.bfloat16
    )


def cut_windows(panels, starts, counts, length):

    def take_one(panel, begin):
        return lax.dynamic_slice_in_dim(panel, begin, length, 1)

    pieces = jax.vmap(jax.vmap(take_one, in_axes=(None, 0)))(panels, starts)
    positions = lax.broadcasted_iota(jnp.int32, (1, 1, 1, length), 3)
    valid_mask = (positions < counts[:, :, None, None]).astype(jnp.float32)
    values = pieces.astype(jnp.float32) * valid_mask
    average = jnp.sum(values, axis=3, keepdims=True) / counts[:, :, None, None].astype(jnp.float32)
    return ((values - average) * valid_mask).astype(jnp.bfloat16)


def whiten(samples, dft_matrix, band_ones, nfreq):
    leading = samples.shape[:-1]
    spectrum = jnp.dot(
        samples.reshape(-1, samples.shape[-1]), dft_matrix, preferred_element_type=jnp.float32
    )
    spectrum = spectrum.reshape(leading + (2 * nfreq,))
    real_part = spectrum[..., :nfreq]
    imag_part = spectrum[..., nfreq:]
    amplitude = jnp.sum(jnp.sqrt(real_part * real_part + imag_part * imag_part), axis=-2)
    smooth = jnp.dot(amplitude.reshape(-1, nfreq), band_ones, precision=lax.Precision.HIGHEST)
    smooth = smooth.reshape(amplitude.shape) / (3.0 * (2 * smooth_half + 1))
    divisor = jnp.concatenate([smooth, smooth], axis=-1) + eps_white
    return (spectrum / divisor[..., None, :]).astype(jnp.bfloat16)


def outer_sum(left_part, right_part):
    return jnp.sum(left_part[:, :, :, None, :] * right_part[:, :, None, :, :], axis=1)


def hour_roots(spectra, first_index, second_index, lag_matrix, nfreq):
    pairs = first_index.shape[0]
    block_size = math.gcd(pairs, 256)
    windows = spectra.shape[1]
    lag_scale = 1.0 / math.sqrt(windows * nfreq)

    def one_block(indices):
        left_side = spectra[indices[0]].astype(jnp.float32)
        right_side = spectra[indices[1]].astype(jnp.float32)
        left_real, left_imag = (left_side[..., :nfreq], left_side[..., nfreq:])
        right_real, right_imag = (right_side[..., :nfreq], right_side[..., nfreq:])
        cross_real = outer_sum(left_real, right_real) + outer_sum(left_imag, right_imag)
        cross_imag = outer_sum(left_imag, right_real) - outer_sum(left_real, right_imag)
        cross = jnp.concatenate([cross_real, cross_imag], axis=-1).astype(jnp.bfloat16)
        lagged = jnp.dot(
            cross.reshape(-1, 2 * nfreq), lag_matrix, preferred_element_type=jnp.float32
        )
        lagged = lagged.reshape(block_size, 9, lag_matrix.shape[1]) * lag_scale
        return jnp.sign(lagged) * (jnp.sqrt(jnp.abs(lagged) + 0.01) - 0.1)

    blocks = (
        first_index.reshape(pairs // block_size, block_size),
        second_index.reshape(pairs // block_size, block_size),
    )
    result = lax.map(one_block, blocks)
    return result.reshape(pairs, 9, lag_matrix.shape[1])


def finish(summed, hours_all):
    average = summed / hours_all
    return jnp.sign(average) * ((jnp.abs(average) + 0.1) * (jnp.abs(average) + 0.1) - 0.01)


def local(raw_panels, window_start, valid_count, send_rows, pair_slots):
    stations = raw_panels.shape[0]
    hours_here = raw_panels.shape[1]
    pair_count = lax.axis_size("pair")
    capacity = send_rows.shape[2]
    send_list = send_rows[0].reshape(-1)
    dft_matrix = make_dft(NFFT, NFREQ)
    band_ones = make_band(NFREQ)
    lag_matrix = make_lags(NFREQ, NFFT, LAGS)
    samples = cut_windows(
        raw_panels.reshape(stations * hours_here, 3, raw_panels.shape[3]),
        window_start.reshape(stations * hours_here, -1),
        valid_count.reshape(stations * hours_here, -1),
        NFFT,
    )
    samples = samples.reshape((stations, hours_here) + samples.shape[1:])
    first_slot = pair_slots[:, 0]
    second_slot = pair_slots[:, 1]
    outgoing = samples[send_list].reshape((pair_count, capacity) + samples.shape[1:])
    received = lax.all_to_all(outgoing, "pair", split_axis=0, concat_axis=0, tiled=True)
    flattened = received.reshape((received.shape[0] * received.shape[1],) + received.shape[2:])
    results = []
    for hour_item in range(flattened.shape[1]):
        spectra = whiten(flattened[:, hour_item], dft_matrix, band_ones, NFREQ)
        results.append(hour_roots(spectra, first_slot, second_slot, lag_matrix, NFREQ))
    hourly = jnp.stack(results, axis=0)
    partial_sum = jnp.sum(hourly, axis=0)
    hours_all = hours_here * lax.axis_size("hour")
    summed = lax.psum(partial_sum, "hour")
    return finish(summed, hours_all)


def solution(mesh):
    return jax.shard_map(
        local,
        mesh=mesh,
        in_specs=(
            P("pair", "hour", None, None),
            P("pair", "hour", None),
            P("pair", "hour", None),
            P("pair", None, None),
            P("pair", None),
        ),
        out_specs=P("pair", None, None),
        check_vma=False,
    )
```

profile of v0, /device:TPU:8, one launch (start us, length us, event | category | flops | bytes accessed | tf_op | source)
XLA Modules:
  0.0 510.1 jit_solution(17804942471653833436)
XLA Ops:
  11.8 241.4 %while.1 = (s32[]{:T(128)}, bf16[48,3,3712]{2,1,0:T(4,128)(2,1)S(1)}, s32[96,3]{0,1:T(4,128)S(1)}, bf16[96,3,1024]{2,1,0:T(4,128)(2,1)}, s32[]{:T(128)}) while((s32[]{:T(128)}, bf16[48,3,3712]{2,1,0:T(4,128)(2,1)S(1)}, s32[96,3]{0,1:T(4,128)S(1)}, bf16[96,3,1024]{2,1,0:T(4,128)(2,1)}, s32[]{:T(128)}) %tuple.50), condition=%wide.while_cond, body=%wide.while_body.sunk | while | flops 2 | bytes 15477 | solution.py:43
  257.0 13.0 %gather_fusion = bf16[128,3,2,3,1024]{4,2,3,1,0:T(2,128)(2,1)} fusion(bf16[16,3,2,3,1024]{4,2,3,1,0:T(2,128)(2,1)S(1)} %copy.237, s32[1024]{0:T(1024)S(1)} %pad_clamp_fusion.2), kind=kCustom, calls=%fused_computation | custom fusion | bytes 9437696 | tf_op jit(solution)/shard_map/gather | solution.py:123
  270.0 7.2 %copy.238 = bf16[32,4,3,2,3,1024]{5,1,4,3,2,0:T(4,128)(2,1)} copy(bf16[32,4,3,2,3,1024]{5,3,4,2,1,0:T(2,128)(2,1)} %bitcast.60) | data formatting | bytes 9437184 | tf_op jit(solution)/shard_map/reshape | solution.py:123
  277.2 7.7 %all-to-all-start = ((bf16[32,4,3,2,3,1024]{5,1,4,3,2,0:T(4,128)(2,1)}), bf16[32,4,3,2,3,1024]{5,1,4,3,2,0:T(4,128)(2,1)}, u32[]{:S(2)}, u32[]{:S(2)}) async-start(bf16[32,4,3,2,3,1024]{5,1,4,3,2,0:T(4,128)(2,1)} %copy.238), calls=%async_computation | async-start | bytes 9437184 | tf_op jit(solution)/shard_map/all_to_all | solution.py:124
  285.2 3.1 multiply_convert_fusion.1
  288.2 8.5 %negate_convert_fusion = (bf16[1024,512]{1,0:T(8,128)(2,1)S(1)}, bf16[1024,512]{1,0:T(8,128)(2,1)S(1)}) fusion(), kind=kLoop, calls=%fused_computation.31 | loop fusion | flops 8912896 | bytes 2097152 | tf_op jit(solution)/shard_map/convert.16
  296.8 50.8 %all-to-all-done = bf16[32,4,3,2,3,1024]{5,1,4,3,2,0:T(4,128)(2,1)} async-done(((bf16[32,4,3,2,3,1024]{5,1,4,3,2,0:T(4,128)(2,1)}), bf16[32,4,3,2,3,1024]{5,1,4,3,2,0:T(4,128)(2,1)}, u32[]{:S(2)}, u32[]{:S(2)}) %all-to-all-start) | async-done | bytes 4718624 | tf_op jit(solution)/shard_map/all_to_all | solution.py:124
  347.6 6.8 %copy.239 = bf16[32,4,3,2,3,1024]{5,1,0,4,3,2:T(4,128)(2,1)} copy(bf16[32,4,3,2,3,1024]{5,1,4,3,2,0:T(4,128)(2,1)} %all-to-all-done) | data formatting | bytes 9437184 | tf_op jit(solution)/shard_map/all_to_all | solution.py:124
  354.4 7.7 %reshape.249 = bf16[128,3,2,3,1024]{4,0,3,2,1:T(8,128)(2,1)} reshape(bf16[32,4,3,2,3,1024]{5,1,0,4,3,2:T(4,128)(2,1)} %copy.239) | data formatting | bytes 9437184 | tf_op jit(solution)/shard_map/reshape | solution.py:125
  362.1 3.3 fusion.9
  365.5 3.5 fusion.13
  368.9 3.3 fusion.17
  374.1 2.8 copy.252
  376.9 4.4 gather_fusion.6
  381.3 4.4 gather_fusion.5
  385.7 2.7 fusion.12
  389.7 3.2 copy.246
  392.9 4.4 gather_fusion.4
  397.2 4.4 gather_fusion.3
  406.3 2.1 gather_fusion.1
  408.4 3.6 gather_fusion.2
  426.0 2.2 multiply_add_fusion
  428.2 72.8 %all-reduce.3.cloned.1.call-done = f32[64,9,256]{2,0,1:T(8,128)} async-done(((f32[64,9,256]{2,0,1:T(8,128)}), f32[64,9,256]{2,0,1:T(8,128)}) %all-reduce.3.cloned.1.call-update) | async-done | bytes 589840 | tf_op jit(solution)/shard_map/psum | solution.py:133
  501.0 2.1 add_multiply_fusion
  (384 shorter events, 271.9 us)
Async XLA Ops:
  6.5 4.7 copy-start.7
  277.2 8.0 %copy-start.11 = (s32[64,2]{0,1:T(2,128)S(1)}, s32[64,2]{0,1:T(2,128)}, u32[]{:S(2)}) copy-start(s32[64,2]{0,1:T(2,128)} %param.9) | copy-start | bytes 1540
  277.2 70.4 %all-to-all-start = ((bf16[32,4,3,2,3,1024]{5,1,4,3,2,0:T(4,128)(2,1)}), bf16[32,4,3,2,3,1024]{5,1,4,3,2,0:T(4,128)(2,1)}, u32[]{:S(2)}, u32[]{:S(2)}) async-start(bf16[32,4,3,2,3,1024]{5,1,4,3,2,0:T(4,128)(2,1)} %copy.238), calls=%async_computation | async-start | bytes 9437184 | tf_op jit(solution)/shard_map/all_to_all | solution.py:124
  284.9 216.1 %all-reduce.3.cloned.1.call-start = ((), (), s32[]{:S(2)}) async-start(), calls=%async_computation.1 | async-start | bytes 1179648 | tf_op jit(solution)/shard_map/psum | solution.py:133
  296.8 68.7 %copy-start.8 = (bf16[1024,512]{1,0:T(8,128)(2,1)}, bf16[1024,512]{1,0:T(8,128)(2,1)S(1)}, u32[]{:S(2)}) copy-start(bf16[1024,512]{1,0:T(8,128)(2,1)S(1)} %get-tuple-element.105) | copy-start | bytes 3145732
  296.8 68.7 %copy-start.9 = (bf16[1024,512]{1,0:T(8,128)(2,1)}, bf16[1024,512]{1,0:T(8,128)(2,1)S(1)}, u32[]{:S(2)}) copy-start(bf16[1024,512]{1,0:T(8,128)(2,1)S(1)} %get-tuple-element.106) | copy-start | bytes 3145732
  362.1 3.4 copy-start.6
  385.7 3.4 copy-start
  405.1 1.2 copy-start.5
  408.4 3.6 copy-start.4
  412.7 1.1 copy-start.3
  416.2 1.1 copy-start.2
  417.8 1.1 copy-start.1
  424.1 1.0 copy-start.10
Sparse Core Ops, SparseCore 0:
  428.3 72.6 all-reduce.2
where the time goes:
time: 520 us; the launch traced here: 510 us
  local copies, waits for them, and re-layouts  320 us (62%)
  waiting for transfers between devices  124 us (24%)
  other arithmetic  28.8 us (6%)
  matrix products  15.1 us (3%)
  between operations  14.2 us (3%)
  starting transfers between devices  7.93 us (2%)
    gather x288, local copies, waits for them, and re-layouts  241 us
    psum x1, waiting for transfers between devices, local(): summed = lax.psum(partial_sum, 'hour')  72.8 us
    all_to_all x1, waiting for transfers between devices, local(): lax.all_to_all(outgoing, 'pair', split_axis=0, concat_axis=0, tiled=True)  50.8 us
    another operation x8, other arithmetic  13.5 us
    gather x1, local copies, waits for them, and re-layouts, local(): samples[send_list].reshape((pair_count, capacity) + samples.shape[1:])  13 us
    gather x3, local copies, waits for them, and re-layouts, one_block(): right_side = spectra[indices[1]].astype(jnp.float32)  12.4 us
    gather x3, local copies, waits for them, and re-layouts, one_block(): left_side = spectra[indices[0]].astype(jnp.float32)  10.9 us
  transfers between devices with their start and end apart: 2, of which 2 were waited for; matrix products, arithmetic and copies ran while one was open for 2% of the time, Pallas kernels for 0%

commit v1 on v0

v1 whole, which is shorter than its diff:
```python
import functools
import math

import jax
import jax.numpy as jnp
import ml_dtypes
import numpy as np
from jax import lax
from jax.experimental import pallas as pl
from jax.experimental.pallas import tpu as pltpu
from jax.sharding import PartitionSpec as P

NFFT = 1024
NFREQ = 512
LAGS = 256
COMPS = 3
WINDOWS = 2
PARTS = 2 * WINDOWS
SMOOTH_HALF = 11
EPS_WHITE = 1e-06
F32 = jnp.float32
BF16 = jnp.bfloat16


def dft_table():
    turns = np.outer(np.arange(NFFT), np.arange(NFREQ)) % NFFT
    angles = turns.astype(np.float32) * np.float32(2.0 * math.pi / NFFT)
    angles = angles.astype(np.float64)
    table = np.concatenate([np.cos(angles), -np.sin(angles)], axis=1)
    return table.astype(np.float32).astype(ml_dtypes.bfloat16)


def band_table():
    index = np.arange(NFREQ)
    band = np.abs(index[:, None] - index[None, :]) <= SMOOTH_HALF
    return band.astype(ml_dtypes.bfloat16)


def lag_table():
    turns = np.outer(np.arange(NFREQ), np.arange(LAGS) - LAGS // 2) % NFFT
    angles = turns.astype(np.float32) * np.float32(2.0 * math.pi / NFFT)
    angles = angles.astype(np.float64)
    weights = np.where(np.arange(NFREQ) == 0, 0.5, 1.0)[:, None]
    table = np.concatenate([weights * np.cos(angles), -weights * np.sin(angles)], axis=0)
    scale = 1.0 / math.sqrt(WINDOWS * NFREQ)
    return (table.astype(np.float32).astype(ml_dtypes.bfloat16) * scale).astype(ml_dtypes.bfloat16)


def column(row, size):
    here = lax.broadcasted_iota(jnp.int32, (size, size), 0)
    there = lax.broadcasted_iota(jnp.int32, (size, size), 1)
    spread = jnp.where(here == there, jnp.broadcast_to(row, (size, size)).astype(F32), 0.0)
    return jnp.sum(spread, axis=1, keepdims=True).astype(jnp.int32)


def cut(panel, start):
    raw = panel.shape[1]
    reach = raw - 2048
    bit = (start & 2048) != 0
    moved = jnp.where(bit, panel[:, 2048:], panel[:, :reach])
    samples = jnp.concatenate([moved, panel[:, reach : NFFT + 2048]], axis=1)
    for size in (1024, 512, 256, 128):
        bit = (start & size) != 0
        keep = NFFT + size
        samples = jnp.where(bit, samples[:, size : size + keep], samples[:, :keep])
    width = samples.shape[1]
    for size in (64, 32, 16, 8, 4, 2, 1):
        bit = (start & size) != 0
        samples = jnp.where(bit, pltpu.roll(samples, width - size, 1), samples)
    return samples[:, :NFFT]


def whiten_kernel(raw_ref, start_ref, count_ref, dft_ref, band_ref, pick_ref, out_ref, seg_ref, spec_ref, white_ref):
    stations = raw_ref.shape[2]
    time = lax.broadcasted_iota(jnp.int32, (stations, NFFT), 1)
    for w in range(WINDOWS):
        start = column(start_ref[0, w : w + 1, :], stations)
        count = column(count_ref[0, w : w + 1, :], stations)
        live = time < count
        share = count.astype(F32)
        for c in range(COMPS):
            piece = cut(raw_ref[0, c].astype(F32), start)
            piece = jnp.where(live, piece, 0.0)
            mean = jnp.sum(piece, axis=1, keepdims=True) / share
            row = (w * COMPS + c) * stations
            seg_ref[row : row + stations, :] = jnp.where(live, piece - mean, 0.0).astype(BF16)
    spec_ref[...] = jnp.dot(seg_ref[...], dft_ref[...], preferred_element_type=F32)
    amps = []
    for w in range(WINDOWS):
        total = jnp.zeros((stations, NFREQ), F32)
        for c in range(COMPS):
            row = (w * COMPS + c) * stations
            real = spec_ref[row : row + stations, :NFREQ]
            imag = spec_ref[row : row + stations, NFREQ:]
            total = total + jnp.sqrt(real * real + imag * imag)
        amps.append(total)
    amp = jnp.concatenate(amps, axis=0)
    rows = WINDOWS * stations
    high = amp.astype(BF16)
    rest = amp - high.astype(F32)
    middle = rest.astype(BF16)
    low = (rest - middle.astype(F32)).astype(BF16)
    sums = jnp.dot(jnp.concatenate([high, middle, low], axis=0), band_ref[...], preferred_element_type=F32)
    smooth = (sums[:rows] + sums[rows : 2 * rows] + sums[2 * rows :]) / (3.0 * (2 * SMOOTH_HALF + 1))
    inverse = 1.0 / (smooth + EPS_WHITE)
    for w in range(WINDOWS):
        factor = inverse[w * stations : (w + 1) * stations]
        for c in range(COMPS):
            row = (w * COMPS + c) * stations
            for r in range(2):
                part = spec_ref[row : row + stations, r * NFREQ : (r + 1) * NFREQ] * factor
                to = (2 * w + r) * stations
                white_ref[to : to + stations, c * NFREQ : (c + 1) * NFREQ] = part.astype(BF16)
    for c in range(COMPS):
        cols = slice(c * NFREQ, (c + 1) * NFREQ)
        picked = jnp.dot(pick_ref[...], white_ref[:, cols], preferred_element_type=F32).astype(BF16)
        out_ref[:, :, cols] = picked.reshape(out_ref.shape[0], out_ref.shape[1], NFREQ)


def correlate_kernel(recv_ref, pick_ref, lag_ref, out_ref, side_ref, cross_ref, total_ref):
    hour = pl.program_id(0)
    pairs = total_ref.shape[0] // (COMPS * COMPS)
    slots = recv_ref.shape[0] * recv_ref.shape[1]
    width = recv_ref.shape[2]
    for c in range(COMPS):
        cols = slice(c * NFREQ, (c + 1) * NFREQ)
        arrived = recv_ref[:, :, cols].reshape(slots, NFREQ)
        side_ref[:, cols] = jnp.dot(pick_ref[...], arrived, preferred_element_type=F32)

    for k in range(0, pairs, 16):
        for f in range(0, NFREQ, 128):
            def load(side, part, comp):
                row = (side * PARTS + part) * pairs + k
                col = comp * NFREQ + f
                return side_ref[row : row + 16, col : col + 128]
            left = [[load(0, part, comp) for comp in range(COMPS)] for part in range(PARTS)]
            right = [[load(1, part, comp) for comp in range(COMPS)] for part in range(PARTS)]
            for i in range(COMPS):
                for j in range(COMPS):
                    real = left[0][i] * right[0][j] + left[2][i] * right[2][j]
                    real = real + (left[1][i] * right[1][j] + left[3][i] * right[3][j])
                    imag = left[1][i] * right[0][j] + left[3][i] * right[2][j]
                    imag = imag - (left[0][i] * right[1][j] + left[2][i] * right[3][j])
                    row = (COMPS * i + j) * pairs + k
                    cross_ref[row : row + 16, f : f + 128] = real.astype(BF16)
                    cross_ref[row : row + 16, NFREQ + f : NFREQ + f + 128] = imag.astype(BF16)
    lagged = jnp.dot(cross_ref[...], lag_ref[...], preferred_element_type=F32)
    root = jnp.sqrt(jnp.abs(lagged) + 0.01) - 0.1
    root = jnp.where(lagged > 0.0, root, jnp.where(lagged < 0.0, -root, 0.0))

    @pl.when(hour == 0)
    def _():
        total_ref[...] = root

    @pl.when(hour > 0)
    def _():
        total_ref[...] += root

    @pl.when(hour == pl.num_programs(0) - 1)
    def _():
        out_ref[...] = total_ref[...].astype(BF16).reshape(out_ref.shape)


def whiten(panels, starts, counts, pick, owners, rows):
    hours, _, stations, raw = panels.shape
    width = COMPS * NFREQ
    whole = lambda shape: pl.BlockSpec(shape, lambda h: (0,) * len(shape))
    return pl.pallas_call(
        whiten_kernel,
        grid=(hours,),
        in_specs=[
            pl.BlockSpec((1, COMPS, stations, raw), lambda h: (h, 0, 0, 0)),
            pl.BlockSpec((1, WINDOWS, stations), lambda h: (h, 0, 0)),
            pl.BlockSpec((1, WINDOWS, stations), lambda h: (h, 0, 0)),
            whole((NFFT, 2 * NFREQ)),
            whole((NFREQ, NFREQ)),
            whole(pick.shape),
        ],
        out_specs=pl.BlockSpec((owners, rows, width), lambda h: (0, h, 0)),
        out_shape=jax.ShapeDtypeStruct((owners, hours * rows, width), BF16),
        scratch_shapes=[
            pltpu.VMEM((WINDOWS * COMPS * stations, NFFT), BF16),
            pltpu.VMEM((WINDOWS * COMPS * stations, 2 * NFREQ), F32),
            pltpu.VMEM((PARTS * stations, width), BF16),
        ],
        compiler_params=pltpu.CompilerParams(vmem_limit_bytes=40 * 2**20),
    )(panels, starts, counts, dft_table(), band_table(), pick)


def correlate(received, pick, pairs, rows, pieces):
    owners, all_rows, width = received.shape
    hours = all_rows // rows
    channels = COMPS * COMPS
    whole = lambda shape: pl.BlockSpec(shape, lambda h: (0,) * len(shape))
    piece = (pieces, channels * pairs // pieces, LAGS)
    return pl.pallas_call(
        correlate_kernel,
        grid=(hours,),
        in_specs=[
            pl.BlockSpec((owners, rows, width), lambda h: (0, h, 0)),
            whole(pick.shape),
            whole((2 * NFREQ, LAGS)),
        ],
        out_specs=whole(piece),
        out_shape=jax.ShapeDtypeStruct(piece, BF16),
        scratch_shapes=[
            pltpu.VMEM((2 * PARTS * pairs, width), F32),
            pltpu.VMEM((channels * pairs, 2 * NFREQ), BF16),
            pltpu.VMEM((channels * pairs, LAGS), F32),
        ],
        compiler_params=pltpu.CompilerParams(vmem_limit_bytes=40 * 2**20),
    )(received, pick, lag_table())


def local(raw_panels, window_start, valid_count, send_rows, pair_slots):
    stations, hours = raw_panels.shape[:2]
    owners, capacity = send_rows.shape[1:]
    pairs = pair_slots.shape[0]
    rows = capacity * PARTS
    hour_devices = lax.axis_size("hour")

    wanted = jnp.broadcast_to(send_rows[0][:, :, None], (owners, capacity, PARTS)).reshape(-1, 1)
    part = jnp.arange(owners * rows, dtype=jnp.int32)[:, None] % PARTS
    source = jnp.arange(PARTS * stations, dtype=jnp.int32)[None, :]
    send_pick = (part * stations + wanted == source).astype(BF16)

    slot = pair_slots.T[:, None, :]
    side_part = jnp.arange(PARTS, dtype=jnp.int32)[None, :, None]
    pair_rows = (slot * PARTS + side_part).reshape(-1, 1)
    arrived = jnp.arange(owners * rows, dtype=jnp.int32)[None, :]
    pair_pick = (pair_rows == arrived).astype(BF16)

    panels = jnp.transpose(raw_panels, (1, 2, 0, 3))
    starts = jnp.transpose(window_start, (1, 2, 0))
    counts = jnp.transpose(valid_count, (1, 2, 0))
    outgoing = whiten(panels, starts, counts, send_pick, owners, rows)
    received = lax.all_to_all(outgoing, "pair", split_axis=0, concat_axis=0, tiled=True)
    partial = correlate(received, pair_pick, pairs, rows, hour_devices)
    shares = lax.all_to_all(partial, "hour", split_axis=0, concat_axis=0, tiled=True)
    average = jnp.sum(shares.astype(F32), axis=0) / (hours * hour_devices)
    size = jnp.abs(average) + 0.1
    stacked = (jnp.sign(average) * (size * size - 0.01)).astype(BF16)
    stacked = lax.all_gather(stacked, "hour", axis=0, tiled=True, axis_index_groups=[list(range(hour_devices))])
    stacked = stacked.reshape(COMPS * COMPS, pairs, LAGS).astype(F32)
    return jnp.transpose(stacked, (1, 0, 2))


def solution(mesh):
    return jax.shard_map(
        local,
        mesh=mesh,
        in_specs=(
            P("pair", "hour", None, None),
            P("pair", "hour", None),
            P("pair", "hour", None),
            P("pair", None, None),
            P("pair", None),
        ),
        out_specs=P("pair", None, None),
        check_vma=False,
    )
```

time: 520 us -> 141 us (0.27); the launches traced: 510 us -> 140 us
  local copies, waits for them, and re-layouts: 320 us -> 8.45 us
  waiting for transfers between devices: 124 us -> 62.4 us
  blocking collectives: 0 us -> 45.7 us
  other arithmetic: 28.8 us -> 1.25 us
  matrix products: 15.1 us -> 0 us
  Pallas kernels: 0 us -> 14.5 us
  between operations: 14.2 us -> 0.11 us
    gather x297 -> x0, local copies, waits for them, and re-layouts: 278 us -> none
    psum x1 -> x0, waiting for transfers between devices: 72.8 us -> none  [local(): summed = lax.psum(partial_sum, 'hour')]
    all_gather x0 -> x1, blocking collectives: none -> 25.1 us  [local(): lax.all_gather(stacked, 'hour', axis=0, tiled=True, axis_index_groups=[li...]
    all_to_all x0 -> x1, blocking collectives: none -> 20.6 us  [local(): lax.all_to_all(partial, 'hour', split_axis=0, concat_axis=0, tiled=True)]
    dot_general x9 -> x0, matrix products: 15.1 us -> none  [the longest x3 10.1 us: whiten(): jnp.dot(samples.reshape(-1, samples.shape[-1]), dft_matrix, preferred_ele...]
    reshape x3 -> x1, local copies, waits for them, and re-layouts: 14.9 us -> 0.13 us  [local(): jnp.broadcast_to(send_rows[0][:, :, None], (owners, capacity, PARTS))]
    pallas_call x0 -> x2, Pallas kernels: none -> 14.5 us  [the longest x1 8.09 us: correlate(): pl.pallas_call(correlate_kernel, grid=(hours,), in_specs=[pl.BlockSpec((o...]
    another operation x8 -> x0, other arithmetic: 13.5 us -> none
  transfers between devices with their start and end apart: 2 -> 1, of which waited for: 2 -> 1; matrix products, arithmetic and copies ran while one was open for 2% -> 0% of each run, Pallas kernels for 0% -> 0%
where the time goes in v1:
time: 141 us; the launch traced here: 140 us
  waiting for transfers between devices  62.4 us (44%)
  blocking collectives  45.7 us (32%)
  Pallas kernels  14.5 us (10%)
  local copies, waits for them, and re-layouts  8.45 us (6%)
  starting transfers between devices  7.71 us (5%)
    all_to_all x1, waiting for transfers between devices, local(): lax.all_to_all(outgoing, 'pair', split_axis=0, concat_axis=0, tiled=True)  62.4 us
    all_gather x1, blocking collectives, local(): lax.all_gather(stacked, 'hour', axis=0, tiled=True, axis_index_groups=[li...  25.1 us
    all_to_all x1, blocking collectives, local(): lax.all_to_all(partial, 'hour', split_axis=0, concat_axis=0, tiled=True)  20.6 us
    pallas_call x1, Pallas kernels, correlate(): pl.pallas_call(correlate_kernel, grid=(hours,), in_specs=[pl.BlockSpec((o...  8.09 us
    all_to_all x1, starting transfers between devices, local(): lax.all_to_all(outgoing, 'pair', split_axis=0, concat_axis=0, tiled=True)  7.71 us
    unnamed x16, local copies, waits for them, and re-layouts  7.39 us
    pallas_call x1, Pallas kernels, whiten(): pl.pallas_call(whiten_kernel, grid=(hours,), in_specs=[pl.BlockSpec((1, C...  6.39 us
  transfers between devices with their start and end apart: 1, of which 1 were waited for; matrix products, arithmetic and copies ran while one was open for 0% of the time, Pallas kernels for 0%

profile of v1, /device:TPU:8, one launch (start us, length us, event | category | flops | bytes accessed | tf_op | source)
XLA Modules:
  0.0 140.1 jit_solution(962463144243603841)
XLA Ops:
  0.0 0.8 copy.10
  0.8 0.1 broadcast_in_dim.5
  0.9 0.1 reshape.48
  1.0 0.1 fusion.1.pick_ref
  1.1 0.0 copy-start.1
  1.2 1.6 %copy-done.1 = bf16[1024,1024]{1,0:T(8,128)(2,1)S(1)} copy-done((bf16[1024,1024]{1,0:T(8,128)(2,1)S(1)}, bf16[1024,1024]{1,0:T(8,128)(2,1)}, u32[]{:S(2)}) %copy-start.1) | copy-done | bytes 2097176
  2.7 0.0 copy-start.2
  2.7 1.2 copy-done.2
  4.0 1.0 copy-done.4
  5.0 0.7 copy-done.5
  5.7 0.7 copy-done.6
  6.4 6.4 %shard_map.82 = bf16[32,48,1536]{2,1,0:T(8,128)(2,1)S(1)} custom-call(bf16[3,3,16,3712]{3,2,1,0:T(8,128)(2,1)S(1)} %bitcast.10, s32[3,2,16]{2,1,0:T(2,128)S(1)} %bitcast.11, s32[3,2,16]{2,1,0:T(2,128)S(1)} %bitcast.12, bf16[1024,1024]{1,0:T(8,128)(2,1)S(1)} %copy-done.1, bf16[512,512]{1,0:T(8,128)(2,1)S(1)} %copy-done.4, bf16[512,64]{1,0:T(8,128)(2,1)S(1)} %fusion.1.pick_ref), custom_call_target="tpu_custom_call" | custom-call | tf_op jit(solution)/shard_map/pallas_call | solution.py:168
  12.8 0.0 copy-start
  12.8 2.2 %copy-done = bf16[32,48,1536]{2,1,0:T(8,128)(2,1)} copy-done((bf16[32,48,1536]{2,1,0:T(8,128)(2,1)}, bf16[32,48,1536]{2,1,0:T(8,128)(2,1)S(1)}, u32[]{:S(2)}) %copy-start) | copy-done | bytes 4718616
  14.9 7.7 %all-to-all-start = ((bf16[32,48,1536]{2,1,0:T(8,128)(2,1)}), bf16[32,48,1536]{2,1,0:T(8,128)(2,1)}, u32[]{:S(2)}, u32[]{:S(2)}) async-start(bf16[32,48,1536]{2,1,0:T(8,128)(2,1)} %copy-done), calls=%async_computation | async-start | bytes 9437184 | tf_op jit(solution)/shard_map/all_to_all | solution.py:237
  22.7 0.0 copy-done.7
  22.7 0.1 add.51
  22.8 0.2 fusion.pick_ref
  22.9 62.4 %all-to-all-done.recv_ref = bf16[32,48,1536]{2,1,0:T(8,128)(2,1)} async-done(((bf16[32,48,1536]{2,1,0:T(8,128)(2,1)}), bf16[32,48,1536]{2,1,0:T(8,128)(2,1)}, u32[]{:S(2)}, u32[]{:S(2)}) %all-to-all-start) | async-done | bytes 4718624 | tf_op jit(solution)/shard_map/all_to_all | solution.py:237
  85.4 0.0 copy-done.3
  85.4 8.1 %shard_map.83 = bf16[8,72,256]{2,1,0:T(8,128)(2,1)S(1)} custom-call(bf16[32,48,1536]{2,1,0:T(8,128)(2,1)} %all-to-all-done.recv_ref, bf16[512,512]{1,0:T(8,128)(2,1)S(1)} %fusion.pick_ref, bf16[1024,256]{1,0:T(8,128)(2,1)S(1)} %copy-done.3), custom_call_target="tpu_custom_call" | custom-call | tf_op jit(solution)/shard_map/pallas_call | solution.py:196
  93.5 20.6 %all_to_all.10 = bf16[8,72,256]{2,1,0:T(8,128)(2,1)S(1)} all-to-all(bf16[8,72,256]{2,1,0:T(8,128)(2,1)S(1)} %shard_map.83), channel_id=1, replica_groups=mesh['hour'=8,'pair'=32] {'hour'}, dimensions={0} | all-to-all | bytes 589824 | tf_op jit(solution)/shard_map/all_to_all | solution.py:239
  114.2 25.1 %all_gather.3 = bf16[576,256]{1,0:T(8,128)(2,1)S(1)} all-gather(bf16[72,256]{1,0:T(8,128)(2,1)S(1)} %multiply_convert_fusion), channel_id=1, replica_groups={{0,32,64,96,128,160,192,224},{1,33,65,97,129,161,193,225},{2,34,66,98,1..., dimensions={0}, use_global_device_ids=true | all-gather | bytes 331776 | tf_op jit(solution)/shard_map/all_gather | solution.py:243
  139.3 0.9 convert_bitcast_fusion
  (10 shorter events, 0.1 us)
Async XLA Ops:
  1.1 1.6 %copy-start.1 = (bf16[1024,1024]{1,0:T(8,128)(2,1)S(1)}, bf16[1024,1024]{1,0:T(8,128)(2,1)}, u32[]{:S(2)}) copy-start(bf16[1024,1024]{1,0:T(8,128)(2,1)} %constant.35.clone.dft_ref) | copy-start | bytes 6291460
  2.7 1.2 copy-start.2
  4.0 1.0 copy-start.4
  5.0 0.7 copy-start.5
  5.7 0.7 copy-start.6
  12.8 2.2 %copy-start = (bf16[32,48,1536]{2,1,0:T(8,128)(2,1)}, bf16[32,48,1536]{2,1,0:T(8,128)(2,1)S(1)}, u32[]{:S(2)}) copy-start(bf16[32,48,1536]{2,1,0:T(8,128)(2,1)S(1)} %shard_map.82) | copy-start | bytes 14155780
  14.9 7.7 %copy-start.7 = (s32[64,2]{0,1:T(2,128)S(1)}, s32[64,2]{0,1:T(2,128)}, u32[]{:S(2)}) copy-start(s32[64,2]{0,1:T(2,128)} %param.12) | copy-start | bytes 1540
  14.9 70.4 %copy-start.3 = (bf16[1024,256]{1,0:T(8,128)(2,1)S(1)}, bf16[1024,256]{1,0:T(8,128)(2,1)}, u32[]{:S(2)}) copy-start(bf16[1024,256]{1,0:T(8,128)(2,1)} %constant.37.clone.lag_ref) | copy-start | bytes 1572868
  14.9 70.4 %all-to-all-start = ((bf16[32,48,1536]{2,1,0:T(8,128)(2,1)}), bf16[32,48,1536]{2,1,0:T(8,128)(2,1)}, u32[]{:S(2)}, u32[]{:S(2)}) async-start(bf16[32,48,1536]{2,1,0:T(8,128)(2,1)} %copy-done), calls=%async_computation | async-start | bytes 9437184 | tf_op jit(solution)/shard_map/all_to_all | solution.py:237

commit v2 on v1

--- a/solution.py
+++ b/solution.py
@@ -18,6 +18,8 @@
 PARTS = 2 * WINDOWS
 SMOOTH_HALF = 11
 EPS_WHITE = 1e-06
+HALF_HOURS = 4
+VMEM_LIMIT = 60 * 2**20
 F32 = jnp.float32
 BF16 = jnp.bfloat16
 
@@ -70,51 +72,88 @@
     return samples[:, :NFFT]
 
 
-def whiten_kernel(raw_ref, start_ref, count_ref, dft_ref, band_ref, pick_ref, out_ref, seg_ref, spec_ref, white_ref):
-    stations = raw_ref.shape[2]
+def whiten_kernel(
+    raw_hbm, start_ref, count_ref, send_ref, dft_hbm, band_hbm, out_hbm,
+    raw_ref, dft_ref, band_ref, seg_ref, spec_ref, white_ref, pick_ref, out_ref, raw_sem, table_sem, out_sem,
+):
+    hours, _, stations, _ = raw_ref.shape
+    capacity, owners = send_ref.shape
+    rows = capacity * PARTS
+    block = COMPS * WINDOWS * stations
+    raw_copies = [pltpu.make_async_copy(raw_hbm.at[h], raw_ref.at[h], raw_sem.at[h]) for h in range(hours)]
+    dft_copy = pltpu.make_async_copy(dft_hbm, dft_ref, table_sem.at[0])
+    band_copy = pltpu.make_async_copy(band_hbm, band_ref, table_sem.at[1])
+    for copy in raw_copies:
+        copy.start()
+    dft_copy.start()
+    band_copy.start()
+
+    out_row = lax.broadcasted_iota(jnp.int32, (owners * rows, owners), 0)
+    owner = lax.broadcasted_iota(jnp.int32, (owners * rows, owners), 1)
+    spread = (out_row // rows == owner).astype(BF16)
+    wanted = lax.dot_general(
+        spread, send_ref[...].astype(F32).astype(BF16), (((1,), (1,)), ((), ())), preferred_element_type=F32
+    )
+    out_row = lax.broadcasted_iota(jnp.int32, (owners * rows, capacity), 0)
+    place = lax.broadcasted_iota(jnp.int32, (owners * rows, capacity), 1)
+    wanted = jnp.sum(jnp.where(out_row % rows // PARTS == place, wanted, 0.0), axis=1, keepdims=True).astype(jnp.int32)
+    out_row = lax.broadcasted_iota(jnp.int32, (owners * rows, PARTS * stations), 0)
+    white_row = lax.broadcasted_iota(jnp.int32, (owners * rows, PARTS * stations), 1)
+    pick_ref[...] = (out_row % PARTS * stations + wanted == white_row).astype(BF16)
+
     time = lax.broadcasted_iota(jnp.int32, (stations, NFFT), 1)
-    for w in range(WINDOWS):
-        start = column(start_ref[0, w : w + 1, :], stations)
-        count = column(count_ref[0, w : w + 1, :], stations)
-        live = time < count
-        share = count.astype(F32)
+    for h in range(hours):
+        raw_copies[h].wait()
+        for w in range(WINDOWS):
+            start = column(start_ref[h, w : w + 1, :], stations)
+            count = column(count_ref[h, w : w + 1, :], stations)
+            live = time < count
+            share = count.astype(F32)
+            for c in range(COMPS):
+                piece = cut(raw_ref[h, c].astype(F32), start)
+                piece = jnp.where(live, piece, 0.0)
+                mean = jnp.sum(piece, axis=1, keepdims=True) / share
+                row = h * block + (w * COMPS + c) * stations
+                seg_ref[row : row + stations, :] = jnp.where(live, piece - mean, 0.0).astype(BF16)
+    dft_copy.wait()
+    band_copy.wait()
+    spec_ref[...] = jnp.dot(seg_ref[...], dft_ref[...], preferred_element_type=F32)
+    out_copies = []
+    for h in range(hours):
+        amps = []
+        for w in range(WINDOWS):
+            total = jnp.zeros((stations, NFREQ), F32)
+            for c in range(COMPS):
+                row = h * block + (w * COMPS + c) * stations
+                real = spec_ref[row : row + stations, :NFREQ]
+                imag = spec_ref[row : row + stations, NFREQ:]
+                total = total + jnp.sqrt(real * real + imag * imag)
+            amps.append(total)
+        amp = jnp.concatenate(amps, axis=0)
+        size = WINDOWS * stations
+        high = amp.astype(BF16)
+        rest = amp - high.astype(F32)
+        middle = rest.astype(BF16)
+        low = (rest - middle.astype(F32)).astype(BF16)
+        sums = jnp.dot(jnp.concatenate([high, middle, low], axis=0), band_ref[...], preferred_element_type=F32)
+        smooth = (sums[:size] + sums[size : 2 * size] + sums[2 * size :]) / (3.0 * (2 * SMOOTH_HALF + 1))
+        inverse = 1.0 / (smooth + EPS_WHITE)
         for c in range(COMPS):
-            piece = cut(raw_ref[0, c].astype(F32), start)
-            piece = jnp.where(live, piece, 0.0)
-            mean = jnp.sum(piece, axis=1, keepdims=True) / share
-            row = (w * COMPS + c) * stations
-            seg_ref[row : row + stations, :] = jnp.where(live, piece - mean, 0.0).astype(BF16)
-    spec_ref[...] = jnp.dot(seg_ref[...], dft_ref[...], preferred_element_type=F32)
-    amps = []
-    for w in range(WINDOWS):
-        total = jnp.zeros((stations, NFREQ), F32)
-        for c in range(COMPS):
-            row = (w * COMPS + c) * stations
-            real = spec_ref[row : row + stations, :NFREQ]
-            imag = spec_ref[row : row + stations, NFREQ:]
-            total = total + jnp.sqrt(real * real + imag * imag)
-        amps.append(total)
-    amp = jnp.concatenate(amps, axis=0)
-    rows = WINDOWS * stations
-    high = amp.astype(BF16)
-    rest = amp - high.astype(F32)
-    middle = rest.astype(BF16)
-    low = (rest - middle.astype(F32)).astype(BF16)
-    sums = jnp.dot(jnp.concatenate([high, middle, low], axis=0), band_ref[...], preferred_element_type=F32)
-    smooth = (sums[:rows] + sums[rows : 2 * rows] + sums[2 * rows :]) / (3.0 * (2 * SMOOTH_HALF + 1))
-    inverse = 1.0 / (smooth + EPS_WHITE)
-    for w in range(WINDOWS):
-        factor = inverse[w * stations : (w + 1) * stations]
-        for c in range(COMPS):
-            row = (w * COMPS + c) * stations
-            for r in range(2):
-                part = spec_ref[row : row + stations, r * NFREQ : (r + 1) * NFREQ] * factor
-                to = (2 * w + r) * stations
-                white_ref[to : to + stations, c * NFREQ : (c + 1) * NFREQ] = part.astype(BF16)
-    for c in range(COMPS):
-        cols = slice(c * NFREQ, (c + 1) * NFREQ)
-        picked = jnp.dot(pick_ref[...], white_ref[:, cols], preferred_element_type=F32).astype(BF16)
-        out_ref[:, :, cols] = picked.reshape(out_ref.shape[0], out_ref.shape[1], NFREQ)
+            cols = slice(c * NFREQ, (c + 1) * NFREQ)
+            for w in range(WINDOWS):
+                factor = inverse[w * stations : (w + 1) * stations]
+                row = h * block + (w * COMPS + c) * stations
+                for r in range(2):
+                    part = spec_ref[row : row + stations, r * NFREQ : (r + 1) * NFREQ] * factor
+                    to = (2 * w + r) * stations
+                    white_ref[h, to : to + stations, cols] = part.astype(BF16)
+            picked = jnp.dot(pick_ref[...], white_ref[h, :, cols], preferred_element_type=F32).astype(BF16)
+            out_ref[h, :, :, cols] = picked.reshape(owners, rows, NFREQ)
+        copy = pltpu.make_async_copy(out_ref.at[h], out_hbm.at[:, pl.ds(h * rows, rows), :], out_sem.at[h])
+        copy.start()
+        out_copies.append(copy)
+    for copy in out_copies:
+        copy.wait()
 
 
 def correlate_kernel(recv_ref, pick_ref, lag_ref, out_ref, side_ref, cross_ref, total_ref):
@@ -161,30 +200,55 @@
         out_ref[...] = total_ref[...].astype(BF16).reshape(out_ref.shape)
 
 
-def whiten(panels, starts, counts, pick, owners, rows):
+def whiten(panels, starts, counts, send):
     hours, _, stations, raw = panels.shape
+    capacity, owners = send.shape
+    rows = capacity * PARTS
     width = COMPS * NFREQ
-    whole = lambda shape: pl.BlockSpec(shape, lambda h: (0,) * len(shape))
+    block = WINDOWS * COMPS * stations
+    hbm = pl.BlockSpec(memory_space=pltpu.HBM)
+    vmem = pl.BlockSpec(memory_space=pltpu.VMEM)
     return pl.pallas_call(
         whiten_kernel,
-        grid=(hours,),
-        in_specs=[
-            pl.BlockSpec((1, COMPS, stations, raw), lambda h: (h, 0, 0, 0)),
-            pl.BlockSpec((1, WINDOWS, stations), lambda h: (h, 0, 0)),
-            pl.BlockSpec((1, WINDOWS, stations), lambda h: (h, 0, 0)),
-            whole((NFFT, 2 * NFREQ)),
-            whole((NFREQ, NFREQ)),
-            whole(pick.shape),
-        ],
-        out_specs=pl.BlockSpec((owners, rows, width), lambda h: (0, h, 0)),
+        in_specs=[hbm, vmem, vmem, vmem, hbm, hbm],
+        out_specs=hbm,
         out_shape=jax.ShapeDtypeStruct((owners, hours * rows, width), BF16),
         scratch_shapes=[
-            pltpu.VMEM((WINDOWS * COMPS * stations, NFFT), BF16),
-            pltpu.VMEM((WINDOWS * COMPS * stations, 2 * NFREQ), F32),
-            pltpu.VMEM((PARTS * stations, width), BF16),
+            pltpu.VMEM(panels.shape, BF16),
+            pltpu.VMEM((NFFT, 2 * NFREQ), BF16),
+            pltpu.VMEM((NFREQ, NFREQ), BF16),
+            pltpu.VMEM((hours * block, NFFT), BF16),
+            pltpu.VMEM((hours * block, 2 * NFREQ), F32),
+            pltpu.VMEM((hours, PARTS * stations, width), BF16),
+            pltpu.VMEM((owners * rows, PARTS * stations), BF16),
+            pltpu.VMEM((hours, owners, rows, width), BF16),
+            pltpu.SemaphoreType.DMA((hours,)),
+            pltpu.SemaphoreType.DMA((2,)),
+            pltpu.SemaphoreType.DMA((hours,)),
         ],
-        compiler_params=pltpu.CompilerParams(vmem_limit_bytes=40 * 2**20),
-    )(panels, starts, counts, dft_table(), band_table(), pick)
+        compiler_params=pltpu.CompilerParams(vmem_limit_bytes=VMEM_LIMIT),
+    )(panels, starts, counts, send, dft_table(), band_table())
+
+
+def gather_kernel(*refs):
+    part_refs, out_ref = refs[:-1], refs[-1]
+    me = lax.axis_index("hour")
+    for k, part_ref in enumerate(part_refs):
+        for far in range(2):
+            out_ref[me ^ (k + HALF_HOURS * far)] = part_ref[far].astype(F32)
+
+
+def gather(mine):
+    def swap(array, distance):
+        return lax.ppermute(array, "hour", [(i, i ^ distance) for i in range(2 * HALF_HOURS)])
+
+    both = jnp.stack([mine, swap(mine, HALF_HOURS)])
+    parts = [both] + [swap(both, k) for k in range(1, HALF_HOURS)]
+    return pl.pallas_call(
+        gather_kernel,
+        out_shape=jax.ShapeDtypeStruct((2 * HALF_HOURS,) + mine.shape, F32),
+        name="spread_result",
+    )(*parts)
 
 
 def correlate(received, pick, pairs, rows, pieces):
@@ -208,7 +272,7 @@
             pltpu.VMEM((channels * pairs, 2 * NFREQ), BF16),
             pltpu.VMEM((channels * pairs, LAGS), F32),
         ],
-        compiler_params=pltpu.CompilerParams(vmem_limit_bytes=40 * 2**20),
+        compiler_params=pltpu.CompilerParams(vmem_limit_bytes=VMEM_LIMIT),
     )(received, pick, lag_table())
 
 
@@ -219,11 +283,6 @@
     rows = capacity * PARTS
     hour_devices = lax.axis_size("hour")
 
-    wanted = jnp.broadcast_to(send_rows[0][:, :, None], (owners, capacity, PARTS)).reshape(-1, 1)
-    part = jnp.arange(owners * rows, dtype=jnp.int32)[:, None] % PARTS
-    source = jnp.arange(PARTS * stations, dtype=jnp.int32)[None, :]
-    send_pick = (part * stations + wanted == source).astype(BF16)
-
     slot = pair_slots.T[:, None, :]
     side_part = jnp.arange(PARTS, dtype=jnp.int32)[None, :, None]
     pair_rows = (slot * PARTS + side_part).reshape(-1, 1)
@@ -233,15 +292,14 @@
     panels = jnp.transpose(raw_panels, (1, 2, 0, 3))
     starts = jnp.transpose(window_start, (1, 2, 0))
     counts = jnp.transpose(valid_count, (1, 2, 0))
-    outgoing = whiten(panels, starts, counts, send_pick, owners, rows)
+    outgoing = whiten(panels, starts, counts, jnp.transpose(send_rows[0]))
     received = lax.all_to_all(outgoing, "pair", split_axis=0, concat_axis=0, tiled=True)
     partial = correlate(received, pair_pick, pairs, rows, hour_devices)
     shares = lax.all_to_all(partial, "hour", split_axis=0, concat_axis=0, tiled=True)
     average = jnp.sum(shares.astype(F32), axis=0) / (hours * hour_devices)
     size = jnp.abs(average) + 0.1
     stacked = (jnp.sign(average) * (size * size - 0.01)).astype(BF16)
-    stacked = lax.all_gather(stacked, "hour", axis=0, tiled=True, axis_index_groups=[list(range(hour_devices))])
-    stacked = stacked.reshape(COMPS * COMPS, pairs, LAGS).astype(F32)
+    stacked = gather(stacked).reshape(COMPS * COMPS, pairs, LAGS)
     return jnp.transpose(stacked, (1, 0, 2))
 
 

time: 141 us -> 127 us (0.901)
  blocking collectives: 45.7 us -> 20.8 us
  waiting for transfers between devices: 62.4 us -> 72.2 us
  local copies, waits for them, and re-layouts: 8.45 us -> 0.72 us
  starting transfers between devices: 7.71 us -> 12.7 us
  Pallas kernels: 14.5 us -> 19.2 us
    all_gather x1 -> x0, blocking collectives: 25.1 us -> none  [local(): lax.all_gather(stacked, 'hour', axis=0, tiled=True, axis_index_groups=[li...]
    ppermute x0 -> x4, waiting for transfers between devices: none -> 10.6 us  [swap(): lax.ppermute(array, 'hour', [(i, i ^ distance) for i in range(2 * HALF_HO...]
    unnamed x16 -> x10, local copies, waits for them, and re-layouts: 7.39 us -> 0.64 us
    ppermute x0 -> x4, starting transfers between devices: none -> 5.12 us  [swap(): lax.ppermute(array, 'hour', [(i, i ^ distance) for i in range(2 * HALF_HO...]
    pallas_call x1 -> x2, Pallas kernels: 6.39 us -> 10.2 us  [the longest x1 8.3 us: whiten(): pl.pallas_call(whiten_kernel, in_specs=[hbm, vmem, vmem, vmem, hbm, hbm],...]
  transfers between devices with their start and end apart: 1 -> 5, of which waited for: 1 -> 4; matrix products, arithmetic and copies ran while one was open for 0% -> 1% of each run, Pallas kernels for 0% -> 0%
where the time goes in v2:
time: 127 us
  waiting for transfers between devices  72.2 us (57%)
  blocking collectives  20.8 us (16%)
  Pallas kernels  19.2 us (15%)
  starting transfers between devices  12.7 us (10%)
    all_to_all x1, waiting for transfers between devices, local(): lax.all_to_all(outgoing, 'pair', split_axis=0, concat_axis=0, tiled=True)  61.6 us
    all_to_all x1, blocking collectives, local(): lax.all_to_all(partial, 'hour', split_axis=0, concat_axis=0, tiled=True)  20.8 us
    ppermute x4, waiting for transfers between devices, swap(): lax.ppermute(array, 'hour', [(i, i ^ distance) for i in range(2 * HALF_HO...  10.6 us
    pallas_call x1, Pallas kernels, correlate(): pl.pallas_call(correlate_kernel, grid=(hours,), in_specs=[pl.BlockSpec((o...  9.08 us
    pallas_call x1, Pallas kernels, whiten(): pl.pallas_call(whiten_kernel, in_specs=[hbm, vmem, vmem, vmem, hbm, hbm],...  8.3 us
    all_to_all x1, starting transfers between devices, local(): lax.all_to_all(outgoing, 'pair', split_axis=0, concat_axis=0, tiled=True)  7.59 us
    ppermute x4, starting transfers between devices, swap(): lax.ppermute(array, 'hour', [(i, i ^ distance) for i in range(2 * HALF_HO...  5.12 us
  transfers between devices with their start and end apart: 5, of which 4 were waited for; matrix products, arithmetic and copies ran while one was open for 1% of the time, Pallas kernels for 0%

profile of v2, /device:TPU:8, one launch (start us, length us, event | category | flops | bytes accessed | tf_op | source)
XLA Modules:
  0.0 126.9 jit_solution(2766094483055177218)
XLA Ops:
  0.0 8.3 %shard_map.82 = bf16[32,48,1536]{2,1,0:T(8,128)(2,1)} custom-call(bf16[3,3,16,3712]{3,2,1,0:T(8,128)(2,1)} %bitcast.14, s32[3,2,16]{2,1,0:T(2,128)} %bitcast.16, s32[3,2,16]{2,1,0:T(2,128)} %bitcast.17, s32[4,32]{1,0:T(4,128)} %bitcast.18, bf16[1024,1024]{1,0:T(8,128)(2,1)} %constant.18.clone.dft_hbm, bf16[512,512]{1,0:T(8,128)(2,1)} %constant.19.clone.band_hbm), custom_call_target="tpu_custom_call" | custom-call | tf_op jit(solution)/shard_map/pallas_call | solution.py:211
  8.3 0.0 copy-start.4
  8.3 7.6 %all-to-all-start = ((bf16[32,48,1536]{2,1,0:T(8,128)(2,1)}), bf16[32,48,1536]{2,1,0:T(8,128)(2,1)}, u32[]{:S(2)}, u32[]{:S(2)}) async-start(bf16[32,48,1536]{2,1,0:T(8,128)(2,1)} %shard_map.82), calls=%async_computation | async-start | bytes 9437184 | tf_op jit(solution)/shard_map/all_to_all | solution.py:296
  15.9 0.0 copy-done.4
  15.9 0.1 add.45
  16.0 0.9 fusion.pick_ref
  17.0 61.6 %all-to-all-done.recv_ref = bf16[32,48,1536]{2,1,0:T(8,128)(2,1)} async-done(((bf16[32,48,1536]{2,1,0:T(8,128)(2,1)}), bf16[32,48,1536]{2,1,0:T(8,128)(2,1)}, u32[]{:S(2)}, u32[]{:S(2)}) %all-to-all-start) | async-done | bytes 4718624 | tf_op jit(solution)/shard_map/all_to_all | solution.py:296
  78.6 9.1 %shard_map.83 = bf16[8,72,256]{2,1,0:T(8,128)(2,1)} custom-call(bf16[32,48,1536]{2,1,0:T(8,128)(2,1)} %all-to-all-done.recv_ref, bf16[512,512]{1,0:T(8,128)(2,1)} %fusion.pick_ref, bf16[1024,256]{1,0:T(8,128)(2,1)} %constant.20.clone.lag_ref), custom_call_target="tpu_custom_call" | custom-call | tf_op jit(solution)/shard_map/pallas_call | solution.py:260
  87.7 20.8 %all_to_all.10 = bf16[8,72,256]{2,1,0:T(8,128)(2,1)S(1)} all-to-all(bf16[8,72,256]{2,1,0:T(8,128)(2,1)} %shard_map.83), channel_id=1, replica_groups=mesh['hour'=8,'pair'=32] {'hour'}, dimensions={0} | all-to-all | bytes 589824 | tf_op jit(solution)/shard_map/all_to_all | solution.py:298
  108.6 0.7 collective-permute-start
  109.3 7.4 %collective-permute-done = bf16[72,256]{1,0:T(8,128)(2,1)S(1)} collective-permute-done((bf16[72,256]{1,0:T(8,128)(2,1)S(1)}, bf16[72,256]{1,0:T(8,128)(2,1)S(1)}, u32[]{:S(2)}, u32[]{:S(2)}) %collective-permute-start) | collective-permute-done | bytes 36896 | tf_op jit(solution)/shard_map/ppermute | solution.py:243
  116.7 0.0 copy-start
  116.7 0.9 collective-permute-start.1
  117.6 0.2 collective-permute-start.2
  117.7 3.4 %collective-permute-start.3 = (bf16[2,72,256]{2,1,0:T(8,128)(2,1)S(1)}, bf16[2,72,256]{2,1,0:T(8,128)(2,1)S(1)}, u32[]{:S(2)}, u32[]{:S(2)}) collective-permute-start(bf16[2,72,256]{2,1,0:T(8,128)(2,1)S(1)} %pad_maximum_fusion.refs_0_), channel_id=1, source_target_pairs={{0,96},{32,64},{64,32},{96,0},{128,224},{160,192},{192,160},{224,1... | collective-permute-start | bytes 221192 | tf_op jit(solution)/shard_map/ppermute | solution.py:243
  121.2 0.0 collective-permute-done.1.refs_1_
  121.2 1.6 %collective-permute-done.2.refs_2_ = bf16[2,72,256]{2,1,0:T(8,128)(2,1)S(1)} collective-permute-done((bf16[2,72,256]{2,1,0:T(8,128)(2,1)S(1)}, bf16[2,72,256]{2,1,0:T(8,128)(2,1)S(1)}, u32[]{:S(2)}, u32[]{:S(2)}) %collective-permute-start.2) | collective-permute-done | bytes 73760 | tf_op jit(solution)/shard_map/ppermute | solution.py:243
  122.8 1.6 %collective-permute-done.3.refs_3_ = bf16[2,72,256]{2,1,0:T(8,128)(2,1)S(1)} collective-permute-done((bf16[2,72,256]{2,1,0:T(8,128)(2,1)S(1)}, bf16[2,72,256]{2,1,0:T(8,128)(2,1)S(1)}, u32[]{:S(2)}, u32[]{:S(2)}) %collective-permute-start.3) | collective-permute-done | bytes 73760 | tf_op jit(solution)/shard_map/ppermute | solution.py:243
  124.4 0.0 copy-done
  124.4 0.0 copy-done.1
  124.4 0.0 copy-done.2
  124.4 0.0 copy-start.3
  124.4 0.6 copy-done.3
  125.0 1.9 %spread_result.1 = f32[8,72,256]{2,1,0:T(8,128)} custom-call(bf16[2,72,256]{2,1,0:T(8,128)(2,1)} %copy-done, bf16[2,72,256]{2,1,0:T(8,128)(2,1)} %copy-done.1, bf16[2,72,256]{2,1,0:T(8,128)(2,1)} %copy-done.2, bf16[2,72,256]{2,1,0:T(8,128)(2,1)} %copy-done.3), custom_call_target="tpu_custom_call" | custom-call | tf_op jit(solution)/shard_map/spread_result/pallas_call | solution.py:247
  (8 shorter events, 0.1 us)
Async XLA Ops:
  8.3 7.6 %copy-start.4 = (s32[64,2]{0,1:T(2,128)S(1)}, s32[64,2]{0,1:T(2,128)}, u32[]{:S(2)}) copy-start(s32[64,2]{0,1:T(2,128)} %param.12) | copy-start | bytes 1540
  8.3 70.3 %all-to-all-start = ((bf16[32,48,1536]{2,1,0:T(8,128)(2,1)}), bf16[32,48,1536]{2,1,0:T(8,128)(2,1)}, u32[]{:S(2)}, u32[]{:S(2)}) async-start(bf16[32,48,1536]{2,1,0:T(8,128)(2,1)} %shard_map.82), calls=%async_computation | async-start | bytes 9437184 | tf_op jit(solution)/shard_map/all_to_all | solution.py:296
  108.6 8.1 %collective-permute-start = (bf16[72,256]{1,0:T(8,128)(2,1)S(1)}, bf16[72,256]{1,0:T(8,128)(2,1)S(1)}, u32[]{:S(2)}, u32[]{:S(2)}) collective-permute-start(bf16[72,256]{1,0:T(8,128)(2,1)S(1)} %multiply_convert_fusion), channel_id=1, source_target_pairs={{0,128},{32,160},{64,192},{96,224},{128,0},{160,32},{192,64},{224,... | collective-permute-start | bytes 110600 | tf_op jit(solution)/shard_map/ppermute | solution.py:243
  116.7 7.7 %copy-start = (bf16[2,72,256]{2,1,0:T(8,128)(2,1)}, bf16[2,72,256]{2,1,0:T(8,128)(2,1)S(1)}, u32[]{:S(2)}) copy-start(bf16[2,72,256]{2,1,0:T(8,128)(2,1)S(1)} %pad_maximum_fusion.refs_0_) | copy-start | bytes 221188
  116.7 4.5 %collective-permute-start.1 = (bf16[2,72,256]{2,1,0:T(8,128)(2,1)S(1)}, bf16[2,72,256]{2,1,0:T(8,128)(2,1)S(1)}, u32[]{:S(2)}, u32[]{:S(2)}) collective-permute-start(bf16[2,72,256]{2,1,0:T(8,128)(2,1)S(1)} %pad_maximum_fusion.refs_0_), channel_id=1, source_target_pairs={{0,32},{32,0},{64,96},{96,64},{128,160},{160,128},{192,224},{224,1... | collective-permute-start | bytes 221192 | tf_op jit(solution)/shard_map/ppermute | solution.py:243
  117.6 5.3 %collective-permute-start.2 = (bf16[2,72,256]{2,1,0:T(8,128)(2,1)S(1)}, bf16[2,72,256]{2,1,0:T(8,128)(2,1)S(1)}, u32[]{:S(2)}, u32[]{:S(2)}) collective-permute-start(bf16[2,72,256]{2,1,0:T(8,128)(2,1)S(1)} %pad_maximum_fusion.refs_0_), channel_id=1, source_target_pairs={{0,64},{32,96},{64,0},{96,32},{128,192},{160,224},{192,128},{224,1... | collective-permute-start | bytes 221192 | tf_op jit(solution)/shard_map/ppermute | solution.py:243
  117.7 6.7 %collective-permute-start.3 = (bf16[2,72,256]{2,1,0:T(8,128)(2,1)S(1)}, bf16[2,72,256]{2,1,0:T(8,128)(2,1)S(1)}, u32[]{:S(2)}, u32[]{:S(2)}) collective-permute-start(bf16[2,72,256]{2,1,0:T(8,128)(2,1)S(1)} %pad_maximum_fusion.refs_0_), channel_id=1, source_target_pairs={{0,96},{32,64},{64,32},{96,0},{128,224},{160,192},{192,160},{224,1... | collective-permute-start | bytes 221192 | tf_op jit(solution)/shard_map/ppermute | solution.py:243
  121.2 3.2 %copy-start.1 = (bf16[2,72,256]{2,1,0:T(8,128)(2,1)}, bf16[2,72,256]{2,1,0:T(8,128)(2,1)S(1)}, u32[]{:S(2)}) copy-start(bf16[2,72,256]{2,1,0:T(8,128)(2,1)S(1)} %collective-permute-done.1.refs_1_) | copy-start | bytes 221188
  122.8 1.6 %copy-start.2 = (bf16[2,72,256]{2,1,0:T(8,128)(2,1)}, bf16[2,72,256]{2,1,0:T(8,128)(2,1)S(1)}, u32[]{:S(2)}) copy-start(bf16[2,72,256]{2,1,0:T(8,128)(2,1)S(1)} %collective-permute-done.2.refs_2_) | copy-start | bytes 221188
  124.4 0.6 copy-start.3

commit v3 on v2

--- a/solution.py
+++ b/solution.py
@@ -19,7 +19,9 @@
 SMOOTH_HALF = 11
 EPS_WHITE = 1e-06
 HALF_HOURS = 4
-VMEM_LIMIT = 60 * 2**20
+WHITEN_VMEM = 58 * 2**20
+CORRELATE_VMEM = 24 * 2**20
+SPREAD_VMEM = 8 * 2**20
 F32 = jnp.float32
 BF16 = jnp.bfloat16
 
@@ -73,20 +75,28 @@
 
 
 def whiten_kernel(
-    raw_hbm, start_ref, count_ref, send_ref, dft_hbm, band_hbm, out_hbm,
-    raw_ref, dft_ref, band_ref, seg_ref, spec_ref, white_ref, pick_ref, out_ref, raw_sem, table_sem, out_sem,
+    raw_hbm, start_hbm, count_hbm, send_hbm, dft_hbm, band_hbm, out_hbm,
+    raw_ref, start_ref, count_ref, send_ref, dft_ref, band_ref, seg_ref, spec_ref, white_ref, pick_ref, out_ref,
+    small_sem, raw_sem, table_sem, out_sem,
 ):
     hours, _, stations, _ = raw_ref.shape
     capacity, owners = send_ref.shape
     rows = capacity * PARTS
     block = COMPS * WINDOWS * stations
+    small_copies = [
+        pltpu.make_async_copy(start_hbm, start_ref, small_sem.at[0]),
+        pltpu.make_async_copy(count_hbm, count_ref, small_sem.at[1]),
+        pltpu.make_async_copy(send_hbm, send_ref, small_sem.at[2]),
+    ]
     raw_copies = [pltpu.make_async_copy(raw_hbm.at[h], raw_ref.at[h], raw_sem.at[h]) for h in range(hours)]
     dft_copy = pltpu.make_async_copy(dft_hbm, dft_ref, table_sem.at[0])
     band_copy = pltpu.make_async_copy(band_hbm, band_ref, table_sem.at[1])
-    for copy in raw_copies:
+    for copy in small_copies + raw_copies:
         copy.start()
     dft_copy.start()
     band_copy.start()
+    for copy in small_copies:
+        copy.wait()
 
     out_row = lax.broadcasted_iota(jnp.int32, (owners * rows, owners), 0)
     owner = lax.broadcasted_iota(jnp.int32, (owners * rows, owners), 1)
@@ -117,8 +127,8 @@
                 seg_ref[row : row + stations, :] = jnp.where(live, piece - mean, 0.0).astype(BF16)
     dft_copy.wait()
     band_copy.wait()
+    out_copies = []
     spec_ref[...] = jnp.dot(seg_ref[...], dft_ref[...], preferred_element_type=F32)
-    out_copies = []
     for h in range(hours):
         amps = []
         for w in range(WINDOWS):
@@ -156,48 +166,64 @@
         copy.wait()
 
 
-def correlate_kernel(recv_ref, pick_ref, lag_ref, out_ref, side_ref, cross_ref, total_ref):
-    hour = pl.program_id(0)
-    pairs = total_ref.shape[0] // (COMPS * COMPS)
-    slots = recv_ref.shape[0] * recv_ref.shape[1]
-    width = recv_ref.shape[2]
-    for c in range(COMPS):
-        cols = slice(c * NFREQ, (c + 1) * NFREQ)
-        arrived = recv_ref[:, :, cols].reshape(slots, NFREQ)
-        side_ref[:, cols] = jnp.dot(pick_ref[...], arrived, preferred_element_type=F32)
-
-    for k in range(0, pairs, 16):
-        for f in range(0, NFREQ, 128):
-            def load(side, part, comp):
-                row = (side * PARTS + part) * pairs + k
-                col = comp * NFREQ + f
-                return side_ref[row : row + 16, col : col + 128]
-            left = [[load(0, part, comp) for comp in range(COMPS)] for part in range(PARTS)]
-            right = [[load(1, part, comp) for comp in range(COMPS)] for part in range(PARTS)]
-            for i in range(COMPS):
-                for j in range(COMPS):
-                    real = left[0][i] * right[0][j] + left[2][i] * right[2][j]
-                    real = real + (left[1][i] * right[1][j] + left[3][i] * right[3][j])
-                    imag = left[1][i] * right[0][j] + left[3][i] * right[2][j]
-                    imag = imag - (left[0][i] * right[1][j] + left[2][i] * right[3][j])
-                    row = (COMPS * i + j) * pairs + k
-                    cross_ref[row : row + 16, f : f + 128] = real.astype(BF16)
-                    cross_ref[row : row + 16, NFREQ + f : NFREQ + f + 128] = imag.astype(BF16)
-    lagged = jnp.dot(cross_ref[...], lag_ref[...], preferred_element_type=F32)
-    root = jnp.sqrt(jnp.abs(lagged) + 0.01) - 0.1
-    root = jnp.where(lagged > 0.0, root, jnp.where(lagged < 0.0, -root, 0.0))
-
-    @pl.when(hour == 0)
-    def _():
-        total_ref[...] = root
-
-    @pl.when(hour > 0)
-    def _():
-        total_ref[...] += root
-
-    @pl.when(hour == pl.num_programs(0) - 1)
-    def _():
-        out_ref[...] = total_ref[...].astype(BF16).reshape(out_ref.shape)
+def correlate_kernel(recv_ref, slots_ref, lag_hbm, out_ref, pick_ref, lag_ref, side_ref, cross_ref, total_ref, sem):
+    pairs = slots_ref.shape[1]
+    owners, all_rows, _ = recv_ref.shape
+    rows = all_rows // cross_ref.shape[0]
+    half = NFREQ // 2
+    lag_copy = pltpu.make_async_copy(lag_hbm, lag_ref, sem)
+    lag_copy.start()
+
+    arrived_row = lax.broadcasted_iota(jnp.int32, (pairs, owners * rows), 1)
+    for side in range(2):
+        first = column(slots_ref[side : side + 1, :], pairs) * PARTS
+        for part in range(PARTS):
+            row = (side * PARTS + part) * pairs
+            pick_ref[row : row + pairs, :] = (first + part == arrived_row).astype(BF16)
+
+    def select(h, n):
+        for c in range(COMPS):
+            col = c * NFREQ + n * half
+            arrived = recv_ref[:, h * rows : (h + 1) * rows, col : col + half].reshape(owners * rows, half)
+            side_ref[n, :, c * half : (c + 1) * half] = jnp.dot(pick_ref[...], arrived, preferred_element_type=F32)
+
+    def cross(h, n):
+        for k in range(0, pairs, 16):
+            for f in range(0, half, 128):
+                def load(side, part, comp):
+                    row = (side * PARTS + part) * pairs + k
+                    col = comp * half + f
+                    return side_ref[n, row : row + 16, col : col + 128]
+                left = [[load(0, part, comp) for comp in range(COMPS)] for part in range(PARTS)]
+                right = [[load(1, part, comp) for comp in range(COMPS)] for part in range(PARTS)]
+                for i in range(COMPS):
+                    for j in range(COMPS):
+                        real = left[0][i] * right[0][j] + left[2][i] * right[2][j]
+                        real = real + (left[1][i] * right[1][j] + left[3][i] * right[3][j])
+                        imag = left[1][i] * right[0][j] + left[3][i] * right[2][j]
+                        imag = imag - (left[0][i] * right[1][j] + left[2][i] * right[3][j])
+                        row = (COMPS * i + j) * pairs + k
+                        col = n * half + f
+                        cross_ref[h, row : row + 16, col : col + 128] = real.astype(BF16)
+                        cross_ref[h, row : row + 16, NFREQ + col : NFREQ + col + 128] = imag.astype(BF16)
+
+    def root(h):
+        lagged = jnp.dot(cross_ref[h], lag_ref[...], preferred_element_type=F32)
+        rooted = jnp.sqrt(jnp.abs(lagged) + 0.01) - 0.1
+        rooted = jnp.where(lagged > 0.0, rooted, jnp.where(lagged < 0.0, -rooted, 0.0))
+        if h == 0:
+            total_ref[...] = rooted
+        elif h < cross_ref.shape[0] - 1:
+            total_ref[...] += rooted
+        else:
+            out_ref[...] = (total_ref[...] + rooted).astype(BF16).reshape(out_ref.shape)
+
+    lag_copy.wait()
+    for h in range(cross_ref.shape[0]):
+        for n in range(2):
+            select(h, n)
+            cross(h, n)
+        root(h)
 
 
 def whiten(panels, starts, counts, send):
@@ -207,14 +233,16 @@
     width = COMPS * NFREQ
     block = WINDOWS * COMPS * stations
     hbm = pl.BlockSpec(memory_space=pltpu.HBM)
-    vmem = pl.BlockSpec(memory_space=pltpu.VMEM)
     return pl.pallas_call(
         whiten_kernel,
-        in_specs=[hbm, vmem, vmem, vmem, hbm, hbm],
+        in_specs=[hbm] * 6,
         out_specs=hbm,
         out_shape=jax.ShapeDtypeStruct((owners, hours * rows, width), BF16),
         scratch_shapes=[
             pltpu.VMEM(panels.shape, BF16),
+            pltpu.VMEM(starts.shape, jnp.int32),
+            pltpu.VMEM(counts.shape, jnp.int32),
+            pltpu.VMEM(send.shape, jnp.int32),
             pltpu.VMEM((NFFT, 2 * NFREQ), BF16),
             pltpu.VMEM((NFREQ, NFREQ), BF16),
             pltpu.VMEM((hours * block, NFFT), BF16),
@@ -222,11 +250,12 @@
             pltpu.VMEM((hours, PARTS * stations, width), BF16),
             pltpu.VMEM((owners * rows, PARTS * stations), BF16),
             pltpu.VMEM((hours, owners, rows, width), BF16),
+            pltpu.SemaphoreType.DMA((3,)),
             pltpu.SemaphoreType.DMA((hours,)),
             pltpu.SemaphoreType.DMA((2,)),
             pltpu.SemaphoreType.DMA((hours,)),
         ],
-        compiler_params=pltpu.CompilerParams(vmem_limit_bytes=VMEM_LIMIT),
+        compiler_params=pltpu.CompilerParams(vmem_limit_bytes=WHITEN_VMEM),
     )(panels, starts, counts, send, dft_table(), band_table())
 
 
@@ -247,54 +276,44 @@
     return pl.pallas_call(
         gather_kernel,
         out_shape=jax.ShapeDtypeStruct((2 * HALF_HOURS,) + mine.shape, F32),
+        compiler_params=pltpu.CompilerParams(vmem_limit_bytes=SPREAD_VMEM),
         name="spread_result",
     )(*parts)
 
 
-def correlate(received, pick, pairs, rows, pieces):
+def correlate(received, slots, hours, pieces):
     owners, all_rows, width = received.shape
-    hours = all_rows // rows
+    pairs = slots.shape[1]
+    rows = all_rows // hours
     channels = COMPS * COMPS
-    whole = lambda shape: pl.BlockSpec(shape, lambda h: (0,) * len(shape))
-    piece = (pieces, channels * pairs // pieces, LAGS)
+    vmem = pl.BlockSpec(memory_space=pltpu.VMEM)
     return pl.pallas_call(
         correlate_kernel,
-        grid=(hours,),
-        in_specs=[
-            pl.BlockSpec((owners, rows, width), lambda h: (0, h, 0)),
-            whole(pick.shape),
-            whole((2 * NFREQ, LAGS)),
+        in_specs=[vmem, vmem, pl.BlockSpec(memory_space=pltpu.HBM)],
+        out_specs=vmem,
+        out_shape=jax.ShapeDtypeStruct((pieces, channels * pairs // pieces, LAGS), BF16),
+        scratch_shapes=[
+            pltpu.VMEM((2 * PARTS * pairs, owners * rows), BF16),
+            pltpu.VMEM((2 * NFREQ, LAGS), BF16),
+            pltpu.VMEM((2, 2 * PARTS * pairs, width // 2), F32),
+            pltpu.VMEM((hours, channels * pairs, 2 * NFREQ), BF16),
+            pltpu.VMEM((channels * pairs, LAGS), F32),
+            pltpu.SemaphoreType.DMA(()),
         ],
-        out_specs=whole(piece),
-        out_shape=jax.ShapeDtypeStruct(piece, BF16),
-        scratch_shapes=[
-            pltpu.VMEM((2 * PARTS * pairs, width), F32),
-            pltpu.VMEM((channels * pairs, 2 * NFREQ), BF16),
-            pltpu.VMEM((channels * pairs, LAGS), F32),
-        ],
-        compiler_params=pltpu.CompilerParams(vmem_limit_bytes=VMEM_LIMIT),
-    )(received, pick, lag_table())
+        compiler_params=pltpu.CompilerParams(vmem_limit_bytes=CORRELATE_VMEM),
+    )(received, slots, lag_table())
 
 
 def local(raw_panels, window_start, valid_count, send_rows, pair_slots):
-    stations, hours = raw_panels.shape[:2]
-    owners, capacity = send_rows.shape[1:]
+    hours = raw_panels.shape[1]
     pairs = pair_slots.shape[0]
-    rows = capacity * PARTS
     hour_devices = lax.axis_size("hour")
-
-    slot = pair_slots.T[:, None, :]
-    side_part = jnp.arange(PARTS, dtype=jnp.int32)[None, :, None]
-    pair_rows = (slot * PARTS + side_part).reshape(-1, 1)
-    arrived = jnp.arange(owners * rows, dtype=jnp.int32)[None, :]
-    pair_pick = (pair_rows == arrived).astype(BF16)
-
     panels = jnp.transpose(raw_panels, (1, 2, 0, 3))
     starts = jnp.transpose(window_start, (1, 2, 0))
     counts = jnp.transpose(valid_count, (1, 2, 0))
     outgoing = whiten(panels, starts, counts, jnp.transpose(send_rows[0]))
     received = lax.all_to_all(outgoing, "pair", split_axis=0, concat_axis=0, tiled=True)
-    partial = correlate(received, pair_pick, pairs, rows, hour_devices)
+    partial = correlate(received, jnp.transpose(pair_slots), hours, hour_devices)
     shares = lax.all_to_all(partial, "hour", split_axis=0, concat_axis=0, tiled=True)
     average = jnp.sum(shares.astype(F32), axis=0) / (hours * hour_devices)
     size = jnp.abs(average) + 0.1

time: 127 us -> 116 us (0.913)
  blocking collectives: 20.8 us -> 84.1 us
  waiting for transfers between devices: 72.2 us -> 10.9 us
  starting transfers between devices: 12.7 us -> 5.12 us
  Pallas kernels: 19.2 us -> 15.2 us
    all_to_all x0 -> x1, blocking collectives: none -> 62.7 us  [local(): lax.all_to_all(outgoing, 'pair', split_axis=0, concat_axis=0, tiled=True)]
    all_to_all x1 -> x0, waiting for transfers between devices: 61.6 us -> none  [local(): lax.all_to_all(outgoing, 'pair', split_axis=0, concat_axis=0, tiled=True)]
    all_to_all x1 -> x0, starting transfers between devices: 7.59 us -> none  [local(): lax.all_to_all(outgoing, 'pair', split_axis=0, concat_axis=0, tiled=True)]
    pallas_call x2, Pallas kernels: 17.4 us -> 14.4 us  [the longest x1 8.36 us: whiten(): pl.pallas_call(whiten_kernel, in_specs=[hbm] * 6, out_specs=hbm, out_shap...]
  transfers between devices with their start and end apart: 5 -> 4, of which waited for: 4 -> 3; matrix products, arithmetic and copies ran while one was open for 1% -> 0% of each run, Pallas kernels for 0% -> 0%
where the time goes in v3:
time: 116 us
  blocking collectives  84.1 us (72%)
  Pallas kernels  15.2 us (13%)
  waiting for transfers between devices  10.9 us (9%)
  starting transfers between devices  5.12 us (4%)
    all_to_all x1, blocking collectives, local(): lax.all_to_all(outgoing, 'pair', split_axis=0, concat_axis=0, tiled=True)  62.7 us
    all_to_all x1, blocking collectives, local(): lax.all_to_all(partial, 'hour', split_axis=0, concat_axis=0, tiled=True)  21.4 us
    ppermute x4, waiting for transfers between devices, swap(): lax.ppermute(array, 'hour', [(i, i ^ distance) for i in range(2 * HALF_HO...  10.9 us
    pallas_call x1, Pallas kernels, whiten(): pl.pallas_call(whiten_kernel, in_specs=[hbm] * 6, out_specs=hbm, out_shap...  8.36 us
    pallas_call x1, Pallas kernels, correlate(): pl.pallas_call(correlate_kernel, in_specs=[vmem, vmem, pl.BlockSpec(memor...  6.01 us
    ppermute x4, starting transfers between devices, swap(): lax.ppermute(array, 'hour', [(i, i ^ distance) for i in range(2 * HALF_HO...  5.12 us
  transfers between devices with their start and end apart: 4, of which 3 were waited for; matrix products, arithmetic and copies ran while one was open for 0% of the time, Pallas kernels for 0%

profile of v3, /device:TPU:8, one launch (start us, length us, event | category | flops | bytes accessed | tf_op | source)
XLA Modules:
  0.0 115.6 jit_solution(17390984023545800460)
XLA Ops:
  0.0 8.4 %shard_map.82 = bf16[32,48,1536]{2,1,0:T(8,128)(2,1)} custom-call(bf16[3,3,16,3712]{3,2,1,0:T(8,128)(2,1)} %bitcast.14, s32[3,2,16]{2,1,0:T(2,128)} %bitcast.16, s32[3,2,16]{2,1,0:T(2,128)} %bitcast.17, s32[4,32]{1,0:T(4,128)} %bitcast.18, bf16[1024,1024]{1,0:T(8,128)(2,1)} %constant.16.clone.dft_hbm, bf16[512,512]{1,0:T(8,128)(2,1)} %constant.17.clone.band_hbm), custom_call_target="tpu_custom_call" | custom-call | tf_op jit(solution)/shard_map/pallas_call | solution.py:236
  8.4 0.0 copy-start
  8.4 0.0 copy-start.1
  8.4 62.7 %all_to_all.10.recv_ref = bf16[32,48,1536]{2,1,0:T(8,128)(2,1)S(1)} all-to-all(bf16[32,48,1536]{2,1,0:T(8,128)(2,1)} %shard_map.82), channel_id=1, replica_groups=mesh['hour'=8,'pair'=32] {'pair'}, dimensions={0} | all-to-all | bytes 9437184 | tf_op jit(solution)/shard_map/all_to_all | solution.py:315
  71.1 0.0 copy-done
  71.1 0.0 copy-done.1
  71.1 6.0 %shard_map.83 = bf16[8,72,256]{2,1,0:T(8,128)(2,1)S(1)} custom-call(bf16[32,48,1536]{2,1,0:T(8,128)(2,1)S(1)} %all_to_all.10.recv_ref, s32[2,64]{1,0:T(2,128)S(1)} %bitcast.13, bf16[1024,256]{1,0:T(8,128)(2,1)S(1)} %copy-done), custom_call_target="tpu_custom_call" | custom-call | tf_op jit(solution)/shard_map/pallas_call | solution.py:290
  77.2 21.4 %all_to_all.11 = bf16[8,72,256]{2,1,0:T(8,128)(2,1)S(1)} all-to-all(bf16[8,72,256]{2,1,0:T(8,128)(2,1)S(1)} %shard_map.83), channel_id=1, replica_groups=mesh['hour'=8,'pair'=32] {'hour'}, dimensions={0} | all-to-all | bytes 589824 | tf_op jit(solution)/shard_map/all_to_all | solution.py:317
  98.6 0.7 collective-permute-start
  99.3 7.6 %collective-permute-done = bf16[72,256]{1,0:T(8,128)(2,1)S(1)} collective-permute-done((bf16[72,256]{1,0:T(8,128)(2,1)S(1)}, bf16[72,256]{1,0:T(8,128)(2,1)S(1)}, u32[]{:S(2)}, u32[]{:S(2)}) %collective-permute-start) | collective-permute-done | bytes 36896 | tf_op jit(solution)/shard_map/ppermute | solution.py:272
  106.9 0.3 collective-permute-start.3
  107.2 1.8 %collective-permute-start.2 = (bf16[2,72,256]{2,1,0:T(8,128)(2,1)S(1)}, bf16[2,72,256]{2,1,0:T(8,128)(2,1)S(1)}, u32[]{:S(2)}, u32[]{:S(2)}) collective-permute-start(bf16[2,72,256]{2,1,0:T(8,128)(2,1)S(1)} %pad_maximum_fusion.refs_0_), channel_id=1, source_target_pairs={{0,64},{32,96},{64,0},{96,32},{128,192},{160,224},{192,128},{224,1... | collective-permute-start | bytes 221192 | tf_op jit(solution)/shard_map/ppermute | solution.py:272
  109.0 2.3 %collective-permute-start.1 = (bf16[2,72,256]{2,1,0:T(8,128)(2,1)S(1)}, bf16[2,72,256]{2,1,0:T(8,128)(2,1)S(1)}, u32[]{:S(2)}, u32[]{:S(2)}) collective-permute-start(bf16[2,72,256]{2,1,0:T(8,128)(2,1)S(1)} %pad_maximum_fusion.refs_0_), channel_id=1, source_target_pairs={{0,32},{32,0},{64,96},{96,64},{128,160},{160,128},{192,224},{224,1... | collective-permute-start | bytes 221192 | tf_op jit(solution)/shard_map/ppermute | solution.py:272
  111.3 1.9 %collective-permute-done.3.refs_3_ = bf16[2,72,256]{2,1,0:T(8,128)(2,1)S(1)} collective-permute-done((bf16[2,72,256]{2,1,0:T(8,128)(2,1)S(1)}, bf16[2,72,256]{2,1,0:T(8,128)(2,1)S(1)}, u32[]{:S(2)}, u32[]{:S(2)}) %collective-permute-start.3) | collective-permute-done | bytes 73760 | tf_op jit(solution)/shard_map/ppermute | solution.py:272
  113.3 1.4 %collective-permute-done.2.refs_2_ = bf16[2,72,256]{2,1,0:T(8,128)(2,1)S(1)} collective-permute-done((bf16[2,72,256]{2,1,0:T(8,128)(2,1)S(1)}, bf16[2,72,256]{2,1,0:T(8,128)(2,1)S(1)}, u32[]{:S(2)}, u32[]{:S(2)}) %collective-permute-start.2) | collective-permute-done | bytes 73760 | tf_op jit(solution)/shard_map/ppermute | solution.py:272
  114.7 0.0 collective-permute-done.1.refs_1_
  114.7 0.9 spread_result.1
  (4 shorter events, 0.1 us)
Async XLA Ops:
  8.4 62.8 %copy-start = (bf16[1024,256]{1,0:T(8,128)(2,1)S(1)}, bf16[1024,256]{1,0:T(8,128)(2,1)}, u32[]{:S(2)}) copy-start(bf16[1024,256]{1,0:T(8,128)(2,1)} %constant.18.clone.lag_hbm) | copy-start | bytes 1572868
  8.4 62.8 %copy-start.1 = (s32[64,2]{0,1:T(2,128)S(1)}, s32[64,2]{0,1:T(2,128)}, u32[]{:S(2)}) copy-start(s32[64,2]{0,1:T(2,128)} %param.12) | copy-start | bytes 1540
  98.6 8.3 %collective-permute-start = (bf16[72,256]{1,0:T(8,128)(2,1)S(1)}, bf16[72,256]{1,0:T(8,128)(2,1)S(1)}, u32[]{:S(2)}, u32[]{:S(2)}) collective-permute-start(bf16[72,256]{1,0:T(8,128)(2,1)S(1)} %multiply_convert_fusion), channel_id=1, source_target_pairs={{0,128},{32,160},{64,192},{96,224},{128,0},{160,32},{192,64},{224,... | collective-permute-start | bytes 110600 | tf_op jit(solution)/shard_map/ppermute | solution.py:272
  106.9 6.4 %collective-permute-start.3 = (bf16[2,72,256]{2,1,0:T(8,128)(2,1)S(1)}, bf16[2,72,256]{2,1,0:T(8,128)(2,1)S(1)}, u32[]{:S(2)}, u32[]{:S(2)}) collective-permute-start(bf16[2,72,256]{2,1,0:T(8,128)(2,1)S(1)} %pad_maximum_fusion.refs_0_), channel_id=1, source_target_pairs={{0,96},{32,64},{64,32},{96,0},{128,224},{160,192},{192,160},{224,1... | collective-permute-start | bytes 221192 | tf_op jit(solution)/shard_map/ppermute | solution.py:272
  107.2 7.5 %collective-permute-start.2 = (bf16[2,72,256]{2,1,0:T(8,128)(2,1)S(1)}, bf16[2,72,256]{2,1,0:T(8,128)(2,1)S(1)}, u32[]{:S(2)}, u32[]{:S(2)}) collective-permute-start(bf16[2,72,256]{2,1,0:T(8,128)(2,1)S(1)} %pad_maximum_fusion.refs_0_), channel_id=1, source_target_pairs={{0,64},{32,96},{64,0},{96,32},{128,192},{160,224},{192,128},{224,1... | collective-permute-start | bytes 221192 | tf_op jit(solution)/shard_map/ppermute | solution.py:272
  109.0 5.7 %collective-permute-start.1 = (bf16[2,72,256]{2,1,0:T(8,128)(2,1)S(1)}, bf16[2,72,256]{2,1,0:T(8,128)(2,1)S(1)}, u32[]{:S(2)}, u32[]{:S(2)}) collective-permute-start(bf16[2,72,256]{2,1,0:T(8,128)(2,1)S(1)} %pad_maximum_fusion.refs_0_), channel_id=1, source_target_pairs={{0,32},{32,0},{64,96},{96,64},{128,160},{160,128},{192,224},{224,1... | collective-permute-start | bytes 221192 | tf_op jit(solution)/shard_map/ppermute | solution.py:272

commit v4 on v3

--- a/solution.py
+++ b/solution.py
@@ -166,7 +166,12 @@
         copy.wait()
 
 
-def correlate_kernel(recv_ref, slots_ref, lag_hbm, out_ref, pick_ref, lag_ref, side_ref, cross_ref, total_ref, sem):
+def share_of(device):
+    return jnp.minimum(device, 2 * HALF_HOURS - 1 - device)
+
+
+def correlate_kernel(recv_ref, slots_ref, lag_hbm, *refs):
+    out_refs, (pick_ref, lag_ref, side_ref, cross_ref, total_ref, sem) = refs[:HALF_HOURS], refs[HALF_HOURS:]
     pairs = slots_ref.shape[1]
     owners, all_rows, _ = recv_ref.shape
     rows = all_rows // cross_ref.shape[0]
@@ -211,12 +216,11 @@
         lagged = jnp.dot(cross_ref[h], lag_ref[...], preferred_element_type=F32)
         rooted = jnp.sqrt(jnp.abs(lagged) + 0.01) - 0.1
         rooted = jnp.where(lagged > 0.0, rooted, jnp.where(lagged < 0.0, -rooted, 0.0))
+        rooted = rooted.reshape(total_ref.shape)
         if h == 0:
             total_ref[...] = rooted
-        elif h < cross_ref.shape[0] - 1:
+        else:
             total_ref[...] += rooted
-        else:
-            out_ref[...] = (total_ref[...] + rooted).astype(BF16).reshape(out_ref.shape)
 
     lag_copy.wait()
     for h in range(cross_ref.shape[0]):
@@ -224,6 +228,9 @@
             select(h, n)
             cross(h, n)
         root(h)
+    me = lax.axis_index("hour")
+    for k, out_ref in enumerate(out_refs):
+        out_ref[...] = total_ref[share_of(me ^ k)].astype(BF16)
 
 
 def whiten(panels, starts, counts, send):
@@ -259,49 +266,57 @@
     )(panels, starts, counts, send, dft_table(), band_table())
 
 
-def gather_kernel(*refs):
-    part_refs, out_ref = refs[:-1], refs[-1]
-    me = lax.axis_index("hour")
-    for k, part_ref in enumerate(part_refs):
-        for far in range(2):
-            out_ref[me ^ (k + HALF_HOURS * far)] = part_ref[far].astype(F32)
-
-
-def gather(mine):
-    def swap(array, distance):
-        return lax.ppermute(array, "hour", [(i, i ^ distance) for i in range(2 * HALF_HOURS)])
-
-    both = jnp.stack([mine, swap(mine, HALF_HOURS)])
-    parts = [both] + [swap(both, k) for k in range(1, HALF_HOURS)]
-    return pl.pallas_call(
-        gather_kernel,
-        out_shape=jax.ShapeDtypeStruct((2 * HALF_HOURS,) + mine.shape, F32),
-        compiler_params=pltpu.CompilerParams(vmem_limit_bytes=SPREAD_VMEM),
-        name="spread_result",
-    )(*parts)
-
-
-def correlate(received, slots, hours, pieces):
+def correlate(received, slots, hours):
     owners, all_rows, width = received.shape
     pairs = slots.shape[1]
     rows = all_rows // hours
     channels = COMPS * COMPS
     vmem = pl.BlockSpec(memory_space=pltpu.VMEM)
+    share = (channels * pairs // HALF_HOURS, LAGS)
     return pl.pallas_call(
         correlate_kernel,
         in_specs=[vmem, vmem, pl.BlockSpec(memory_space=pltpu.HBM)],
-        out_specs=vmem,
-        out_shape=jax.ShapeDtypeStruct((pieces, channels * pairs // pieces, LAGS), BF16),
+        out_specs=[vmem] * HALF_HOURS,
+        out_shape=[jax.ShapeDtypeStruct(share, BF16)] * HALF_HOURS,
         scratch_shapes=[
             pltpu.VMEM((2 * PARTS * pairs, owners * rows), BF16),
             pltpu.VMEM((2 * NFREQ, LAGS), BF16),
             pltpu.VMEM((2, 2 * PARTS * pairs, width // 2), F32),
             pltpu.VMEM((hours, channels * pairs, 2 * NFREQ), BF16),
-            pltpu.VMEM((channels * pairs, LAGS), F32),
+            pltpu.VMEM((HALF_HOURS,) + share, F32),
             pltpu.SemaphoreType.DMA(()),
         ],
         compiler_params=pltpu.CompilerParams(vmem_limit_bytes=CORRELATE_VMEM),
     )(received, slots, lag_table())
+
+
+def spread_kernel(*refs):
+    part_refs, out_ref = refs[:-1], refs[-1]
+    me = lax.axis_index("hour")
+    for k, part_ref in enumerate(part_refs):
+        out_ref[share_of(me ^ k)] = part_ref[...].astype(F32)
+
+
+def swap(array, distance):
+    return lax.ppermute(array, "hour", [(i, i ^ distance) for i in range(2 * HALF_HOURS)])
+
+
+def stack_hours(shares, hours_all):
+    mine = shares[0].astype(F32)
+    for k in range(1, HALF_HOURS):
+        mine = mine + swap(shares[k], k).astype(F32)
+    mine = mine.astype(BF16)
+    other = swap(mine, 2 * HALF_HOURS - 1)
+    average = (mine.astype(F32) + other.astype(F32)) / hours_all
+    size = jnp.abs(average) + 0.1
+    stacked = (jnp.sign(average) * (size * size - 0.01)).astype(BF16)
+    parts = [stacked] + [swap(stacked, k) for k in range(1, HALF_HOURS)]
+    return pl.pallas_call(
+        spread_kernel,
+        out_shape=jax.ShapeDtypeStruct((HALF_HOURS,) + stacked.shape, F32),
+        compiler_params=pltpu.CompilerParams(vmem_limit_bytes=SPREAD_VMEM),
+        name="spread_result",
+    )(*parts)
 
 
 def local(raw_panels, window_start, valid_count, send_rows, pair_slots):
@@ -313,12 +328,9 @@
     counts = jnp.transpose(valid_count, (1, 2, 0))
     outgoing = whiten(panels, starts, counts, jnp.transpose(send_rows[0]))
     received = lax.all_to_all(outgoing, "pair", split_axis=0, concat_axis=0, tiled=True)
-    partial = correlate(received, jnp.transpose(pair_slots), hours, hour_devices)
-    shares = lax.all_to_all(partial, "hour", split_axis=0, concat_axis=0, tiled=True)
-    average = jnp.sum(shares.astype(F32), axis=0) / (hours * hour_devices)
-    size = jnp.abs(average) + 0.1
-    stacked = (jnp.sign(average) * (size * size - 0.01)).astype(BF16)
-    stacked = gather(stacked).reshape(COMPS * COMPS, pairs, LAGS)
+    shares = correlate(received, jnp.transpose(pair_slots), hours)
+    stacked = stack_hours(shares, hours * hour_devices)
+    stacked = stacked.reshape(COMPS * COMPS, pairs, LAGS)
     return jnp.transpose(stacked, (1, 0, 2))
 
 

time: 116 us -> 106 us (0.914)
  blocking collectives: 84.1 us -> 62.7 us
  starting transfers between devices: 5.12 us -> 14.2 us
  waiting for transfers between devices: 10.9 us -> 13.5 us
    all_to_all x1 -> x0, blocking collectives: 21.4 us -> none  [local(): lax.all_to_all(partial, 'hour', split_axis=0, concat_axis=0, tiled=True)]
    ppermute x4 -> x7, starting transfers between devices: 5.12 us -> 14.2 us  [swap(): lax.ppermute(array, 'hour', [(i, i ^ distance) for i in range(2 * HALF_HO...]
    ppermute x4 -> x7, waiting for transfers between devices: 10.9 us -> 13.5 us  [swap(): lax.ppermute(array, 'hour', [(i, i ^ distance) for i in range(2 * HALF_HO...]
  transfers between devices with their start and end apart: 4 -> 7, of which waited for: 3 -> 5; matrix products, arithmetic and copies ran while one was open for 0% -> 0% of each run, Pallas kernels for 0% -> 0%
where the time goes in v4:
time: 106 us
  blocking collectives  62.7 us (59%)
  Pallas kernels  15.4 us (15%)
  starting transfers between devices  14.2 us (13%)
  waiting for transfers between devices  13.5 us (13%)
    all_to_all x1, blocking collectives, local(): lax.all_to_all(outgoing, 'pair', split_axis=0, concat_axis=0, tiled=True)  62.7 us
    ppermute x7, starting transfers between devices, swap(): lax.ppermute(array, 'hour', [(i, i ^ distance) for i in range(2 * HALF_HO...  14.2 us
    ppermute x7, waiting for transfers between devices, swap(): lax.ppermute(array, 'hour', [(i, i ^ distance) for i in range(2 * HALF_HO...  13.5 us
    pallas_call x1, Pallas kernels, whiten(): pl.pallas_call(whiten_kernel, in_specs=[hbm] * 6, out_specs=hbm, out_shap...  8.46 us
    pallas_call x1, Pallas kernels, correlate(): pl.pallas_call(correlate_kernel, in_specs=[vmem, vmem, pl.BlockSpec(memor...  6.05 us
  transfers between devices with their start and end apart: 7, of which 5 were waited for; matrix products, arithmetic and copies ran while one was open for 0% of the time, Pallas kernels for 0%

profile of v4, /device:TPU:8, one launch (start us, length us, event | category | flops | bytes accessed | tf_op | source)
XLA Modules:
  0.0 106.0 jit_solution(14158873162302095461)
XLA Ops:
  0.0 8.5 %shard_map.82 = bf16[32,48,1536]{2,1,0:T(8,128)(2,1)} custom-call(bf16[3,3,16,3712]{3,2,1,0:T(8,128)(2,1)} %bitcast.11, s32[3,2,16]{2,1,0:T(2,128)} %bitcast.12, s32[3,2,16]{2,1,0:T(2,128)} %bitcast.13, s32[4,32]{1,0:T(4,128)} %bitcast.14, bf16[1024,1024]{1,0:T(8,128)(2,1)} %constant.14.clone.dft_hbm, bf16[512,512]{1,0:T(8,128)(2,1)} %constant.15.clone.band_hbm), custom_call_target="tpu_custom_call" | custom-call | tf_op jit(solution)/shard_map/pallas_call | solution.py:243
  8.5 0.0 copy-start
  8.5 0.0 copy-start.1
  8.5 62.7 %all_to_all.5.recv_ref = bf16[32,48,1536]{2,1,0:T(8,128)(2,1)S(1)} all-to-all(bf16[32,48,1536]{2,1,0:T(8,128)(2,1)} %shard_map.82), channel_id=1, replica_groups=mesh['hour'=8,'pair'=32] {'pair'}, dimensions={0} | all-to-all | bytes 9437184 | tf_op jit(solution)/shard_map/all_to_all | solution.py:330
  71.2 0.0 copy-done
  71.2 0.0 copy-done.1
  71.2 6.0 %shard_map.83 = (bf16[144,256]{1,0:T(8,128)(2,1)S(1)}, bf16[144,256]{1,0:T(8,128)(2,1)S(1)}, bf16[144,256]{1,0:T(8,128)(2,1)S(1)}, bf16[144,256]{1,0:T(8,128)(2,1)S(1)}) custom-call(bf16[32,48,1536]{2,1,0:T(8,128)(2,1)S(1)} %all_to_all.5.recv_ref, s32[2,64]{1,0:T(2,128)S(1)} %bitcast.10, bf16[1024,256]{1,0:T(8,128)(2,1)S(1)} %copy-done), custom_call_target="tpu_custom_call" | custom-call | tf_op jit(solution)/shard_map/pallas_call | solution.py:276
  77.3 2.0 %collective-permute-start = (bf16[144,256]{1,0:T(8,128)(2,1)S(1)}, bf16[144,256]{1,0:T(8,128)(2,1)S(1)}, u32[]{:S(2)}, u32[]{:S(2)}) collective-permute-start(bf16[144,256]{1,0:T(8,128)(2,1)S(1)} %get-tuple-element.10), channel_id=1, source_target_pairs={{0,32},{32,0},{64,96},{96,64},{128,160},{160,128},{192,224},{224,1... | collective-permute-start | bytes 221192 | tf_op jit(solution)/shard_map/ppermute | solution.py:301
  79.3 3.3 %collective-permute-start.1 = (bf16[144,256]{1,0:T(8,128)(2,1)S(1)}, bf16[144,256]{1,0:T(8,128)(2,1)S(1)}, u32[]{:S(2)}, u32[]{:S(2)}) collective-permute-start(bf16[144,256]{1,0:T(8,128)(2,1)S(1)} %get-tuple-element.11), channel_id=1, source_target_pairs={{0,64},{32,96},{64,0},{96,32},{128,192},{160,224},{192,128},{224,1... | collective-permute-start | bytes 221192 | tf_op jit(solution)/shard_map/ppermute | solution.py:301
  82.6 0.0 collective-permute-start.2
  82.6 0.0 collective-permute-done
  82.6 5.3 %collective-permute-done.1 = bf16[144,256]{1,0:T(8,128)(2,1)S(1)} collective-permute-done((bf16[144,256]{1,0:T(8,128)(2,1)S(1)}, bf16[144,256]{1,0:T(8,128)(2,1)S(1)}, u32[]{:S(2)}, u32[]{:S(2)}) %collective-permute-start.1) | collective-permute-done | bytes 73760 | tf_op jit(solution)/shard_map/ppermute | solution.py:301
  87.9 0.9 collective-permute-done.2
  88.8 4.5 %collective-permute-start.3 = (bf16[144,256]{1,0:T(8,128)(2,1)S(1)}, bf16[144,256]{1,0:T(8,128)(2,1)S(1)}, u32[]{:S(2)}, u32[]{:S(2)}) collective-permute-start(bf16[144,256]{1,0:T(8,128)(2,1)S(1)} %add_convert_fusion), channel_id=1, source_target_pairs={{0,224},{32,192},{64,160},{96,128},{128,96},{160,64},{192,32},{224... | collective-permute-start | bytes 221192 | tf_op jit(solution)/shard_map/ppermute | solution.py:301
  93.3 3.7 %collective-permute-done.3 = bf16[144,256]{1,0:T(8,128)(2,1)S(1)} collective-permute-done((bf16[144,256]{1,0:T(8,128)(2,1)S(1)}, bf16[144,256]{1,0:T(8,128)(2,1)S(1)}, u32[]{:S(2)}, u32[]{:S(2)}) %collective-permute-start.3) | collective-permute-done | bytes 73760 | tf_op jit(solution)/shard_map/ppermute | solution.py:301
  97.0 0.1 multiply_convert_fusion.refs_0_
  97.0 2.2 %collective-permute-start.6 = (bf16[144,256]{1,0:T(8,128)(2,1)S(1)}, bf16[144,256]{1,0:T(8,128)(2,1)S(1)}, u32[]{:S(2)}, u32[]{:S(2)}) collective-permute-start(bf16[144,256]{1,0:T(8,128)(2,1)S(1)} %multiply_convert_fusion.refs_0_), channel_id=1, source_target_pairs={{0,96},{32,64},{64,32},{96,0},{128,224},{160,192},{192,160},{224,1... | collective-permute-start | bytes 221192 | tf_op jit(solution)/shard_map/ppermute | solution.py:301
  99.2 0.5 collective-permute-start.5
  99.7 1.8 %collective-permute-start.4 = (bf16[144,256]{1,0:T(8,128)(2,1)S(1)}, bf16[144,256]{1,0:T(8,128)(2,1)S(1)}, u32[]{:S(2)}, u32[]{:S(2)}) collective-permute-start(bf16[144,256]{1,0:T(8,128)(2,1)S(1)} %multiply_convert_fusion.refs_0_), channel_id=1, source_target_pairs={{0,32},{32,0},{64,96},{96,64},{128,160},{160,128},{192,224},{224,1... | collective-permute-start | bytes 221192 | tf_op jit(solution)/shard_map/ppermute | solution.py:301
  101.5 1.8 %collective-permute-done.6.refs_3_ = bf16[144,256]{1,0:T(8,128)(2,1)S(1)} collective-permute-done((bf16[144,256]{1,0:T(8,128)(2,1)S(1)}, bf16[144,256]{1,0:T(8,128)(2,1)S(1)}, u32[]{:S(2)}, u32[]{:S(2)}) %collective-permute-start.6) | collective-permute-done | bytes 73760 | tf_op jit(solution)/shard_map/ppermute | solution.py:301
  103.3 1.9 %collective-permute-done.5.refs_2_ = bf16[144,256]{1,0:T(8,128)(2,1)S(1)} collective-permute-done((bf16[144,256]{1,0:T(8,128)(2,1)S(1)}, bf16[144,256]{1,0:T(8,128)(2,1)S(1)}, u32[]{:S(2)}, u32[]{:S(2)}) %collective-permute-start.5) | collective-permute-done | bytes 73760 | tf_op jit(solution)/shard_map/ppermute | solution.py:301
  105.2 0.0 collective-permute-done.4.refs_1_
  105.2 0.9 spread_result.1
  (1 shorter events, 0.0 us)
Async XLA Ops:
  8.5 62.8 %copy-start = (bf16[1024,256]{1,0:T(8,128)(2,1)S(1)}, bf16[1024,256]{1,0:T(8,128)(2,1)}, u32[]{:S(2)}) copy-start(bf16[1024,256]{1,0:T(8,128)(2,1)} %constant.16.clone.lag_hbm) | copy-start | bytes 1572868
  8.5 62.7 %copy-start.1 = (s32[64,2]{0,1:T(2,128)S(1)}, s32[64,2]{0,1:T(2,128)}, u32[]{:S(2)}) copy-start(s32[64,2]{0,1:T(2,128)} %param.12) | copy-start | bytes 1540
  77.3 5.3 %collective-permute-start = (bf16[144,256]{1,0:T(8,128)(2,1)S(1)}, bf16[144,256]{1,0:T(8,128)(2,1)S(1)}, u32[]{:S(2)}, u32[]{:S(2)}) collective-permute-start(bf16[144,256]{1,0:T(8,128)(2,1)S(1)} %get-tuple-element.10), channel_id=1, source_target_pairs={{0,32},{32,0},{64,96},{96,64},{128,160},{160,128},{192,224},{224,1... | collective-permute-start | bytes 221192 | tf_op jit(solution)/shard_map/ppermute | solution.py:301
  79.3 8.6 %collective-permute-start.1 = (bf16[144,256]{1,0:T(8,128)(2,1)S(1)}, bf16[144,256]{1,0:T(8,128)(2,1)S(1)}, u32[]{:S(2)}, u32[]{:S(2)}) collective-permute-start(bf16[144,256]{1,0:T(8,128)(2,1)S(1)} %get-tuple-element.11), channel_id=1, source_target_pairs={{0,64},{32,96},{64,0},{96,32},{128,192},{160,224},{192,128},{224,1... | collective-permute-start | bytes 221192 | tf_op jit(solution)/shard_map/ppermute | solution.py:301
  82.6 6.2 %collective-permute-start.2 = (bf16[144,256]{1,0:T(8,128)(2,1)S(1)}, bf16[144,256]{1,0:T(8,128)(2,1)S(1)}, u32[]{:S(2)}, u32[]{:S(2)}) collective-permute-start(bf16[144,256]{1,0:T(8,128)(2,1)S(1)} %get-tuple-element.12), channel_id=1, source_target_pairs={{0,96},{32,64},{64,32},{96,0},{128,224},{160,192},{192,160},{224,1... | collective-permute-start | bytes 221192 | tf_op jit(solution)/shard_map/ppermute | solution.py:301
  88.8 8.1 %collective-permute-start.3 = (bf16[144,256]{1,0:T(8,128)(2,1)S(1)}, bf16[144,256]{1,0:T(8,128)(2,1)S(1)}, u32[]{:S(2)}, u32[]{:S(2)}) collective-permute-start(bf16[144,256]{1,0:T(8,128)(2,1)S(1)} %add_convert_fusion), channel_id=1, source_target_pairs={{0,224},{32,192},{64,160},{96,128},{128,96},{160,64},{192,32},{224... | collective-permute-start | bytes 221192 | tf_op jit(solution)/shard_map/ppermute | solution.py:301
  97.0 6.2 %collective-permute-start.6 = (bf16[144,256]{1,0:T(8,128)(2,1)S(1)}, bf16[144,256]{1,0:T(8,128)(2,1)S(1)}, u32[]{:S(2)}, u32[]{:S(2)}) collective-permute-start(bf16[144,256]{1,0:T(8,128)(2,1)S(1)} %multiply_convert_fusion.refs_0_), channel_id=1, source_target_pairs={{0,96},{32,64},{64,32},{96,0},{128,224},{160,192},{192,160},{224,1... | collective-permute-start | bytes 221192 | tf_op jit(solution)/shard_map/ppermute | solution.py:301
  99.2 6.0 %collective-permute-start.5 = (bf16[144,256]{1,0:T(8,128)(2,1)S(1)}, bf16[144,256]{1,0:T(8,128)(2,1)S(1)}, u32[]{:S(2)}, u32[]{:S(2)}) collective-permute-start(bf16[144,256]{1,0:T(8,128)(2,1)S(1)} %multiply_convert_fusion.refs_0_), channel_id=1, source_target_pairs={{0,64},{32,96},{64,0},{96,32},{128,192},{160,224},{192,128},{224,1... | collective-permute-start | bytes 221192 | tf_op jit(solution)/shard_map/ppermute | solution.py:301
  99.7 5.4 %collective-permute-start.4 = (bf16[144,256]{1,0:T(8,128)(2,1)S(1)}, bf16[144,256]{1,0:T(8,128)(2,1)S(1)}, u32[]{:S(2)}, u32[]{:S(2)}) collective-permute-start(bf16[144,256]{1,0:T(8,128)(2,1)S(1)} %multiply_convert_fusion.refs_0_), channel_id=1, source_target_pairs={{0,32},{32,0},{64,96},{96,64},{128,160},{160,128},{192,224},{224,1... | collective-permute-start | bytes 221192 | tf_op jit(solution)/shard_map/ppermute | solution.py:301

commit v5 on v4

--- a/solution.py
+++ b/solution.py
@@ -58,7 +58,7 @@
 
 
 def cut(panel, start):
-    raw = panel.shape[1]
+    stations, raw = panel.shape
     reach = raw - 2048
     bit = (start & 2048) != 0
     moved = jnp.where(bit, panel[:, 2048:], panel[:, :reach])
@@ -67,11 +67,14 @@
         bit = (start & size) != 0
         keep = NFFT + size
         samples = jnp.where(bit, samples[:, size : size + keep], samples[:, :keep])
-    width = samples.shape[1]
-    for size in (64, 32, 16, 8, 4, 2, 1):
-        bit = (start & size) != 0
-        samples = jnp.where(bit, pltpu.roll(samples, width - size, 1), samples)
-    return samples[:, :NFFT]
+    place = lax.broadcasted_iota(jnp.int32, (stations, 128), 1) + (start & 127)
+    inside = place & 127
+    turned = [
+        jnp.take_along_axis(samples[:, t : t + 128], inside, axis=1, mode="promise_in_bounds")
+        for t in range(0, NFFT + 128, 128)
+    ]
+    beyond = place >= 128
+    return jnp.concatenate([jnp.where(beyond, turned[t + 1], turned[t]) for t in range(NFFT // 128)], axis=1)
 
 
 def whiten_kernel(
@@ -223,11 +226,14 @@
             total_ref[...] += rooted
 
     lag_copy.wait()
-    for h in range(cross_ref.shape[0]):
-        for n in range(2):
-            select(h, n)
-            cross(h, n)
-        root(h)
+    steps = [(h, n) for h in range(cross_ref.shape[0]) for n in range(2)]
+    select(*steps[0])
+    for now, later in zip(steps, steps[1:] + [None]):
+        if later is not None:
+            select(*later)
+        cross(*now)
+        if now[1] == 1:
+            root(now[0])
     me = lax.axis_index("hour")
     for k, out_ref in enumerate(out_refs):
         out_ref[...] = total_ref[share_of(me ^ k)].astype(BF16)

time: 106 us -> 105 us (level)
  Pallas kernels: 15.4 us -> 14.1 us
where the time goes in v5:
time: 105 us
  blocking collectives  62.7 us (60%)
  starting transfers between devices  14.2 us (14%)
  Pallas kernels  14.1 us (13%)
  waiting for transfers between devices  13.5 us (13%)
    all_to_all x1, blocking collectives, local(): lax.all_to_all(outgoing, 'pair', split_axis=0, concat_axis=0, tiled=True)  62.7 us
    ppermute x7, starting transfers between devices, swap(): lax.ppermute(array, 'hour', [(i, i ^ distance) for i in range(2 * HALF_HO...  14.2 us
    ppermute x7, waiting for transfers between devices, swap(): lax.ppermute(array, 'hour', [(i, i ^ distance) for i in range(2 * HALF_HO...  13.5 us
    pallas_call x1, Pallas kernels, whiten(): pl.pallas_call(whiten_kernel, in_specs=[hbm] * 6, out_specs=hbm, out_shap...  7.42 us
    pallas_call x1, Pallas kernels, correlate(): pl.pallas_call(correlate_kernel, in_specs=[vmem, vmem, pl.BlockSpec(memor...  5.8 us
  transfers between devices with their start and end apart: 7, of which 5 were waited for; matrix products, arithmetic and copies ran while one was open for 0% of the time, Pallas kernels for 0%

profile of v5, /device:TPU:8, one launch (start us, length us, event | category | flops | bytes accessed | tf_op | source)
XLA Modules:
  0.0 104.8 jit_solution(7828971978892113827)
XLA Ops:
  0.0 7.4 %shard_map.82 = bf16[32,48,1536]{2,1,0:T(8,128)(2,1)} custom-call(bf16[3,3,16,3712]{3,2,1,0:T(8,128)(2,1)} %bitcast.11, s32[3,2,16]{2,1,0:T(2,128)} %bitcast.12, s32[3,2,16]{2,1,0:T(2,128)} %bitcast.13, s32[4,32]{1,0:T(4,128)} %bitcast.14, bf16[1024,1024]{1,0:T(8,128)(2,1)} %constant.14.clone.dft_hbm, bf16[512,512]{1,0:T(8,128)(2,1)} %constant.15.clone.band_hbm), custom_call_target="tpu_custom_call" | custom-call | tf_op jit(solution)/shard_map/pallas_call | solution.py:249
  7.4 0.0 copy-start
  7.4 0.0 copy-start.1
  7.5 62.7 %all_to_all.5.recv_ref = bf16[32,48,1536]{2,1,0:T(8,128)(2,1)S(1)} all-to-all(bf16[32,48,1536]{2,1,0:T(8,128)(2,1)} %shard_map.82), channel_id=1, replica_groups=mesh['hour'=8,'pair'=32] {'pair'}, dimensions={0} | all-to-all | bytes 9437184 | tf_op jit(solution)/shard_map/all_to_all | solution.py:336
  70.2 0.0 copy-done
  70.2 0.0 copy-done.1
  70.2 5.8 %shard_map.83 = (bf16[144,256]{1,0:T(8,128)(2,1)S(1)}, bf16[144,256]{1,0:T(8,128)(2,1)S(1)}, bf16[144,256]{1,0:T(8,128)(2,1)S(1)}, bf16[144,256]{1,0:T(8,128)(2,1)S(1)}) custom-call(bf16[32,48,1536]{2,1,0:T(8,128)(2,1)S(1)} %all_to_all.5.recv_ref, s32[2,64]{1,0:T(2,128)S(1)} %bitcast.10, bf16[1024,256]{1,0:T(8,128)(2,1)S(1)} %copy-done), custom_call_target="tpu_custom_call" | custom-call | tf_op jit(solution)/shard_map/pallas_call | solution.py:282
  76.0 2.0 %collective-permute-start = (bf16[144,256]{1,0:T(8,128)(2,1)S(1)}, bf16[144,256]{1,0:T(8,128)(2,1)S(1)}, u32[]{:S(2)}, u32[]{:S(2)}) collective-permute-start(bf16[144,256]{1,0:T(8,128)(2,1)S(1)} %get-tuple-element.10), channel_id=1, source_target_pairs={{0,32},{32,0},{64,96},{96,64},{128,160},{160,128},{192,224},{224,1... | collective-permute-start | bytes 221192 | tf_op jit(solution)/shard_map/ppermute | solution.py:307
  78.0 3.3 %collective-permute-start.1 = (bf16[144,256]{1,0:T(8,128)(2,1)S(1)}, bf16[144,256]{1,0:T(8,128)(2,1)S(1)}, u32[]{:S(2)}, u32[]{:S(2)}) collective-permute-start(bf16[144,256]{1,0:T(8,128)(2,1)S(1)} %get-tuple-element.11), channel_id=1, source_target_pairs={{0,64},{32,96},{64,0},{96,32},{128,192},{160,224},{192,128},{224,1... | collective-permute-start | bytes 221192 | tf_op jit(solution)/shard_map/ppermute | solution.py:307
  81.3 0.0 collective-permute-start.2
  81.3 0.0 collective-permute-done
  81.3 5.3 %collective-permute-done.1 = bf16[144,256]{1,0:T(8,128)(2,1)S(1)} collective-permute-done((bf16[144,256]{1,0:T(8,128)(2,1)S(1)}, bf16[144,256]{1,0:T(8,128)(2,1)S(1)}, u32[]{:S(2)}, u32[]{:S(2)}) %collective-permute-start.1) | collective-permute-done | bytes 73760 | tf_op jit(solution)/shard_map/ppermute | solution.py:307
  86.6 0.9 collective-permute-done.2
  87.5 4.5 %collective-permute-start.3 = (bf16[144,256]{1,0:T(8,128)(2,1)S(1)}, bf16[144,256]{1,0:T(8,128)(2,1)S(1)}, u32[]{:S(2)}, u32[]{:S(2)}) collective-permute-start(bf16[144,256]{1,0:T(8,128)(2,1)S(1)} %add_convert_fusion), channel_id=1, source_target_pairs={{0,224},{32,192},{64,160},{96,128},{128,96},{160,64},{192,32},{224... | collective-permute-start | bytes 221192 | tf_op jit(solution)/shard_map/ppermute | solution.py:307
  92.0 3.6 %collective-permute-done.3 = bf16[144,256]{1,0:T(8,128)(2,1)S(1)} collective-permute-done((bf16[144,256]{1,0:T(8,128)(2,1)S(1)}, bf16[144,256]{1,0:T(8,128)(2,1)S(1)}, u32[]{:S(2)}, u32[]{:S(2)}) %collective-permute-start.3) | collective-permute-done | bytes 73760 | tf_op jit(solution)/shard_map/ppermute | solution.py:307
  95.7 0.1 multiply_convert_fusion.refs_0_
  95.8 2.2 %collective-permute-start.6 = (bf16[144,256]{1,0:T(8,128)(2,1)S(1)}, bf16[144,256]{1,0:T(8,128)(2,1)S(1)}, u32[]{:S(2)}, u32[]{:S(2)}) collective-permute-start(bf16[144,256]{1,0:T(8,128)(2,1)S(1)} %multiply_convert_fusion.refs_0_), channel_id=1, source_target_pairs={{0,96},{32,64},{64,32},{96,0},{128,224},{160,192},{192,160},{224,1... | collective-permute-start | bytes 221192 | tf_op jit(solution)/shard_map/ppermute | solution.py:307
  97.9 0.5 collective-permute-start.5
  98.5 1.8 %collective-permute-start.4 = (bf16[144,256]{1,0:T(8,128)(2,1)S(1)}, bf16[144,256]{1,0:T(8,128)(2,1)S(1)}, u32[]{:S(2)}, u32[]{:S(2)}) collective-permute-start(bf16[144,256]{1,0:T(8,128)(2,1)S(1)} %multiply_convert_fusion.refs_0_), channel_id=1, source_target_pairs={{0,32},{32,0},{64,96},{96,64},{128,160},{160,128},{192,224},{224,1... | collective-permute-start | bytes 221192 | tf_op jit(solution)/shard_map/ppermute | solution.py:307
  100.2 1.8 %collective-permute-done.6.refs_3_ = bf16[144,256]{1,0:T(8,128)(2,1)S(1)} collective-permute-done((bf16[144,256]{1,0:T(8,128)(2,1)S(1)}, bf16[144,256]{1,0:T(8,128)(2,1)S(1)}, u32[]{:S(2)}, u32[]{:S(2)}) %collective-permute-start.6) | collective-permute-done | bytes 73760 | tf_op jit(solution)/shard_map/ppermute | solution.py:307
  102.0 1.9 %collective-permute-done.5.refs_2_ = bf16[144,256]{1,0:T(8,128)(2,1)S(1)} collective-permute-done((bf16[144,256]{1,0:T(8,128)(2,1)S(1)}, bf16[144,256]{1,0:T(8,128)(2,1)S(1)}, u32[]{:S(2)}, u32[]{:S(2)}) %collective-permute-start.5) | collective-permute-done | bytes 73760 | tf_op jit(solution)/shard_map/ppermute | solution.py:307
  103.9 0.0 collective-permute-done.4.refs_1_
  103.9 0.9 spread_result.1
  (1 shorter events, 0.0 us)
Async XLA Ops:
  7.4 62.7 %copy-start = (bf16[1024,256]{1,0:T(8,128)(2,1)S(1)}, bf16[1024,256]{1,0:T(8,128)(2,1)}, u32[]{:S(2)}) copy-start(bf16[1024,256]{1,0:T(8,128)(2,1)} %constant.16.clone.lag_hbm) | copy-start | bytes 1572868
  7.4 62.7 %copy-start.1 = (s32[64,2]{0,1:T(2,128)S(1)}, s32[64,2]{0,1:T(2,128)}, u32[]{:S(2)}) copy-start(s32[64,2]{0,1:T(2,128)} %param.12) | copy-start | bytes 1540
  76.0 5.3 %collective-permute-start = (bf16[144,256]{1,0:T(8,128)(2,1)S(1)}, bf16[144,256]{1,0:T(8,128)(2,1)S(1)}, u32[]{:S(2)}, u32[]{:S(2)}) collective-permute-start(bf16[144,256]{1,0:T(8,128)(2,1)S(1)} %get-tuple-element.10), channel_id=1, source_target_pairs={{0,32},{32,0},{64,96},{96,64},{128,160},{160,128},{192,224},{224,1... | collective-permute-start | bytes 221192 | tf_op jit(solution)/shard_map/ppermute | solution.py:307
  78.0 8.6 %collective-permute-start.1 = (bf16[144,256]{1,0:T(8,128)(2,1)S(1)}, bf16[144,256]{1,0:T(8,128)(2,1)S(1)}, u32[]{:S(2)}, u32[]{:S(2)}) collective-permute-start(bf16[144,256]{1,0:T(8,128)(2,1)S(1)} %get-tuple-element.11), channel_id=1, source_target_pairs={{0,64},{32,96},{64,0},{96,32},{128,192},{160,224},{192,128},{224,1... | collective-permute-start | bytes 221192 | tf_op jit(solution)/shard_map/ppermute | solution.py:307
  81.3 6.2 %collective-permute-start.2 = (bf16[144,256]{1,0:T(8,128)(2,1)S(1)}, bf16[144,256]{1,0:T(8,128)(2,1)S(1)}, u32[]{:S(2)}, u32[]{:S(2)}) collective-permute-start(bf16[144,256]{1,0:T(8,128)(2,1)S(1)} %get-tuple-element.12), channel_id=1, source_target_pairs={{0,96},{32,64},{64,32},{96,0},{128,224},{160,192},{192,160},{224,1... | collective-permute-start | bytes 221192 | tf_op jit(solution)/shard_map/ppermute | solution.py:307
  87.5 8.1 %collective-permute-start.3 = (bf16[144,256]{1,0:T(8,128)(2,1)S(1)}, bf16[144,256]{1,0:T(8,128)(2,1)S(1)}, u32[]{:S(2)}, u32[]{:S(2)}) collective-permute-start(bf16[144,256]{1,0:T(8,128)(2,1)S(1)} %add_convert_fusion), channel_id=1, source_target_pairs={{0,224},{32,192},{64,160},{96,128},{128,96},{160,64},{192,32},{224... | collective-permute-start | bytes 221192 | tf_op jit(solution)/shard_map/ppermute | solution.py:307
  95.8 6.2 %collective-permute-start.6 = (bf16[144,256]{1,0:T(8,128)(2,1)S(1)}, bf16[144,256]{1,0:T(8,128)(2,1)S(1)}, u32[]{:S(2)}, u32[]{:S(2)}) collective-permute-start(bf16[144,256]{1,0:T(8,128)(2,1)S(1)} %multiply_convert_fusion.refs_0_), channel_id=1, source_target_pairs={{0,96},{32,64},{64,32},{96,0},{128,224},{160,192},{192,160},{224,1... | collective-permute-start | bytes 221192 | tf_op jit(solution)/shard_map/ppermute | solution.py:307
  97.9 6.0 %collective-permute-start.5 = (bf16[144,256]{1,0:T(8,128)(2,1)S(1)}, bf16[144,256]{1,0:T(8,128)(2,1)S(1)}, u32[]{:S(2)}, u32[]{:S(2)}) collective-permute-start(bf16[144,256]{1,0:T(8,128)(2,1)S(1)} %multiply_convert_fusion.refs_0_), channel_id=1, source_target_pairs={{0,64},{32,96},{64,0},{96,32},{128,192},{160,224},{192,128},{224,1... | collective-permute-start | bytes 221192 | tf_op jit(solution)/shard_map/ppermute | solution.py:307
  98.5 5.5 %collective-permute-start.4 = (bf16[144,256]{1,0:T(8,128)(2,1)S(1)}, bf16[144,256]{1,0:T(8,128)(2,1)S(1)}, u32[]{:S(2)}, u32[]{:S(2)}) collective-permute-start(bf16[144,256]{1,0:T(8,128)(2,1)S(1)} %multiply_convert_fusion.refs_0_), channel_id=1, source_target_pairs={{0,32},{32,0},{64,96},{96,64},{128,160},{160,128},{192,224},{224,1... | collective-permute-start | bytes 221192 | tf_op jit(solution)/shard_map/ppermute | solution.py:307

commit v6 on v5

--- a/solution.py
+++ b/solution.py
@@ -19,6 +19,7 @@
 SMOOTH_HALF = 11
 EPS_WHITE = 1e-06
 HALF_HOURS = 4
+PARTNER = 6
 WHITEN_VMEM = 58 * 2**20
 CORRELATE_VMEM = 24 * 2**20
 SPREAD_VMEM = 8 * 2**20
@@ -115,7 +116,9 @@
     pick_ref[...] = (out_row % PARTS * stations + wanted == white_row).astype(BF16)
 
     time = lax.broadcasted_iota(jnp.int32, (stations, NFFT), 1)
-    for h in range(hours):
+    out_copies = []
+
+    def cut_hour(h):
         raw_copies[h].wait()
         for w in range(WINDOWS):
             start = column(start_ref[h, w : w + 1, :], stations)
@@ -128,11 +131,10 @@
                 mean = jnp.sum(piece, axis=1, keepdims=True) / share
                 row = h * block + (w * COMPS + c) * stations
                 seg_ref[row : row + stations, :] = jnp.where(live, piece - mean, 0.0).astype(BF16)
-    dft_copy.wait()
-    band_copy.wait()
-    out_copies = []
-    spec_ref[...] = jnp.dot(seg_ref[...], dft_ref[...], preferred_element_type=F32)
-    for h in range(hours):
+
+    def send_hour(h):
+        here = slice(h * block, (h + 1) * block)
+        spec_ref[here, :] = jnp.dot(seg_ref[here, :], dft_ref[...], preferred_element_type=F32)
         amps = []
         for w in range(WINDOWS):
             total = jnp.zeros((stations, NFREQ), F32)
@@ -165,12 +167,20 @@
         copy = pltpu.make_async_copy(out_ref.at[h], out_hbm.at[:, pl.ds(h * rows, rows), :], out_sem.at[h])
         copy.start()
         out_copies.append(copy)
+
+    cut_hour(0)
+    dft_copy.wait()
+    band_copy.wait()
+    for h in range(hours):
+        if h + 1 < hours:
+            cut_hour(h + 1)
+        send_hour(h)
     for copy in out_copies:
         copy.wait()
 
 
 def share_of(device):
-    return jnp.minimum(device, 2 * HALF_HOURS - 1 - device)
+    return jnp.where(device < HALF_HOURS, device, device ^ PARTNER)
 
 
 def correlate_kernel(recv_ref, slots_ref, lag_hbm, *refs):
@@ -217,8 +227,9 @@
 
     def root(h):
         lagged = jnp.dot(cross_ref[h], lag_ref[...], preferred_element_type=F32)
-        rooted = jnp.sqrt(jnp.abs(lagged) + 0.01) - 0.1
-        rooted = jnp.where(lagged > 0.0, rooted, jnp.where(lagged < 0.0, -rooted, 0.0))
+        size = jnp.abs(lagged) + 0.01
+        rooted = size * lax.rsqrt(size) - 0.1
+        rooted = jnp.where(lagged < 0.0, -rooted, rooted)
         rooted = rooted.reshape(total_ref.shape)
         if h == 0:
             total_ref[...] = rooted
@@ -312,7 +323,7 @@
     for k in range(1, HALF_HOURS):
         mine = mine + swap(shares[k], k).astype(F32)
     mine = mine.astype(BF16)
-    other = swap(mine, 2 * HALF_HOURS - 1)
+    other = swap(mine, PARTNER)
     average = (mine.astype(F32) + other.astype(F32)) / hours_all
     size = jnp.abs(average) + 0.1
     stacked = (jnp.sign(average) * (size * size - 0.01)).astype(BF16)

time: 105 us -> 105 us (level)
  no operation moved by 1% of the time
where the time goes in v6:
time: 105 us; the launch traced here: 104 us
  blocking collectives  62.7 us (60%)
  starting transfers between devices  15.2 us (14%)
  Pallas kernels  13.5 us (13%)
  waiting for transfers between devices  12.7 us (12%)
    all_to_all x1, blocking collectives, local(): lax.all_to_all(outgoing, 'pair', split_axis=0, concat_axis=0, tiled=True)  62.7 us
    ppermute x7, starting transfers between devices, swap(): lax.ppermute(array, 'hour', [(i, i ^ distance) for i in range(2 * HALF_HO...  15.2 us
    ppermute x7, waiting for transfers between devices, swap(): lax.ppermute(array, 'hour', [(i, i ^ distance) for i in range(2 * HALF_HO...  12.7 us
    pallas_call x1, Pallas kernels, whiten(): pl.pallas_call(whiten_kernel, in_specs=[hbm] * 6, out_specs=hbm, out_shap...  7.23 us
    pallas_call x1, Pallas kernels, correlate(): pl.pallas_call(correlate_kernel, in_specs=[vmem, vmem, pl.BlockSpec(memor...  5.43 us
  transfers between devices with their start and end apart: 7, of which 5 were waited for; matrix products, arithmetic and copies ran while one was open for 0% of the time, Pallas kernels for 0%

profile of v6, /device:TPU:8, one launch (start us, length us, event | category | flops | bytes accessed | tf_op | source)
XLA Modules:
  0.0 104.4 jit_solution(13568835738124797171)
XLA Ops:
  0.0 7.2 %shard_map.82 = bf16[32,48,1536]{2,1,0:T(8,128)(2,1)} custom-call(bf16[3,3,16,3712]{3,2,1,0:T(8,128)(2,1)} %bitcast.11, s32[3,2,16]{2,1,0:T(2,128)} %bitcast.12, s32[3,2,16]{2,1,0:T(2,128)} %bitcast.13, s32[4,32]{1,0:T(4,128)} %bitcast.14, bf16[1024,1024]{1,0:T(8,128)(2,1)} %constant.14.clone.dft_hbm, bf16[512,512]{1,0:T(8,128)(2,1)} %constant.15.clone.band_hbm), custom_call_target="tpu_custom_call" | custom-call | tf_op jit(solution)/shard_map/pallas_call | solution.py:260
  7.2 0.0 copy-start
  7.2 0.0 copy-start.1
  7.3 62.7 %all_to_all.5.recv_ref = bf16[32,48,1536]{2,1,0:T(8,128)(2,1)S(1)} all-to-all(bf16[32,48,1536]{2,1,0:T(8,128)(2,1)} %shard_map.82), channel_id=1, replica_groups=mesh['hour'=8,'pair'=32] {'pair'}, dimensions={0} | all-to-all | bytes 9437184 | tf_op jit(solution)/shard_map/all_to_all | solution.py:347
  70.0 0.0 copy-done
  70.0 0.0 copy-done.1
  70.0 5.4 %shard_map.83 = (bf16[144,256]{1,0:T(8,128)(2,1)S(1)}, bf16[144,256]{1,0:T(8,128)(2,1)S(1)}, bf16[144,256]{1,0:T(8,128)(2,1)S(1)}, bf16[144,256]{1,0:T(8,128)(2,1)S(1)}) custom-call(bf16[32,48,1536]{2,1,0:T(8,128)(2,1)S(1)} %all_to_all.5.recv_ref, s32[2,64]{1,0:T(2,128)S(1)} %bitcast.10, bf16[1024,256]{1,0:T(8,128)(2,1)S(1)} %copy-done), custom_call_target="tpu_custom_call" | custom-call | tf_op jit(solution)/shard_map/pallas_call | solution.py:293
  75.4 2.0 %collective-permute-start = (bf16[144,256]{1,0:T(8,128)(2,1)S(1)}, bf16[144,256]{1,0:T(8,128)(2,1)S(1)}, u32[]{:S(2)}, u32[]{:S(2)}) collective-permute-start(bf16[144,256]{1,0:T(8,128)(2,1)S(1)} %get-tuple-element.10), channel_id=1, source_target_pairs={{0,32},{32,0},{64,96},{96,64},{128,160},{160,128},{192,224},{224,1... | collective-permute-start | bytes 221192 | tf_op jit(solution)/shard_map/ppermute | solution.py:318
  77.4 3.3 %collective-permute-start.1 = (bf16[144,256]{1,0:T(8,128)(2,1)S(1)}, bf16[144,256]{1,0:T(8,128)(2,1)S(1)}, u32[]{:S(2)}, u32[]{:S(2)}) collective-permute-start(bf16[144,256]{1,0:T(8,128)(2,1)S(1)} %get-tuple-element.11), channel_id=1, source_target_pairs={{0,64},{32,96},{64,0},{96,32},{128,192},{160,224},{192,128},{224,1... | collective-permute-start | bytes 221192 | tf_op jit(solution)/shard_map/ppermute | solution.py:318
  80.7 0.0 collective-permute-start.2
  80.7 0.0 collective-permute-done
  80.7 5.3 %collective-permute-done.1 = bf16[144,256]{1,0:T(8,128)(2,1)S(1)} collective-permute-done((bf16[144,256]{1,0:T(8,128)(2,1)S(1)}, bf16[144,256]{1,0:T(8,128)(2,1)S(1)}, u32[]{:S(2)}, u32[]{:S(2)}) %collective-permute-start.1) | collective-permute-done | bytes 73760 | tf_op jit(solution)/shard_map/ppermute | solution.py:318
  86.1 0.9 collective-permute-done.2
  87.0 5.4 %collective-permute-start.3 = (bf16[144,256]{1,0:T(8,128)(2,1)S(1)}, bf16[144,256]{1,0:T(8,128)(2,1)S(1)}, u32[]{:S(2)}, u32[]{:S(2)}) collective-permute-start(bf16[144,256]{1,0:T(8,128)(2,1)S(1)} %add_convert_fusion), channel_id=1, source_target_pairs={{0,192},{32,224},{64,128},{96,160},{128,64},{160,96},{192,0},{224,... | collective-permute-start | bytes 221192 | tf_op jit(solution)/shard_map/ppermute | solution.py:318
  92.4 2.6 %collective-permute-done.3 = bf16[144,256]{1,0:T(8,128)(2,1)S(1)} collective-permute-done((bf16[144,256]{1,0:T(8,128)(2,1)S(1)}, bf16[144,256]{1,0:T(8,128)(2,1)S(1)}, u32[]{:S(2)}, u32[]{:S(2)}) %collective-permute-start.3) | collective-permute-done | bytes 73760 | tf_op jit(solution)/shard_map/ppermute | solution.py:318
  95.0 0.1 multiply_convert_fusion.refs_0_
  95.1 2.0 %collective-permute-start.6 = (bf16[144,256]{1,0:T(8,128)(2,1)S(1)}, bf16[144,256]{1,0:T(8,128)(2,1)S(1)}, u32[]{:S(2)}, u32[]{:S(2)}) collective-permute-start(bf16[144,256]{1,0:T(8,128)(2,1)S(1)} %multiply_convert_fusion.refs_0_), channel_id=1, source_target_pairs={{0,96},{32,64},{64,32},{96,0},{128,224},{160,192},{192,160},{224,1... | collective-permute-start | bytes 221192 | tf_op jit(solution)/shard_map/ppermute | solution.py:318
  97.1 1.1 %collective-permute-start.5 = (bf16[144,256]{1,0:T(8,128)(2,1)S(1)}, bf16[144,256]{1,0:T(8,128)(2,1)S(1)}, u32[]{:S(2)}, u32[]{:S(2)}) collective-permute-start(bf16[144,256]{1,0:T(8,128)(2,1)S(1)} %multiply_convert_fusion.refs_0_), channel_id=1, source_target_pairs={{0,64},{32,96},{64,0},{96,32},{128,192},{160,224},{192,128},{224,1... | collective-permute-start | bytes 221192 | tf_op jit(solution)/shard_map/ppermute | solution.py:318
  98.2 1.4 %collective-permute-start.4 = (bf16[144,256]{1,0:T(8,128)(2,1)S(1)}, bf16[144,256]{1,0:T(8,128)(2,1)S(1)}, u32[]{:S(2)}, u32[]{:S(2)}) collective-permute-start(bf16[144,256]{1,0:T(8,128)(2,1)S(1)} %multiply_convert_fusion.refs_0_), channel_id=1, source_target_pairs={{0,32},{32,0},{64,96},{96,64},{128,160},{160,128},{192,224},{224,1... | collective-permute-start | bytes 221192 | tf_op jit(solution)/shard_map/ppermute | solution.py:318
  99.6 1.9 %collective-permute-done.6.refs_3_ = bf16[144,256]{1,0:T(8,128)(2,1)S(1)} collective-permute-done((bf16[144,256]{1,0:T(8,128)(2,1)S(1)}, bf16[144,256]{1,0:T(8,128)(2,1)S(1)}, u32[]{:S(2)}, u32[]{:S(2)}) %collective-permute-start.6) | collective-permute-done | bytes 73760 | tf_op jit(solution)/shard_map/ppermute | solution.py:318
  101.5 2.0 %collective-permute-done.5.refs_2_ = bf16[144,256]{1,0:T(8,128)(2,1)S(1)} collective-permute-done((bf16[144,256]{1,0:T(8,128)(2,1)S(1)}, bf16[144,256]{1,0:T(8,128)(2,1)S(1)}, u32[]{:S(2)}, u32[]{:S(2)}) %collective-permute-start.5) | collective-permute-done | bytes 73760 | tf_op jit(solution)/shard_map/ppermute | solution.py:318
  103.5 0.0 collective-permute-done.4.refs_1_
  103.5 0.9 spread_result.1
  (1 shorter events, 0.0 us)
Async XLA Ops:
  7.2 62.8 %copy-start = (bf16[1024,256]{1,0:T(8,128)(2,1)S(1)}, bf16[1024,256]{1,0:T(8,128)(2,1)}, u32[]{:S(2)}) copy-start(bf16[1024,256]{1,0:T(8,128)(2,1)} %constant.16.clone.lag_hbm) | copy-start | bytes 1572868
  7.2 62.7 %copy-start.1 = (s32[64,2]{0,1:T(2,128)S(1)}, s32[64,2]{0,1:T(2,128)}, u32[]{:S(2)}) copy-start(s32[64,2]{0,1:T(2,128)} %param.12) | copy-start | bytes 1540
  75.4 5.3 %collective-permute-start = (bf16[144,256]{1,0:T(8,128)(2,1)S(1)}, bf16[144,256]{1,0:T(8,128)(2,1)S(1)}, u32[]{:S(2)}, u32[]{:S(2)}) collective-permute-start(bf16[144,256]{1,0:T(8,128)(2,1)S(1)} %get-tuple-element.10), channel_id=1, source_target_pairs={{0,32},{32,0},{64,96},{96,64},{128,160},{160,128},{192,224},{224,1... | collective-permute-start | bytes 221192 | tf_op jit(solution)/shard_map/ppermute | solution.py:318
  77.4 8.6 %collective-permute-start.1 = (bf16[144,256]{1,0:T(8,128)(2,1)S(1)}, bf16[144,256]{1,0:T(8,128)(2,1)S(1)}, u32[]{:S(2)}, u32[]{:S(2)}) collective-permute-start(bf16[144,256]{1,0:T(8,128)(2,1)S(1)} %get-tuple-element.11), channel_id=1, source_target_pairs={{0,64},{32,96},{64,0},{96,32},{128,192},{160,224},{192,128},{224,1... | collective-permute-start | bytes 221192 | tf_op jit(solution)/shard_map/ppermute | solution.py:318
  80.7 6.2 %collective-permute-start.2 = (bf16[144,256]{1,0:T(8,128)(2,1)S(1)}, bf16[144,256]{1,0:T(8,128)(2,1)S(1)}, u32[]{:S(2)}, u32[]{:S(2)}) collective-permute-start(bf16[144,256]{1,0:T(8,128)(2,1)S(1)} %get-tuple-element.12), channel_id=1, source_target_pairs={{0,96},{32,64},{64,32},{96,0},{128,224},{160,192},{192,160},{224,1... | collective-permute-start | bytes 221192 | tf_op jit(solution)/shard_map/ppermute | solution.py:318
  87.0 8.1 %collective-permute-start.3 = (bf16[144,256]{1,0:T(8,128)(2,1)S(1)}, bf16[144,256]{1,0:T(8,128)(2,1)S(1)}, u32[]{:S(2)}, u32[]{:S(2)}) collective-permute-start(bf16[144,256]{1,0:T(8,128)(2,1)S(1)} %add_convert_fusion), channel_id=1, source_target_pairs={{0,192},{32,224},{64,128},{96,160},{128,64},{160,96},{192,0},{224,... | collective-permute-start | bytes 221192 | tf_op jit(solution)/shard_map/ppermute | solution.py:318
  95.1 6.4 %collective-permute-start.6 = (bf16[144,256]{1,0:T(8,128)(2,1)S(1)}, bf16[144,256]{1,0:T(8,128)(2,1)S(1)}, u32[]{:S(2)}, u32[]{:S(2)}) collective-permute-start(bf16[144,256]{1,0:T(8,128)(2,1)S(1)} %multiply_convert_fusion.refs_0_), channel_id=1, source_target_pairs={{0,96},{32,64},{64,32},{96,0},{128,224},{160,192},{192,160},{224,1... | collective-permute-start | bytes 221192 | tf_op jit(solution)/shard_map/ppermute | solution.py:318
  97.1 6.4 %collective-permute-start.5 = (bf16[144,256]{1,0:T(8,128)(2,1)S(1)}, bf16[144,256]{1,0:T(8,128)(2,1)S(1)}, u32[]{:S(2)}, u32[]{:S(2)}) collective-permute-start(bf16[144,256]{1,0:T(8,128)(2,1)S(1)} %multiply_convert_fusion.refs_0_), channel_id=1, source_target_pairs={{0,64},{32,96},{64,0},{96,32},{128,192},{160,224},{192,128},{224,1... | collective-permute-start | bytes 221192 | tf_op jit(solution)/shard_map/ppermute | solution.py:318
  98.2 5.3 %collective-permute-start.4 = (bf16[144,256]{1,0:T(8,128)(2,1)S(1)}, bf16[144,256]{1,0:T(8,128)(2,1)S(1)}, u32[]{:S(2)}, u32[]{:S(2)}) collective-permute-start(bf16[144,256]{1,0:T(8,128)(2,1)S(1)} %multiply_convert_fusion.refs_0_), channel_id=1, source_target_pairs={{0,32},{32,0},{64,96},{96,64},{128,160},{160,128},{192,224},{224,1... | collective-permute-start | bytes 221192 | tf_op jit(solution)/shard_map/ppermute | solution.py:318

commit v7 on v6

--- a/solution.py
+++ b/solution.py
@@ -19,7 +19,6 @@
 SMOOTH_HALF = 11
 EPS_WHITE = 1e-06
 HALF_HOURS = 4
-PARTNER = 6
 WHITEN_VMEM = 58 * 2**20
 CORRELATE_VMEM = 24 * 2**20
 SPREAD_VMEM = 8 * 2**20
@@ -180,7 +179,7 @@
 
 
 def share_of(device):
-    return jnp.where(device < HALF_HOURS, device, device ^ PARTNER)
+    return jnp.minimum(device, 2 * HALF_HOURS - 1 - device)
 
 
 def correlate_kernel(recv_ref, slots_ref, lag_hbm, *refs):
@@ -323,7 +322,7 @@
     for k in range(1, HALF_HOURS):
         mine = mine + swap(shares[k], k).astype(F32)
     mine = mine.astype(BF16)
-    other = swap(mine, PARTNER)
+    other = swap(mine, 2 * HALF_HOURS - 1)
     average = (mine.astype(F32) + other.astype(F32)) / hours_all
     size = jnp.abs(average) + 0.1
     stacked = (jnp.sign(average) * (size * size - 0.01)).astype(BF16)

time: 105 us -> 104 us (level)
  no operation moved by 1% of the time
where the time goes in v7:
time: 104 us
  blocking collectives  62.7 us (60%)
  starting transfers between devices  14.2 us (14%)
  Pallas kernels  13.5 us (13%)
  waiting for transfers between devices  13.5 us (13%)
    all_to_all x1, blocking collectives, local(): lax.all_to_all(outgoing, 'pair', split_axis=0, concat_axis=0, tiled=True)  62.7 us
    ppermute x7, starting transfers between devices, swap(): lax.ppermute(array, 'hour', [(i, i ^ distance) for i in range(2 * HALF_HO...  14.2 us
    ppermute x7, waiting for transfers between devices, swap(): lax.ppermute(array, 'hour', [(i, i ^ distance) for i in range(2 * HALF_HO...  13.5 us
    pallas_call x1, Pallas kernels, whiten(): pl.pallas_call(whiten_kernel, in_specs=[hbm] * 6, out_specs=hbm, out_shap...  7.23 us
    pallas_call x1, Pallas kernels, correlate(): pl.pallas_call(correlate_kernel, in_specs=[vmem, vmem, pl.BlockSpec(memor...  5.43 us
  transfers between devices with their start and end apart: 7, of which 5 were waited for; matrix products, arithmetic and copies ran while one was open for 0% of the time, Pallas kernels for 0%

profile of v7, /device:TPU:8, one launch (start us, length us, event | category | flops | bytes accessed | tf_op | source)
XLA Modules:
  0.0 104.2 jit_solution(12510741514973910466)
XLA Ops:
  0.0 7.2 %shard_map.82 = bf16[32,48,1536]{2,1,0:T(8,128)(2,1)} custom-call(bf16[3,3,16,3712]{3,2,1,0:T(8,128)(2,1)} %bitcast.11, s32[3,2,16]{2,1,0:T(2,128)} %bitcast.12, s32[3,2,16]{2,1,0:T(2,128)} %bitcast.13, s32[4,32]{1,0:T(4,128)} %bitcast.14, bf16[1024,1024]{1,0:T(8,128)(2,1)} %constant.14.clone.dft_hbm, bf16[512,512]{1,0:T(8,128)(2,1)} %constant.15.clone.band_hbm), custom_call_target="tpu_custom_call" | custom-call | tf_op jit(solution)/shard_map/pallas_call | solution.py:259
  7.2 0.0 copy-start
  7.2 0.0 copy-start.1
  7.3 62.7 %all_to_all.5.recv_ref = bf16[32,48,1536]{2,1,0:T(8,128)(2,1)S(1)} all-to-all(bf16[32,48,1536]{2,1,0:T(8,128)(2,1)} %shard_map.82), channel_id=1, replica_groups=mesh['hour'=8,'pair'=32] {'pair'}, dimensions={0} | all-to-all | bytes 9437184 | tf_op jit(solution)/shard_map/all_to_all | solution.py:346
  70.0 0.0 copy-done
  70.0 0.0 copy-done.1
  70.0 5.4 %shard_map.83 = (bf16[144,256]{1,0:T(8,128)(2,1)S(1)}, bf16[144,256]{1,0:T(8,128)(2,1)S(1)}, bf16[144,256]{1,0:T(8,128)(2,1)S(1)}, bf16[144,256]{1,0:T(8,128)(2,1)S(1)}) custom-call(bf16[32,48,1536]{2,1,0:T(8,128)(2,1)S(1)} %all_to_all.5.recv_ref, s32[2,64]{1,0:T(2,128)S(1)} %bitcast.10, bf16[1024,256]{1,0:T(8,128)(2,1)S(1)} %copy-done), custom_call_target="tpu_custom_call" | custom-call | tf_op jit(solution)/shard_map/pallas_call | solution.py:292
  75.4 2.0 %collective-permute-start = (bf16[144,256]{1,0:T(8,128)(2,1)S(1)}, bf16[144,256]{1,0:T(8,128)(2,1)S(1)}, u32[]{:S(2)}, u32[]{:S(2)}) collective-permute-start(bf16[144,256]{1,0:T(8,128)(2,1)S(1)} %get-tuple-element.10), channel_id=1, source_target_pairs={{0,32},{32,0},{64,96},{96,64},{128,160},{160,128},{192,224},{224,1... | collective-permute-start | bytes 221192 | tf_op jit(solution)/shard_map/ppermute | solution.py:317
  77.4 3.3 %collective-permute-start.1 = (bf16[144,256]{1,0:T(8,128)(2,1)S(1)}, bf16[144,256]{1,0:T(8,128)(2,1)S(1)}, u32[]{:S(2)}, u32[]{:S(2)}) collective-permute-start(bf16[144,256]{1,0:T(8,128)(2,1)S(1)} %get-tuple-element.11), channel_id=1, source_target_pairs={{0,64},{32,96},{64,0},{96,32},{128,192},{160,224},{192,128},{224,1... | collective-permute-start | bytes 221192 | tf_op jit(solution)/shard_map/ppermute | solution.py:317
  80.7 0.0 collective-permute-start.2
  80.7 0.0 collective-permute-done
  80.7 5.3 %collective-permute-done.1 = bf16[144,256]{1,0:T(8,128)(2,1)S(1)} collective-permute-done((bf16[144,256]{1,0:T(8,128)(2,1)S(1)}, bf16[144,256]{1,0:T(8,128)(2,1)S(1)}, u32[]{:S(2)}, u32[]{:S(2)}) %collective-permute-start.1) | collective-permute-done | bytes 73760 | tf_op jit(solution)/shard_map/ppermute | solution.py:317
  86.1 0.9 collective-permute-done.2
  87.0 4.5 %collective-permute-start.3 = (bf16[144,256]{1,0:T(8,128)(2,1)S(1)}, bf16[144,256]{1,0:T(8,128)(2,1)S(1)}, u32[]{:S(2)}, u32[]{:S(2)}) collective-permute-start(bf16[144,256]{1,0:T(8,128)(2,1)S(1)} %add_convert_fusion), channel_id=1, source_target_pairs={{0,224},{32,192},{64,160},{96,128},{128,96},{160,64},{192,32},{224... | collective-permute-start | bytes 221192 | tf_op jit(solution)/shard_map/ppermute | solution.py:317
  91.4 3.7 %collective-permute-done.3 = bf16[144,256]{1,0:T(8,128)(2,1)S(1)} collective-permute-done((bf16[144,256]{1,0:T(8,128)(2,1)S(1)}, bf16[144,256]{1,0:T(8,128)(2,1)S(1)}, u32[]{:S(2)}, u32[]{:S(2)}) %collective-permute-start.3) | collective-permute-done | bytes 73760 | tf_op jit(solution)/shard_map/ppermute | solution.py:317
  95.1 0.1 multiply_convert_fusion.refs_0_
  95.2 2.2 %collective-permute-start.6 = (bf16[144,256]{1,0:T(8,128)(2,1)S(1)}, bf16[144,256]{1,0:T(8,128)(2,1)S(1)}, u32[]{:S(2)}, u32[]{:S(2)}) collective-permute-start(bf16[144,256]{1,0:T(8,128)(2,1)S(1)} %multiply_convert_fusion.refs_0_), channel_id=1, source_target_pairs={{0,96},{32,64},{64,32},{96,0},{128,224},{160,192},{192,160},{224,1... | collective-permute-start | bytes 221192 | tf_op jit(solution)/shard_map/ppermute | solution.py:317
  97.4 0.5 collective-permute-start.5
  97.9 1.8 %collective-permute-start.4 = (bf16[144,256]{1,0:T(8,128)(2,1)S(1)}, bf16[144,256]{1,0:T(8,128)(2,1)S(1)}, u32[]{:S(2)}, u32[]{:S(2)}) collective-permute-start(bf16[144,256]{1,0:T(8,128)(2,1)S(1)} %multiply_convert_fusion.refs_0_), channel_id=1, source_target_pairs={{0,32},{32,0},{64,96},{96,64},{128,160},{160,128},{192,224},{224,1... | collective-permute-start | bytes 221192 | tf_op jit(solution)/shard_map/ppermute | solution.py:317
  99.7 1.8 %collective-permute-done.6.refs_3_ = bf16[144,256]{1,0:T(8,128)(2,1)S(1)} collective-permute-done((bf16[144,256]{1,0:T(8,128)(2,1)S(1)}, bf16[144,256]{1,0:T(8,128)(2,1)S(1)}, u32[]{:S(2)}, u32[]{:S(2)}) %collective-permute-start.6) | collective-permute-done | bytes 73760 | tf_op jit(solution)/shard_map/ppermute | solution.py:317
  101.4 1.9 %collective-permute-done.5.refs_2_ = bf16[144,256]{1,0:T(8,128)(2,1)S(1)} collective-permute-done((bf16[144,256]{1,0:T(8,128)(2,1)S(1)}, bf16[144,256]{1,0:T(8,128)(2,1)S(1)}, u32[]{:S(2)}, u32[]{:S(2)}) %collective-permute-start.5) | collective-permute-done | bytes 73760 | tf_op jit(solution)/shard_map/ppermute | solution.py:317
  103.3 0.0 collective-permute-done.4.refs_1_
  103.3 0.9 spread_result.1
  (1 shorter events, 0.0 us)
Async XLA Ops:
  7.2 62.8 %copy-start = (bf16[1024,256]{1,0:T(8,128)(2,1)S(1)}, bf16[1024,256]{1,0:T(8,128)(2,1)}, u32[]{:S(2)}) copy-start(bf16[1024,256]{1,0:T(8,128)(2,1)} %constant.16.clone.lag_hbm) | copy-start | bytes 1572868
  7.2 62.7 %copy-start.1 = (s32[64,2]{0,1:T(2,128)S(1)}, s32[64,2]{0,1:T(2,128)}, u32[]{:S(2)}) copy-start(s32[64,2]{0,1:T(2,128)} %param.12) | copy-start | bytes 1540
  75.4 5.3 %collective-permute-start = (bf16[144,256]{1,0:T(8,128)(2,1)S(1)}, bf16[144,256]{1,0:T(8,128)(2,1)S(1)}, u32[]{:S(2)}, u32[]{:S(2)}) collective-permute-start(bf16[144,256]{1,0:T(8,128)(2,1)S(1)} %get-tuple-element.10), channel_id=1, source_target_pairs={{0,32},{32,0},{64,96},{96,64},{128,160},{160,128},{192,224},{224,1... | collective-permute-start | bytes 221192 | tf_op jit(solution)/shard_map/ppermute | solution.py:317
  77.4 8.6 %collective-permute-start.1 = (bf16[144,256]{1,0:T(8,128)(2,1)S(1)}, bf16[144,256]{1,0:T(8,128)(2,1)S(1)}, u32[]{:S(2)}, u32[]{:S(2)}) collective-permute-start(bf16[144,256]{1,0:T(8,128)(2,1)S(1)} %get-tuple-element.11), channel_id=1, source_target_pairs={{0,64},{32,96},{64,0},{96,32},{128,192},{160,224},{192,128},{224,1... | collective-permute-start | bytes 221192 | tf_op jit(solution)/shard_map/ppermute | solution.py:317
  80.7 6.2 %collective-permute-start.2 = (bf16[144,256]{1,0:T(8,128)(2,1)S(1)}, bf16[144,256]{1,0:T(8,128)(2,1)S(1)}, u32[]{:S(2)}, u32[]{:S(2)}) collective-permute-start(bf16[144,256]{1,0:T(8,128)(2,1)S(1)} %get-tuple-element.12), channel_id=1, source_target_pairs={{0,96},{32,64},{64,32},{96,0},{128,224},{160,192},{192,160},{224,1... | collective-permute-start | bytes 221192 | tf_op jit(solution)/shard_map/ppermute | solution.py:317
  87.0 8.2 %collective-permute-start.3 = (bf16[144,256]{1,0:T(8,128)(2,1)S(1)}, bf16[144,256]{1,0:T(8,128)(2,1)S(1)}, u32[]{:S(2)}, u32[]{:S(2)}) collective-permute-start(bf16[144,256]{1,0:T(8,128)(2,1)S(1)} %add_convert_fusion), channel_id=1, source_target_pairs={{0,224},{32,192},{64,160},{96,128},{128,96},{160,64},{192,32},{224... | collective-permute-start | bytes 221192 | tf_op jit(solution)/shard_map/ppermute | solution.py:317
  95.2 6.2 %collective-permute-start.6 = (bf16[144,256]{1,0:T(8,128)(2,1)S(1)}, bf16[144,256]{1,0:T(8,128)(2,1)S(1)}, u32[]{:S(2)}, u32[]{:S(2)}) collective-permute-start(bf16[144,256]{1,0:T(8,128)(2,1)S(1)} %multiply_convert_fusion.refs_0_), channel_id=1, source_target_pairs={{0,96},{32,64},{64,32},{96,0},{128,224},{160,192},{192,160},{224,1... | collective-permute-start | bytes 221192 | tf_op jit(solution)/shard_map/ppermute | solution.py:317
  97.4 6.0 %collective-permute-start.5 = (bf16[144,256]{1,0:T(8,128)(2,1)S(1)}, bf16[144,256]{1,0:T(8,128)(2,1)S(1)}, u32[]{:S(2)}, u32[]{:S(2)}) collective-permute-start(bf16[144,256]{1,0:T(8,128)(2,1)S(1)} %multiply_convert_fusion.refs_0_), channel_id=1, source_target_pairs={{0,64},{32,96},{64,0},{96,32},{128,192},{160,224},{192,128},{224,1... | collective-permute-start | bytes 221192 | tf_op jit(solution)/shard_map/ppermute | solution.py:317
  97.9 5.4 %collective-permute-start.4 = (bf16[144,256]{1,0:T(8,128)(2,1)S(1)}, bf16[144,256]{1,0:T(8,128)(2,1)S(1)}, u32[]{:S(2)}, u32[]{:S(2)}) collective-permute-start(bf16[144,256]{1,0:T(8,128)(2,1)S(1)} %multiply_convert_fusion.refs_0_), channel_id=1, source_target_pairs={{0,32},{32,0},{64,96},{96,64},{128,160},{160,128},{192,224},{224,1... | collective-permute-start | bytes 221192 | tf_op jit(solution)/shard_map/ppermute | solution.py:317

commit v8 on v7

--- a/solution.py
+++ b/solution.py
@@ -182,14 +182,12 @@
     return jnp.minimum(device, 2 * HALF_HOURS - 1 - device)
 
 
-def correlate_kernel(recv_ref, slots_ref, lag_hbm, *refs):
-    out_refs, (pick_ref, lag_ref, side_ref, cross_ref, total_ref, sem) = refs[:HALF_HOURS], refs[HALF_HOURS:]
+def correlate_kernel(recv_ref, slots_ref, lag_ref, *refs):
+    out_refs, (pick_ref, side_ref, cross_ref, total_ref) = refs[:HALF_HOURS], refs[HALF_HOURS:]
     pairs = slots_ref.shape[1]
     owners, all_rows, _ = recv_ref.shape
     rows = all_rows // cross_ref.shape[0]
     half = NFREQ // 2
-    lag_copy = pltpu.make_async_copy(lag_hbm, lag_ref, sem)
-    lag_copy.start()
 
     arrived_row = lax.broadcasted_iota(jnp.int32, (pairs, owners * rows), 1)
     for side in range(2):
@@ -235,7 +233,6 @@
         else:
             total_ref[...] += rooted
 
-    lag_copy.wait()
     steps = [(h, n) for h in range(cross_ref.shape[0]) for n in range(2)]
     select(*steps[0])
     for now, later in zip(steps, steps[1:] + [None]):
@@ -291,16 +288,14 @@
     share = (channels * pairs // HALF_HOURS, LAGS)
     return pl.pallas_call(
         correlate_kernel,
-        in_specs=[vmem, vmem, pl.BlockSpec(memory_space=pltpu.HBM)],
+        in_specs=[vmem, vmem, vmem],
         out_specs=[vmem] * HALF_HOURS,
         out_shape=[jax.ShapeDtypeStruct(share, BF16)] * HALF_HOURS,
         scratch_shapes=[
             pltpu.VMEM((2 * PARTS * pairs, owners * rows), BF16),
-            pltpu.VMEM((2 * NFREQ, LAGS), BF16),
             pltpu.VMEM((2, 2 * PARTS * pairs, width // 2), F32),
             pltpu.VMEM((hours, channels * pairs, 2 * NFREQ), BF16),
             pltpu.VMEM((HALF_HOURS,) + share, F32),
-            pltpu.SemaphoreType.DMA(()),
         ],
         compiler_params=pltpu.CompilerParams(vmem_limit_bytes=CORRELATE_VMEM),
     )(received, slots, lag_table())
@@ -319,14 +314,15 @@
 
 def stack_hours(shares, hours_all):
     mine = shares[0].astype(F32)
-    for k in range(1, HALF_HOURS):
+    for k in (2, 1, 3):
         mine = mine + swap(shares[k], k).astype(F32)
     mine = mine.astype(BF16)
     other = swap(mine, 2 * HALF_HOURS - 1)
     average = (mine.astype(F32) + other.astype(F32)) / hours_all
     size = jnp.abs(average) + 0.1
     stacked = (jnp.sign(average) * (size * size - 0.01)).astype(BF16)
-    parts = [stacked] + [swap(stacked, k) for k in range(1, HALF_HOURS)]
+    others = {k: swap(stacked, k) for k in (1, 2, 3)}
+    parts = [stacked] + [others[k] for k in range(1, HALF_HOURS)]
     return pl.pallas_call(
         spread_kernel,
         out_shape=jax.ShapeDtypeStruct((HALF_HOURS,) + stacked.shape, F32),

time: 104 us -> 104 us (level)
  transfers between devices with their start and end apart: 7 -> 7, of which waited for: 5 -> 6; matrix products, arithmetic and copies ran while one was open for 0% -> 0% of each run, Pallas kernels for 0% -> 0%
where the time goes in v8:
time: 104 us
  blocking collectives  62.7 us (60%)
  waiting for transfers between devices  13.7 us (13%)
  starting transfers between devices  13.5 us (13%)
  Pallas kernels  13.4 us (13%)
    all_to_all x1, blocking collectives, local(): lax.all_to_all(outgoing, 'pair', split_axis=0, concat_axis=0, tiled=True)  62.7 us
    ppermute x7, waiting for transfers between devices, swap(): lax.ppermute(array, 'hour', [(i, i ^ distance) for i in range(2 * HALF_HO...  13.7 us
    ppermute x7, starting transfers between devices, swap(): lax.ppermute(array, 'hour', [(i, i ^ distance) for i in range(2 * HALF_HO...  13.5 us
    pallas_call x1, Pallas kernels, whiten(): pl.pallas_call(whiten_kernel, in_specs=[hbm] * 6, out_specs=hbm, out_shap...  7.23 us
    pallas_call x1, Pallas kernels, correlate(): pl.pallas_call(correlate_kernel, in_specs=[vmem, vmem, vmem], out_specs=[...  5.31 us
  transfers between devices with their start and end apart: 7, of which 6 were waited for; matrix products, arithmetic and copies ran while one was open for 0% of the time, Pallas kernels for 0%

profile of v8, /device:TPU:8, one launch (start us, length us, event | category | flops | bytes accessed | tf_op | source)
XLA Modules:
  0.0 103.5 jit_solution(607325107749199504)
XLA Ops:
  0.0 7.2 %shard_map.82 = bf16[32,48,1536]{2,1,0:T(8,128)(2,1)} custom-call(bf16[3,3,16,3712]{3,2,1,0:T(8,128)(2,1)} %bitcast.11, s32[3,2,16]{2,1,0:T(2,128)} %bitcast.12, s32[3,2,16]{2,1,0:T(2,128)} %bitcast.13, s32[4,32]{1,0:T(4,128)} %bitcast.14, bf16[1024,1024]{1,0:T(8,128)(2,1)} %constant.14.clone.dft_hbm, bf16[512,512]{1,0:T(8,128)(2,1)} %constant.15.clone.band_hbm), custom_call_target="tpu_custom_call" | custom-call | tf_op jit(solution)/shard_map/pallas_call | solution.py:256
  7.2 0.0 copy-start
  7.2 0.0 copy-start.1
  7.3 62.7 %all_to_all.5.recv_ref = bf16[32,48,1536]{2,1,0:T(8,128)(2,1)S(1)} all-to-all(bf16[32,48,1536]{2,1,0:T(8,128)(2,1)} %shard_map.82), channel_id=1, replica_groups=mesh['hour'=8,'pair'=32] {'pair'}, dimensions={0} | all-to-all | bytes 9437184 | tf_op jit(solution)/shard_map/all_to_all | solution.py:342
  70.0 0.0 copy-done
  70.0 0.0 copy-done.1
  70.0 5.3 %shard_map.83 = (bf16[144,256]{1,0:T(8,128)(2,1)S(1)}, bf16[144,256]{1,0:T(8,128)(2,1)S(1)}, bf16[144,256]{1,0:T(8,128)(2,1)S(1)}, bf16[144,256]{1,0:T(8,128)(2,1)S(1)}) custom-call(bf16[32,48,1536]{2,1,0:T(8,128)(2,1)S(1)} %all_to_all.5.recv_ref, s32[2,64]{1,0:T(2,128)S(1)} %bitcast.10, bf16[1024,256]{1,0:T(8,128)(2,1)S(1)} %copy-done), custom_call_target="tpu_custom_call" | custom-call | tf_op jit(solution)/shard_map/pallas_call | solution.py:289
  75.3 3.4 %collective-permute-start = (bf16[144,256]{1,0:T(8,128)(2,1)S(1)}, bf16[144,256]{1,0:T(8,128)(2,1)S(1)}, u32[]{:S(2)}, u32[]{:S(2)}) collective-permute-start(bf16[144,256]{1,0:T(8,128)(2,1)S(1)} %get-tuple-element.10), channel_id=1, source_target_pairs={{0,64},{32,96},{64,0},{96,32},{128,192},{160,224},{192,128},{224,1... | collective-permute-start | bytes 221192 | tf_op jit(solution)/shard_map/ppermute | solution.py:312
  78.7 1.9 %collective-permute-start.1 = (bf16[144,256]{1,0:T(8,128)(2,1)S(1)}, bf16[144,256]{1,0:T(8,128)(2,1)S(1)}, u32[]{:S(2)}, u32[]{:S(2)}) collective-permute-start(bf16[144,256]{1,0:T(8,128)(2,1)S(1)} %get-tuple-element.11), channel_id=1, source_target_pairs={{0,32},{32,0},{64,96},{96,64},{128,160},{160,128},{192,224},{224,1... | collective-permute-start | bytes 221192 | tf_op jit(solution)/shard_map/ppermute | solution.py:312
  80.6 0.0 collective-permute-start.2
  80.6 2.3 %collective-permute-done = bf16[144,256]{1,0:T(8,128)(2,1)S(1)} collective-permute-done((bf16[144,256]{1,0:T(8,128)(2,1)S(1)}, bf16[144,256]{1,0:T(8,128)(2,1)S(1)}, u32[]{:S(2)}, u32[]{:S(2)}) %collective-permute-start) | collective-permute-done | bytes 73760 | tf_op jit(solution)/shard_map/ppermute | solution.py:312
  82.9 0.3 collective-permute-done.1
  83.2 3.5 %collective-permute-done.2 = bf16[144,256]{1,0:T(8,128)(2,1)S(1)} collective-permute-done((bf16[144,256]{1,0:T(8,128)(2,1)S(1)}, bf16[144,256]{1,0:T(8,128)(2,1)S(1)}, u32[]{:S(2)}, u32[]{:S(2)}) %collective-permute-start.2) | collective-permute-done | bytes 73760 | tf_op jit(solution)/shard_map/ppermute | solution.py:312
  86.8 3.8 %collective-permute-start.3 = (bf16[144,256]{1,0:T(8,128)(2,1)S(1)}, bf16[144,256]{1,0:T(8,128)(2,1)S(1)}, u32[]{:S(2)}, u32[]{:S(2)}) collective-permute-start(bf16[144,256]{1,0:T(8,128)(2,1)S(1)} %add_convert_fusion), channel_id=1, source_target_pairs={{0,224},{32,192},{64,160},{96,128},{128,96},{160,64},{192,32},{224... | collective-permute-start | bytes 221192 | tf_op jit(solution)/shard_map/ppermute | solution.py:312
  90.6 3.8 %collective-permute-done.3 = bf16[144,256]{1,0:T(8,128)(2,1)S(1)} collective-permute-done((bf16[144,256]{1,0:T(8,128)(2,1)S(1)}, bf16[144,256]{1,0:T(8,128)(2,1)S(1)}, u32[]{:S(2)}, u32[]{:S(2)}) %collective-permute-start.3) | collective-permute-done | bytes 73760 | tf_op jit(solution)/shard_map/ppermute | solution.py:312
  94.4 0.1 multiply_convert_fusion.refs_0_
  94.5 1.7 %collective-permute-start.6 = (bf16[144,256]{1,0:T(8,128)(2,1)S(1)}, bf16[144,256]{1,0:T(8,128)(2,1)S(1)}, u32[]{:S(2)}, u32[]{:S(2)}) collective-permute-start(bf16[144,256]{1,0:T(8,128)(2,1)S(1)} %multiply_convert_fusion.refs_0_), channel_id=1, source_target_pairs={{0,96},{32,64},{64,32},{96,0},{128,224},{160,192},{192,160},{224,1... | collective-permute-start | bytes 221192 | tf_op jit(solution)/shard_map/ppermute | solution.py:312
  96.2 0.8 collective-permute-start.5
  97.0 1.9 %collective-permute-start.4 = (bf16[144,256]{1,0:T(8,128)(2,1)S(1)}, bf16[144,256]{1,0:T(8,128)(2,1)S(1)}, u32[]{:S(2)}, u32[]{:S(2)}) collective-permute-start(bf16[144,256]{1,0:T(8,128)(2,1)S(1)} %multiply_convert_fusion.refs_0_), channel_id=1, source_target_pairs={{0,32},{32,0},{64,96},{96,64},{128,160},{160,128},{192,224},{224,1... | collective-permute-start | bytes 221192 | tf_op jit(solution)/shard_map/ppermute | solution.py:312
  98.9 2.3 %collective-permute-done.6.refs_3_ = bf16[144,256]{1,0:T(8,128)(2,1)S(1)} collective-permute-done((bf16[144,256]{1,0:T(8,128)(2,1)S(1)}, bf16[144,256]{1,0:T(8,128)(2,1)S(1)}, u32[]{:S(2)}, u32[]{:S(2)}) %collective-permute-start.6) | collective-permute-done | bytes 73760 | tf_op jit(solution)/shard_map/ppermute | solution.py:312
  101.2 1.5 %collective-permute-done.5.refs_2_ = bf16[144,256]{1,0:T(8,128)(2,1)S(1)} collective-permute-done((bf16[144,256]{1,0:T(8,128)(2,1)S(1)}, bf16[144,256]{1,0:T(8,128)(2,1)S(1)}, u32[]{:S(2)}, u32[]{:S(2)}) %collective-permute-start.5) | collective-permute-done | bytes 73760 | tf_op jit(solution)/shard_map/ppermute | solution.py:312
  102.7 0.0 collective-permute-done.4.refs_1_
  102.7 0.9 spread_result.1
  (1 shorter events, 0.0 us)
Async XLA Ops:
  7.2 62.8 %copy-start = (bf16[1024,256]{1,0:T(8,128)(2,1)S(1)}, bf16[1024,256]{1,0:T(8,128)(2,1)}, u32[]{:S(2)}) copy-start(bf16[1024,256]{1,0:T(8,128)(2,1)} %constant.16.clone.lag_ref) | copy-start | bytes 1572868
  7.2 62.7 %copy-start.1 = (s32[64,2]{0,1:T(2,128)S(1)}, s32[64,2]{0,1:T(2,128)}, u32[]{:S(2)}) copy-start(s32[64,2]{0,1:T(2,128)} %param.12) | copy-start | bytes 1540
  75.3 7.6 %collective-permute-start = (bf16[144,256]{1,0:T(8,128)(2,1)S(1)}, bf16[144,256]{1,0:T(8,128)(2,1)S(1)}, u32[]{:S(2)}, u32[]{:S(2)}) collective-permute-start(bf16[144,256]{1,0:T(8,128)(2,1)S(1)} %get-tuple-element.10), channel_id=1, source_target_pairs={{0,64},{32,96},{64,0},{96,32},{128,192},{160,224},{192,128},{224,1... | collective-permute-start | bytes 221192 | tf_op jit(solution)/shard_map/ppermute | solution.py:312
  78.7 4.5 %collective-permute-start.1 = (bf16[144,256]{1,0:T(8,128)(2,1)S(1)}, bf16[144,256]{1,0:T(8,128)(2,1)S(1)}, u32[]{:S(2)}, u32[]{:S(2)}) collective-permute-start(bf16[144,256]{1,0:T(8,128)(2,1)S(1)} %get-tuple-element.11), channel_id=1, source_target_pairs={{0,32},{32,0},{64,96},{96,64},{128,160},{160,128},{192,224},{224,1... | collective-permute-start | bytes 221192 | tf_op jit(solution)/shard_map/ppermute | solution.py:312
  80.6 6.2 %collective-permute-start.2 = (bf16[144,256]{1,0:T(8,128)(2,1)S(1)}, bf16[144,256]{1,0:T(8,128)(2,1)S(1)}, u32[]{:S(2)}, u32[]{:S(2)}) collective-permute-start(bf16[144,256]{1,0:T(8,128)(2,1)S(1)} %get-tuple-element.12), channel_id=1, source_target_pairs={{0,96},{32,64},{64,32},{96,0},{128,224},{160,192},{192,160},{224,1... | collective-permute-start | bytes 221192 | tf_op jit(solution)/shard_map/ppermute | solution.py:312
  86.8 7.6 %collective-permute-start.3 = (bf16[144,256]{1,0:T(8,128)(2,1)S(1)}, bf16[144,256]{1,0:T(8,128)(2,1)S(1)}, u32[]{:S(2)}, u32[]{:S(2)}) collective-permute-start(bf16[144,256]{1,0:T(8,128)(2,1)S(1)} %add_convert_fusion), channel_id=1, source_target_pairs={{0,224},{32,192},{64,160},{96,128},{128,96},{160,64},{192,32},{224... | collective-permute-start | bytes 221192 | tf_op jit(solution)/shard_map/ppermute | solution.py:312
  94.5 6.7 %collective-permute-start.6 = (bf16[144,256]{1,0:T(8,128)(2,1)S(1)}, bf16[144,256]{1,0:T(8,128)(2,1)S(1)}, u32[]{:S(2)}, u32[]{:S(2)}) collective-permute-start(bf16[144,256]{1,0:T(8,128)(2,1)S(1)} %multiply_convert_fusion.refs_0_), channel_id=1, source_target_pairs={{0,96},{32,64},{64,32},{96,0},{128,224},{160,192},{192,160},{224,1... | collective-permute-start | bytes 221192 | tf_op jit(solution)/shard_map/ppermute | solution.py:312
  96.2 6.5 %collective-permute-start.5 = (bf16[144,256]{1,0:T(8,128)(2,1)S(1)}, bf16[144,256]{1,0:T(8,128)(2,1)S(1)}, u32[]{:S(2)}, u32[]{:S(2)}) collective-permute-start(bf16[144,256]{1,0:T(8,128)(2,1)S(1)} %multiply_convert_fusion.refs_0_), channel_id=1, source_target_pairs={{0,64},{32,96},{64,0},{96,32},{128,192},{160,224},{192,128},{224,1... | collective-permute-start | bytes 221192 | tf_op jit(solution)/shard_map/ppermute | solution.py:312
  97.0 5.6 %collective-permute-start.4 = (bf16[144,256]{1,0:T(8,128)(2,1)S(1)}, bf16[144,256]{1,0:T(8,128)(2,1)S(1)}, u32[]{:S(2)}, u32[]{:S(2)}) collective-permute-start(bf16[144,256]{1,0:T(8,128)(2,1)S(1)} %multiply_convert_fusion.refs_0_), channel_id=1, source_target_pairs={{0,32},{32,0},{64,96},{96,64},{128,160},{160,128},{192,224},{224,1... | collective-permute-start | bytes 221192 | tf_op jit(solution)/shard_map/ppermute | solution.py:312

commit v9 on v8

--- a/solution.py
+++ b/solution.py
@@ -78,9 +78,9 @@
 
 
 def whiten_kernel(
-    raw_hbm, start_hbm, count_hbm, send_hbm, dft_hbm, band_hbm, out_hbm,
+    raw_hbm, start_hbm, count_hbm, send_hbm, slots_hbm, dft_hbm, band_hbm, out_hbm, pair_hbm,
     raw_ref, start_ref, count_ref, send_ref, dft_ref, band_ref, seg_ref, spec_ref, white_ref, pick_ref, out_ref,
-    small_sem, raw_sem, table_sem, out_sem,
+    slots_ref, pair_ref, small_sem, raw_sem, table_sem, out_sem, pair_sem,
 ):
     hours, _, stations, _ = raw_ref.shape
     capacity, owners = send_ref.shape
@@ -90,6 +90,7 @@
         pltpu.make_async_copy(start_hbm, start_ref, small_sem.at[0]),
         pltpu.make_async_copy(count_hbm, count_ref, small_sem.at[1]),
         pltpu.make_async_copy(send_hbm, send_ref, small_sem.at[2]),
+        pltpu.make_async_copy(slots_hbm, slots_ref, small_sem.at[3]),
     ]
     raw_copies = [pltpu.make_async_copy(raw_hbm.at[h], raw_ref.at[h], raw_sem.at[h]) for h in range(hours)]
     dft_copy = pltpu.make_async_copy(dft_hbm, dft_ref, table_sem.at[0])
@@ -113,6 +114,17 @@
     out_row = lax.broadcasted_iota(jnp.int32, (owners * rows, PARTS * stations), 0)
     white_row = lax.broadcasted_iota(jnp.int32, (owners * rows, PARTS * stations), 1)
     pick_ref[...] = (out_row % PARTS * stations + wanted == white_row).astype(BF16)
+
+    pairs = slots_ref.shape[1]
+    arrived_row = lax.broadcasted_iota(jnp.int32, (pairs, owners * rows), 1)
+    for side in range(2):
+        first = column(slots_ref[side : side + 1, :], pairs) * PARTS
+        for part in range(PARTS):
+            row = (side * PARTS + part) * pairs
+            pair_ref[row : row + pairs, :] = (first + part == arrived_row).astype(BF16)
+
+    pair_copy = pltpu.make_async_copy(pair_ref, pair_hbm, pair_sem)
+    pair_copy.start()
 
     time = lax.broadcasted_iota(jnp.int32, (stations, NFFT), 1)
     out_copies = []
@@ -176,25 +188,19 @@
         send_hour(h)
     for copy in out_copies:
         copy.wait()
+    pair_copy.wait()
 
 
 def share_of(device):
     return jnp.minimum(device, 2 * HALF_HOURS - 1 - device)
 
 
-def correlate_kernel(recv_ref, slots_ref, lag_ref, *refs):
-    out_refs, (pick_ref, side_ref, cross_ref, total_ref) = refs[:HALF_HOURS], refs[HALF_HOURS:]
-    pairs = slots_ref.shape[1]
+def correlate_kernel(recv_ref, pick_ref, lag_ref, *refs):
+    out_refs, (side_ref, cross_ref, total_ref) = refs[:HALF_HOURS], refs[HALF_HOURS:]
+    pairs = pick_ref.shape[0] // (2 * PARTS)
     owners, all_rows, _ = recv_ref.shape
     rows = all_rows // cross_ref.shape[0]
     half = NFREQ // 2
-
-    arrived_row = lax.broadcasted_iota(jnp.int32, (pairs, owners * rows), 1)
-    for side in range(2):
-        first = column(slots_ref[side : side + 1, :], pairs) * PARTS
-        for part in range(PARTS):
-            row = (side * PARTS + part) * pairs
-            pick_ref[row : row + pairs, :] = (first + part == arrived_row).astype(BF16)
 
     def select(h, n):
         for c in range(COMPS):
@@ -246,18 +252,22 @@
         out_ref[...] = total_ref[share_of(me ^ k)].astype(BF16)
 
 
-def whiten(panels, starts, counts, send):
+def whiten(panels, starts, counts, send, slots):
     hours, _, stations, raw = panels.shape
     capacity, owners = send.shape
     rows = capacity * PARTS
     width = COMPS * NFREQ
     block = WINDOWS * COMPS * stations
+    pair_pick = (2 * PARTS * slots.shape[1], owners * rows)
     hbm = pl.BlockSpec(memory_space=pltpu.HBM)
     return pl.pallas_call(
         whiten_kernel,
-        in_specs=[hbm] * 6,
-        out_specs=hbm,
-        out_shape=jax.ShapeDtypeStruct((owners, hours * rows, width), BF16),
+        in_specs=[hbm] * 7,
+        out_specs=[hbm, hbm],
+        out_shape=[
+            jax.ShapeDtypeStruct((owners, hours * rows, width), BF16),
+            jax.ShapeDtypeStruct(pair_pick, BF16),
+        ],
         scratch_shapes=[
             pltpu.VMEM(panels.shape, BF16),
             pltpu.VMEM(starts.shape, jnp.int32),
@@ -270,18 +280,21 @@
             pltpu.VMEM((hours, PARTS * stations, width), BF16),
             pltpu.VMEM((owners * rows, PARTS * stations), BF16),
             pltpu.VMEM((hours, owners, rows, width), BF16),
-            pltpu.SemaphoreType.DMA((3,)),
+            pltpu.VMEM(slots.shape, jnp.int32),
+            pltpu.VMEM(pair_pick, BF16),
+            pltpu.SemaphoreType.DMA((4,)),
             pltpu.SemaphoreType.DMA((hours,)),
             pltpu.SemaphoreType.DMA((2,)),
             pltpu.SemaphoreType.DMA((hours,)),
+            pltpu.SemaphoreType.DMA(()),
         ],
         compiler_params=pltpu.CompilerParams(vmem_limit_bytes=WHITEN_VMEM),
-    )(panels, starts, counts, send, dft_table(), band_table())
-
-
-def correlate(received, slots, hours):
+    )(panels, starts, counts, send, slots, dft_table(), band_table())
+
+
+def correlate(received, pick, hours):
     owners, all_rows, width = received.shape
-    pairs = slots.shape[1]
+    pairs = pick.shape[0] // (2 * PARTS)
     rows = all_rows // hours
     channels = COMPS * COMPS
     vmem = pl.BlockSpec(memory_space=pltpu.VMEM)
@@ -292,13 +305,12 @@
         out_specs=[vmem] * HALF_HOURS,
         out_shape=[jax.ShapeDtypeStruct(share, BF16)] * HALF_HOURS,
         scratch_shapes=[
-            pltpu.VMEM((2 * PARTS * pairs, owners * rows), BF16),
             pltpu.VMEM((2, 2 * PARTS * pairs, width // 2), F32),
             pltpu.VMEM((hours, channels * pairs, 2 * NFREQ), BF16),
             pltpu.VMEM((HALF_HOURS,) + share, F32),
         ],
         compiler_params=pltpu.CompilerParams(vmem_limit_bytes=CORRELATE_VMEM),
-    )(received, slots, lag_table())
+    )(received, pick, lag_table())
 
 
 def spread_kernel(*refs):
@@ -338,9 +350,9 @@
     panels = jnp.transpose(raw_panels, (1, 2, 0, 3))
     starts = jnp.transpose(window_start, (1, 2, 0))
     counts = jnp.transpose(valid_count, (1, 2, 0))
-    outgoing = whiten(panels, starts, counts, jnp.transpose(send_rows[0]))
+    outgoing, pick = whiten(panels, starts, counts, jnp.transpose(send_rows[0]), jnp.transpose(pair_slots))
     received = lax.all_to_all(outgoing, "pair", split_axis=0, concat_axis=0, tiled=True)
-    shares = correlate(received, jnp.transpose(pair_slots), hours)
+    shares = correlate(received, pick, hours)
     stacked = stack_hours(shares, hours * hour_devices)
     stacked = stacked.reshape(COMPS * COMPS, pairs, LAGS)
     return jnp.transpose(stacked, (1, 0, 2))

time: 104 us -> 104 us (level)
  no operation moved by 1% of the time
where the time goes in v9:
time: 104 us
  blocking collectives  62.7 us (60%)
  waiting for transfers between devices  13.7 us (13%)
  starting transfers between devices  13.5 us (13%)
  Pallas kernels  13.4 us (13%)
    all_to_all x1, blocking collectives, local(): lax.all_to_all(outgoing, 'pair', split_axis=0, concat_axis=0, tiled=True)  62.7 us
    ppermute x7, waiting for transfers between devices, swap(): lax.ppermute(array, 'hour', [(i, i ^ distance) for i in range(2 * HALF_HO...  13.7 us
    ppermute x7, starting transfers between devices, swap(): lax.ppermute(array, 'hour', [(i, i ^ distance) for i in range(2 * HALF_HO...  13.5 us
    pallas_call x1, Pallas kernels, whiten(): pl.pallas_call(whiten_kernel, in_specs=[hbm] * 7, out_specs=[hbm, hbm], o...  7.32 us
    pallas_call x1, Pallas kernels, correlate(): pl.pallas_call(correlate_kernel, in_specs=[vmem, vmem, vmem], out_specs=[...  5.25 us
  transfers between devices with their start and end apart: 7, of which 6 were waited for; matrix products, arithmetic and copies ran while one was open for 0% of the time, Pallas kernels for 0%

profile of v9, /device:TPU:8, one launch (start us, length us, event | category | flops | bytes accessed | tf_op | source)
XLA Modules:
  0.0 103.6 jit_solution(7397725886353528614)
XLA Ops:
  0.0 7.3 %shard_map.82 = (bf16[32,48,1536]{2,1,0:T(8,128)(2,1)}, bf16[512,512]{1,0:T(8,128)(2,1)}) custom-call(bf16[3,3,16,3712]{3,2,1,0:T(8,128)(2,1)} %bitcast.10, s32[3,2,16]{2,1,0:T(2,128)} %bitcast.11, s32[3,2,16]{2,1,0:T(2,128)} %bitcast.12, s32[4,32]{1,0:T(4,128)} %bitcast.13, s32[2,64]{1,0:T(2,128)} %bitcast.14, bf16[1024,1024]{1,0:T(8,128)(2,1)} %constant.14.clone.dft_hbm, ...), custom_call_target="tpu_custom_call" | custom-call | tf_op jit(solution)/shard_map/pallas_call | solution.py:263
  7.3 0.0 copy-start
  7.3 0.0 copy-start.1
  7.4 62.7 %all_to_all.5.recv_ref = bf16[32,48,1536]{2,1,0:T(8,128)(2,1)S(1)} all-to-all(bf16[32,48,1536]{2,1,0:T(8,128)(2,1)} %get-tuple-element.11), channel_id=1, replica_groups=mesh['hour'=8,'pair'=32] {'pair'}, dimensions={0} | all-to-all | bytes 9437184 | tf_op jit(solution)/shard_map/all_to_all | solution.py:354
  70.1 0.0 copy-done
  70.1 0.0 copy-done.1
  70.1 5.3 %shard_map.83 = (bf16[144,256]{1,0:T(8,128)(2,1)S(1)}, bf16[144,256]{1,0:T(8,128)(2,1)S(1)}, bf16[144,256]{1,0:T(8,128)(2,1)S(1)}, bf16[144,256]{1,0:T(8,128)(2,1)S(1)}) custom-call(bf16[32,48,1536]{2,1,0:T(8,128)(2,1)S(1)} %all_to_all.5.recv_ref, bf16[512,512]{1,0:T(8,128)(2,1)S(1)} %copy-done.1, bf16[1024,256]{1,0:T(8,128)(2,1)S(1)} %copy-done), custom_call_target="tpu_custom_call" | custom-call | tf_op jit(solution)/shard_map/pallas_call | solution.py:302
  75.3 3.4 %collective-permute-start = (bf16[144,256]{1,0:T(8,128)(2,1)S(1)}, bf16[144,256]{1,0:T(8,128)(2,1)S(1)}, u32[]{:S(2)}, u32[]{:S(2)}) collective-permute-start(bf16[144,256]{1,0:T(8,128)(2,1)S(1)} %get-tuple-element.14), channel_id=1, source_target_pairs={{0,64},{32,96},{64,0},{96,32},{128,192},{160,224},{192,128},{224,1... | collective-permute-start | bytes 221192 | tf_op jit(solution)/shard_map/ppermute | solution.py:324
  78.7 1.9 %collective-permute-start.1 = (bf16[144,256]{1,0:T(8,128)(2,1)S(1)}, bf16[144,256]{1,0:T(8,128)(2,1)S(1)}, u32[]{:S(2)}, u32[]{:S(2)}) collective-permute-start(bf16[144,256]{1,0:T(8,128)(2,1)S(1)} %get-tuple-element.15), channel_id=1, source_target_pairs={{0,32},{32,0},{64,96},{96,64},{128,160},{160,128},{192,224},{224,1... | collective-permute-start | bytes 221192 | tf_op jit(solution)/shard_map/ppermute | solution.py:324
  80.6 0.0 collective-permute-start.2
  80.6 2.3 %collective-permute-done = bf16[144,256]{1,0:T(8,128)(2,1)S(1)} collective-permute-done((bf16[144,256]{1,0:T(8,128)(2,1)S(1)}, bf16[144,256]{1,0:T(8,128)(2,1)S(1)}, u32[]{:S(2)}, u32[]{:S(2)}) %collective-permute-start) | collective-permute-done | bytes 73760 | tf_op jit(solution)/shard_map/ppermute | solution.py:324
  83.0 0.3 collective-permute-done.1
  83.2 3.5 %collective-permute-done.2 = bf16[144,256]{1,0:T(8,128)(2,1)S(1)} collective-permute-done((bf16[144,256]{1,0:T(8,128)(2,1)S(1)}, bf16[144,256]{1,0:T(8,128)(2,1)S(1)}, u32[]{:S(2)}, u32[]{:S(2)}) %collective-permute-start.2) | collective-permute-done | bytes 73760 | tf_op jit(solution)/shard_map/ppermute | solution.py:324
  86.8 3.8 %collective-permute-start.3 = (bf16[144,256]{1,0:T(8,128)(2,1)S(1)}, bf16[144,256]{1,0:T(8,128)(2,1)S(1)}, u32[]{:S(2)}, u32[]{:S(2)}) collective-permute-start(bf16[144,256]{1,0:T(8,128)(2,1)S(1)} %add_convert_fusion), channel_id=1, source_target_pairs={{0,224},{32,192},{64,160},{96,128},{128,96},{160,64},{192,32},{224... | collective-permute-start | bytes 221192 | tf_op jit(solution)/shard_map/ppermute | solution.py:324
  90.6 3.8 %collective-permute-done.3 = bf16[144,256]{1,0:T(8,128)(2,1)S(1)} collective-permute-done((bf16[144,256]{1,0:T(8,128)(2,1)S(1)}, bf16[144,256]{1,0:T(8,128)(2,1)S(1)}, u32[]{:S(2)}, u32[]{:S(2)}) %collective-permute-start.3) | collective-permute-done | bytes 73760 | tf_op jit(solution)/shard_map/ppermute | solution.py:324
  94.4 0.1 multiply_convert_fusion.refs_0_
  94.5 1.7 %collective-permute-start.6 = (bf16[144,256]{1,0:T(8,128)(2,1)S(1)}, bf16[144,256]{1,0:T(8,128)(2,1)S(1)}, u32[]{:S(2)}, u32[]{:S(2)}) collective-permute-start(bf16[144,256]{1,0:T(8,128)(2,1)S(1)} %multiply_convert_fusion.refs_0_), channel_id=1, source_target_pairs={{0,96},{32,64},{64,32},{96,0},{128,224},{160,192},{192,160},{224,1... | collective-permute-start | bytes 221192 | tf_op jit(solution)/shard_map/ppermute | solution.py:324
  96.2 0.8 collective-permute-start.5
  97.1 1.9 %collective-permute-start.4 = (bf16[144,256]{1,0:T(8,128)(2,1)S(1)}, bf16[144,256]{1,0:T(8,128)(2,1)S(1)}, u32[]{:S(2)}, u32[]{:S(2)}) collective-permute-start(bf16[144,256]{1,0:T(8,128)(2,1)S(1)} %multiply_convert_fusion.refs_0_), channel_id=1, source_target_pairs={{0,32},{32,0},{64,96},{96,64},{128,160},{160,128},{192,224},{224,1... | collective-permute-start | bytes 221192 | tf_op jit(solution)/shard_map/ppermute | solution.py:324
  99.0 2.2 %collective-permute-done.6.refs_3_ = bf16[144,256]{1,0:T(8,128)(2,1)S(1)} collective-permute-done((bf16[144,256]{1,0:T(8,128)(2,1)S(1)}, bf16[144,256]{1,0:T(8,128)(2,1)S(1)}, u32[]{:S(2)}, u32[]{:S(2)}) %collective-permute-start.6) | collective-permute-done | bytes 73760 | tf_op jit(solution)/shard_map/ppermute | solution.py:324
  101.2 1.5 %collective-permute-done.5.refs_2_ = bf16[144,256]{1,0:T(8,128)(2,1)S(1)} collective-permute-done((bf16[144,256]{1,0:T(8,128)(2,1)S(1)}, bf16[144,256]{1,0:T(8,128)(2,1)S(1)}, u32[]{:S(2)}, u32[]{:S(2)}) %collective-permute-start.5) | collective-permute-done | bytes 73760 | tf_op jit(solution)/shard_map/ppermute | solution.py:324
  102.7 0.0 collective-permute-done.4.refs_1_
  102.7 0.9 spread_result.1
  (1 shorter events, 0.0 us)
Async XLA Ops:
  7.3 62.8 %copy-start = (bf16[1024,256]{1,0:T(8,128)(2,1)S(1)}, bf16[1024,256]{1,0:T(8,128)(2,1)}, u32[]{:S(2)}) copy-start(bf16[1024,256]{1,0:T(8,128)(2,1)} %constant.16.clone.lag_ref) | copy-start | bytes 1572868
  7.3 62.7 %copy-start.1 = (bf16[512,512]{1,0:T(8,128)(2,1)S(1)}, bf16[512,512]{1,0:T(8,128)(2,1)}, u32[]{:S(2)}) copy-start(bf16[512,512]{1,0:T(8,128)(2,1)} %get-tuple-element.12.pick_ref) | copy-start | bytes 1572868
  75.3 7.6 %collective-permute-start = (bf16[144,256]{1,0:T(8,128)(2,1)S(1)}, bf16[144,256]{1,0:T(8,128)(2,1)S(1)}, u32[]{:S(2)}, u32[]{:S(2)}) collective-permute-start(bf16[144,256]{1,0:T(8,128)(2,1)S(1)} %get-tuple-element.14), channel_id=1, source_target_pairs={{0,64},{32,96},{64,0},{96,32},{128,192},{160,224},{192,128},{224,1... | collective-permute-start | bytes 221192 | tf_op jit(solution)/shard_map/ppermute | solution.py:324
  78.7 4.5 %collective-permute-start.1 = (bf16[144,256]{1,0:T(8,128)(2,1)S(1)}, bf16[144,256]{1,0:T(8,128)(2,1)S(1)}, u32[]{:S(2)}, u32[]{:S(2)}) collective-permute-start(bf16[144,256]{1,0:T(8,128)(2,1)S(1)} %get-tuple-element.15), channel_id=1, source_target_pairs={{0,32},{32,0},{64,96},{96,64},{128,160},{160,128},{192,224},{224,1... | collective-permute-start | bytes 221192 | tf_op jit(solution)/shard_map/ppermute | solution.py:324
  80.6 6.2 %collective-permute-start.2 = (bf16[144,256]{1,0:T(8,128)(2,1)S(1)}, bf16[144,256]{1,0:T(8,128)(2,1)S(1)}, u32[]{:S(2)}, u32[]{:S(2)}) collective-permute-start(bf16[144,256]{1,0:T(8,128)(2,1)S(1)} %get-tuple-element.16), channel_id=1, source_target_pairs={{0,96},{32,64},{64,32},{96,0},{128,224},{160,192},{192,160},{224,1... | collective-permute-start | bytes 221192 | tf_op jit(solution)/shard_map/ppermute | solution.py:324
  86.8 7.6 %collective-permute-start.3 = (bf16[144,256]{1,0:T(8,128)(2,1)S(1)}, bf16[144,256]{1,0:T(8,128)(2,1)S(1)}, u32[]{:S(2)}, u32[]{:S(2)}) collective-permute-start(bf16[144,256]{1,0:T(8,128)(2,1)S(1)} %add_convert_fusion), channel_id=1, source_target_pairs={{0,224},{32,192},{64,160},{96,128},{128,96},{160,64},{192,32},{224... | collective-permute-start | bytes 221192 | tf_op jit(solution)/shard_map/ppermute | solution.py:324
  94.5 6.7 %collective-permute-start.6 = (bf16[144,256]{1,0:T(8,128)(2,1)S(1)}, bf16[144,256]{1,0:T(8,128)(2,1)S(1)}, u32[]{:S(2)}, u32[]{:S(2)}) collective-permute-start(bf16[144,256]{1,0:T(8,128)(2,1)S(1)} %multiply_convert_fusion.refs_0_), channel_id=1, source_target_pairs={{0,96},{32,64},{64,32},{96,0},{128,224},{160,192},{192,160},{224,1... | collective-permute-start | bytes 221192 | tf_op jit(solution)/shard_map/ppermute | solution.py:324
  96.2 6.5 %collective-permute-start.5 = (bf16[144,256]{1,0:T(8,128)(2,1)S(1)}, bf16[144,256]{1,0:T(8,128)(2,1)S(1)}, u32[]{:S(2)}, u32[]{:S(2)}) collective-permute-start(bf16[144,256]{1,0:T(8,128)(2,1)S(1)} %multiply_convert_fusion.refs_0_), channel_id=1, source_target_pairs={{0,64},{32,96},{64,0},{96,32},{128,192},{160,224},{192,128},{224,1... | collective-permute-start | bytes 221192 | tf_op jit(solution)/shard_map/ppermute | solution.py:324
  97.1 5.6 %collective-permute-start.4 = (bf16[144,256]{1,0:T(8,128)(2,1)S(1)}, bf16[144,256]{1,0:T(8,128)(2,1)S(1)}, u32[]{:S(2)}, u32[]{:S(2)}) collective-permute-start(bf16[144,256]{1,0:T(8,128)(2,1)S(1)} %multiply_convert_fusion.refs_0_), channel_id=1, source_target_pairs={{0,32},{32,0},{64,96},{96,64},{128,160},{160,128},{192,224},{224,1... | collective-permute-start | bytes 221192 | tf_op jit(solution)/shard_map/ppermute | solution.py:324

commit v10 on v9

--- a/solution.py
+++ b/solution.py
@@ -333,7 +333,7 @@
     average = (mine.astype(F32) + other.astype(F32)) / hours_all
     size = jnp.abs(average) + 0.1
     stacked = (jnp.sign(average) * (size * size - 0.01)).astype(BF16)
-    others = {k: swap(stacked, k) for k in (1, 2, 3)}
+    others = {k: swap(stacked, k) for k in (1, 3, 2)}
     parts = [stacked] + [others[k] for k in range(1, HALF_HOURS)]
     return pl.pallas_call(
         spread_kernel,

time: 104 us -> 104 us (level)
  no operation moved by 1% of the time
where the time goes in v10:
time: 104 us
  blocking collectives  62.7 us (60%)
  waiting for transfers between devices  13.7 us (13%)
  starting transfers between devices  13.5 us (13%)
  Pallas kernels  13.4 us (13%)
    all_to_all x1, blocking collectives, local(): lax.all_to_all(outgoing, 'pair', split_axis=0, concat_axis=0, tiled=True)  62.7 us
    ppermute x7, waiting for transfers between devices, swap(): lax.ppermute(array, 'hour', [(i, i ^ distance) for i in range(2 * HALF_HO...  13.7 us
    ppermute x7, starting transfers between devices, swap(): lax.ppermute(array, 'hour', [(i, i ^ distance) for i in range(2 * HALF_HO...  13.5 us
    pallas_call x1, Pallas kernels, whiten(): pl.pallas_call(whiten_kernel, in_specs=[hbm] * 7, out_specs=[hbm, hbm], o...  7.32 us
    pallas_call x1, Pallas kernels, correlate(): pl.pallas_call(correlate_kernel, in_specs=[vmem, vmem, vmem], out_specs=[...  5.25 us
  transfers between devices with their start and end apart: 7, of which 6 were waited for; matrix products, arithmetic and copies ran while one was open for 0% of the time, Pallas kernels for 0%

profile of v10, /device:TPU:8, one launch (start us, length us, event | category | flops | bytes accessed | tf_op | source)
XLA Modules:
  0.0 103.6 jit_solution(7397725886353528614)
XLA Ops:
  0.0 7.3 %shard_map.82 = (bf16[32,48,1536]{2,1,0:T(8,128)(2,1)}, bf16[512,512]{1,0:T(8,128)(2,1)}) custom-call(bf16[3,3,16,3712]{3,2,1,0:T(8,128)(2,1)} %bitcast.10, s32[3,2,16]{2,1,0:T(2,128)} %bitcast.11, s32[3,2,16]{2,1,0:T(2,128)} %bitcast.12, s32[4,32]{1,0:T(4,128)} %bitcast.13, s32[2,64]{1,0:T(2,128)} %bitcast.14, bf16[1024,1024]{1,0:T(8,128)(2,1)} %constant.14.clone.dft_hbm, ...), custom_call_target="tpu_custom_call" | custom-call | tf_op jit(solution)/shard_map/pallas_call | solution.py:263
  7.3 0.0 copy-start
  7.3 0.0 copy-start.1
  7.4 62.7 %all_to_all.5.recv_ref = bf16[32,48,1536]{2,1,0:T(8,128)(2,1)S(1)} all-to-all(bf16[32,48,1536]{2,1,0:T(8,128)(2,1)} %get-tuple-element.11), channel_id=1, replica_groups=mesh['hour'=8,'pair'=32] {'pair'}, dimensions={0} | all-to-all | bytes 9437184 | tf_op jit(solution)/shard_map/all_to_all | solution.py:354
  70.1 0.0 copy-done
  70.1 0.0 copy-done.1
  70.1 5.3 %shard_map.83 = (bf16[144,256]{1,0:T(8,128)(2,1)S(1)}, bf16[144,256]{1,0:T(8,128)(2,1)S(1)}, bf16[144,256]{1,0:T(8,128)(2,1)S(1)}, bf16[144,256]{1,0:T(8,128)(2,1)S(1)}) custom-call(bf16[32,48,1536]{2,1,0:T(8,128)(2,1)S(1)} %all_to_all.5.recv_ref, bf16[512,512]{1,0:T(8,128)(2,1)S(1)} %copy-done.1, bf16[1024,256]{1,0:T(8,128)(2,1)S(1)} %copy-done), custom_call_target="tpu_custom_call" | custom-call | tf_op jit(solution)/shard_map/pallas_call | solution.py:302
  75.3 3.4 %collective-permute-start = (bf16[144,256]{1,0:T(8,128)(2,1)S(1)}, bf16[144,256]{1,0:T(8,128)(2,1)S(1)}, u32[]{:S(2)}, u32[]{:S(2)}) collective-permute-start(bf16[144,256]{1,0:T(8,128)(2,1)S(1)} %get-tuple-element.14), channel_id=1, source_target_pairs={{0,64},{32,96},{64,0},{96,32},{128,192},{160,224},{192,128},{224,1... | collective-permute-start | bytes 221192 | tf_op jit(solution)/shard_map/ppermute | solution.py:324
  78.7 1.9 %collective-permute-start.1 = (bf16[144,256]{1,0:T(8,128)(2,1)S(1)}, bf16[144,256]{1,0:T(8,128)(2,1)S(1)}, u32[]{:S(2)}, u32[]{:S(2)}) collective-permute-start(bf16[144,256]{1,0:T(8,128)(2,1)S(1)} %get-tuple-element.15), channel_id=1, source_target_pairs={{0,32},{32,0},{64,96},{96,64},{128,160},{160,128},{192,224},{224,1... | collective-permute-start | bytes 221192 | tf_op jit(solution)/shard_map/ppermute | solution.py:324
  80.6 0.0 collective-permute-start.2
  80.6 2.3 %collective-permute-done = bf16[144,256]{1,0:T(8,128)(2,1)S(1)} collective-permute-done((bf16[144,256]{1,0:T(8,128)(2,1)S(1)}, bf16[144,256]{1,0:T(8,128)(2,1)S(1)}, u32[]{:S(2)}, u32[]{:S(2)}) %collective-permute-start) | collective-permute-done | bytes 73760 | tf_op jit(solution)/shard_map/ppermute | solution.py:324
  83.0 0.3 collective-permute-done.1
  83.2 3.5 %collective-permute-done.2 = bf16[144,256]{1,0:T(8,128)(2,1)S(1)} collective-permute-done((bf16[144,256]{1,0:T(8,128)(2,1)S(1)}, bf16[144,256]{1,0:T(8,128)(2,1)S(1)}, u32[]{:S(2)}, u32[]{:S(2)}) %collective-permute-start.2) | collective-permute-done | bytes 73760 | tf_op jit(solution)/shard_map/ppermute | solution.py:324
  86.8 3.8 %collective-permute-start.3 = (bf16[144,256]{1,0:T(8,128)(2,1)S(1)}, bf16[144,256]{1,0:T(8,128)(2,1)S(1)}, u32[]{:S(2)}, u32[]{:S(2)}) collective-permute-start(bf16[144,256]{1,0:T(8,128)(2,1)S(1)} %add_convert_fusion), channel_id=1, source_target_pairs={{0,224},{32,192},{64,160},{96,128},{128,96},{160,64},{192,32},{224... | collective-permute-start | bytes 221192 | tf_op jit(solution)/shard_map/ppermute | solution.py:324
  90.6 3.8 %collective-permute-done.3 = bf16[144,256]{1,0:T(8,128)(2,1)S(1)} collective-permute-done((bf16[144,256]{1,0:T(8,128)(2,1)S(1)}, bf16[144,256]{1,0:T(8,128)(2,1)S(1)}, u32[]{:S(2)}, u32[]{:S(2)}) %collective-permute-start.3) | collective-permute-done | bytes 73760 | tf_op jit(solution)/shard_map/ppermute | solution.py:324
  94.4 0.1 multiply_convert_fusion.refs_0_
  94.5 1.7 %collective-permute-start.6 = (bf16[144,256]{1,0:T(8,128)(2,1)S(1)}, bf16[144,256]{1,0:T(8,128)(2,1)S(1)}, u32[]{:S(2)}, u32[]{:S(2)}) collective-permute-start(bf16[144,256]{1,0:T(8,128)(2,1)S(1)} %multiply_convert_fusion.refs_0_), channel_id=1, source_target_pairs={{0,96},{32,64},{64,32},{96,0},{128,224},{160,192},{192,160},{224,1... | collective-permute-start | bytes 221192 | tf_op jit(solution)/shard_map/ppermute | solution.py:324
  96.2 0.8 collective-permute-start.5
  97.1 1.9 %collective-permute-start.4 = (bf16[144,256]{1,0:T(8,128)(2,1)S(1)}, bf16[144,256]{1,0:T(8,128)(2,1)S(1)}, u32[]{:S(2)}, u32[]{:S(2)}) collective-permute-start(bf16[144,256]{1,0:T(8,128)(2,1)S(1)} %multiply_convert_fusion.refs_0_), channel_id=1, source_target_pairs={{0,32},{32,0},{64,96},{96,64},{128,160},{160,128},{192,224},{224,1... | collective-permute-start | bytes 221192 | tf_op jit(solution)/shard_map/ppermute | solution.py:324
  99.0 2.2 %collective-permute-done.6.refs_3_ = bf16[144,256]{1,0:T(8,128)(2,1)S(1)} collective-permute-done((bf16[144,256]{1,0:T(8,128)(2,1)S(1)}, bf16[144,256]{1,0:T(8,128)(2,1)S(1)}, u32[]{:S(2)}, u32[]{:S(2)}) %collective-permute-start.6) | collective-permute-done | bytes 73760 | tf_op jit(solution)/shard_map/ppermute | solution.py:324
  101.2 1.5 %collective-permute-done.5.refs_2_ = bf16[144,256]{1,0:T(8,128)(2,1)S(1)} collective-permute-done((bf16[144,256]{1,0:T(8,128)(2,1)S(1)}, bf16[144,256]{1,0:T(8,128)(2,1)S(1)}, u32[]{:S(2)}, u32[]{:S(2)}) %collective-permute-start.5) | collective-permute-done | bytes 73760 | tf_op jit(solution)/shard_map/ppermute | solution.py:324
  102.7 0.0 collective-permute-done.4.refs_1_
  102.7 0.9 spread_result.1
  (1 shorter events, 0.0 us)
Async XLA Ops:
  7.3 62.8 %copy-start = (bf16[1024,256]{1,0:T(8,128)(2,1)S(1)}, bf16[1024,256]{1,0:T(8,128)(2,1)}, u32[]{:S(2)}) copy-start(bf16[1024,256]{1,0:T(8,128)(2,1)} %constant.16.clone.lag_ref) | copy-start | bytes 1572868
  7.3 62.7 %copy-start.1 = (bf16[512,512]{1,0:T(8,128)(2,1)S(1)}, bf16[512,512]{1,0:T(8,128)(2,1)}, u32[]{:S(2)}) copy-start(bf16[512,512]{1,0:T(8,128)(2,1)} %get-tuple-element.12.pick_ref) | copy-start | bytes 1572868
  75.3 7.6 %collective-permute-start = (bf16[144,256]{1,0:T(8,128)(2,1)S(1)}, bf16[144,256]{1,0:T(8,128)(2,1)S(1)}, u32[]{:S(2)}, u32[]{:S(2)}) collective-permute-start(bf16[144,256]{1,0:T(8,128)(2,1)S(1)} %get-tuple-element.14), channel_id=1, source_target_pairs={{0,64},{32,96},{64,0},{96,32},{128,192},{160,224},{192,128},{224,1... | collective-permute-start | bytes 221192 | tf_op jit(solution)/shard_map/ppermute | solution.py:324
  78.7 4.5 %collective-permute-start.1 = (bf16[144,256]{1,0:T(8,128)(2,1)S(1)}, bf16[144,256]{1,0:T(8,128)(2,1)S(1)}, u32[]{:S(2)}, u32[]{:S(2)}) collective-permute-start(bf16[144,256]{1,0:T(8,128)(2,1)S(1)} %get-tuple-element.15), channel_id=1, source_target_pairs={{0,32},{32,0},{64,96},{96,64},{128,160},{160,128},{192,224},{224,1... | collective-permute-start | bytes 221192 | tf_op jit(solution)/shard_map/ppermute | solution.py:324
  80.6 6.2 %collective-permute-start.2 = (bf16[144,256]{1,0:T(8,128)(2,1)S(1)}, bf16[144,256]{1,0:T(8,128)(2,1)S(1)}, u32[]{:S(2)}, u32[]{:S(2)}) collective-permute-start(bf16[144,256]{1,0:T(8,128)(2,1)S(1)} %get-tuple-element.16), channel_id=1, source_target_pairs={{0,96},{32,64},{64,32},{96,0},{128,224},{160,192},{192,160},{224,1... | collective-permute-start | bytes 221192 | tf_op jit(solution)/shard_map/ppermute | solution.py:324
  86.8 7.6 %collective-permute-start.3 = (bf16[144,256]{1,0:T(8,128)(2,1)S(1)}, bf16[144,256]{1,0:T(8,128)(2,1)S(1)}, u32[]{:S(2)}, u32[]{:S(2)}) collective-permute-start(bf16[144,256]{1,0:T(8,128)(2,1)S(1)} %add_convert_fusion), channel_id=1, source_target_pairs={{0,224},{32,192},{64,160},{96,128},{128,96},{160,64},{192,32},{224... | collective-permute-start | bytes 221192 | tf_op jit(solution)/shard_map/ppermute | solution.py:324
  94.5 6.7 %collective-permute-start.6 = (bf16[144,256]{1,0:T(8,128)(2,1)S(1)}, bf16[144,256]{1,0:T(8,128)(2,1)S(1)}, u32[]{:S(2)}, u32[]{:S(2)}) collective-permute-start(bf16[144,256]{1,0:T(8,128)(2,1)S(1)} %multiply_convert_fusion.refs_0_), channel_id=1, source_target_pairs={{0,96},{32,64},{64,32},{96,0},{128,224},{160,192},{192,160},{224,1... | collective-permute-start | bytes 221192 | tf_op jit(solution)/shard_map/ppermute | solution.py:324
  96.2 6.5 %collective-permute-start.5 = (bf16[144,256]{1,0:T(8,128)(2,1)S(1)}, bf16[144,256]{1,0:T(8,128)(2,1)S(1)}, u32[]{:S(2)}, u32[]{:S(2)}) collective-permute-start(bf16[144,256]{1,0:T(8,128)(2,1)S(1)} %multiply_convert_fusion.refs_0_), channel_id=1, source_target_pairs={{0,64},{32,96},{64,0},{96,32},{128,192},{160,224},{192,128},{224,1... | collective-permute-start | bytes 221192 | tf_op jit(solution)/shard_map/ppermute | solution.py:324
  97.1 5.6 %collective-permute-start.4 = (bf16[144,256]{1,0:T(8,128)(2,1)S(1)}, bf16[144,256]{1,0:T(8,128)(2,1)S(1)}, u32[]{:S(2)}, u32[]{:S(2)}) collective-permute-start(bf16[144,256]{1,0:T(8,128)(2,1)S(1)} %multiply_convert_fusion.refs_0_), channel_id=1, source_target_pairs={{0,32},{32,0},{64,96},{96,64},{128,160},{160,128},{192,224},{224,1... | collective-permute-start | bytes 221192 | tf_op jit(solution)/shard_map/ppermute | solution.py:324
